TPU v7x, 32 devices: a whole 2x2x4 slice. The times are simulated.
32 devices in a mesh: dp: 16 (over z, x, core), tensor: 2 (over y).
Axes of the slice: x: 2, y: 2, z: 4, core: 2. Of those that a mesh axis runs over, the one named last changes fastest.
Arguments:
- page_tokens: bfloat16 [16, 708, 768], P('dp'), may hold values from -6 to 6
- patch_counts: int32 [16], P('dp'), may hold values from 49 to 196, as said below
- token_boxes: int32 [16, 2, 708], P('dp'), may hold values from 0 to 511
- text_weight: bfloat16 [3, 3, 768], replicated, may hold values from -1 to 1
- patch_weight: bfloat16 [9, 768], replicated, may hold values from -1.25 to 1.25
- query_weight: bfloat16 [768, 768], P(None, 'tensor'), may hold values from -0.21875 to 0.21875
- query_bias: bfloat16 [768], P('tensor'), may hold values from -1.5 to 1.5
- key_weight: bfloat16 [768, 768], P(None, 'tensor'), may hold values from -0.21875 to 0.21875
- value_weight: bfloat16 [768, 768], P(None, 'tensor'), may hold values from -0.21875 to 0.21875
- value_bias: bfloat16 [768], P('tensor'), may hold values from -1.5 to 1.5
- out_weight: bfloat16 [768, 768], P('tensor'), may hold values from -0.875 to 0.875
- out_bias: bfloat16 [768], replicated, may hold values from -1.5 to 1.5
- line_table: bfloat16 [32, 12], P(None, 'tensor'), may hold values from -3.5 to 3.5
- width_table: bfloat16 [64, 12], P(None, 'tensor'), may hold values from -3.5 to 3.5
- height_table: bfloat16 [64, 12], P(None, 'tensor'), may hold values from -3.5 to 3.5
- norm1_gain: bfloat16 [768], replicated, may hold values from 0.5 to 1.5
- norm1_shift: bfloat16 [768], replicated, may hold values from -1.5 to 1.5
- inner_weight: bfloat16 [768, 3072], P(None, 'tensor'), may hold values from -0.21875 to 0.21875
- inner_bias: bfloat16 [3072], P('tensor'), may hold values from -1.5 to 1.5
- outer_weight: bfloat16 [3072, 768], P('tensor'), may hold values from -0.109375 to 0.109375
- outer_bias: bfloat16 [768], replicated, may hold values from -1.5 to 1.5
- norm2_gain: bfloat16 [768], replicated, may hold values from 0.5 to 1.5
- norm2_shift: bfloat16 [768], replicated, may hold values from -1.5 to 1.5
- cotangent: bfloat16 [16, 708, 768], P('dp'), may hold values from -6 to 6
Outputs:
- layer_output: bfloat16 [16, 708, 768], P('dp')
- input_grad: bfloat16 [16, 708, 768], P('dp')
- grad_text_weight: float32 [3, 3, 768], P(None, None, 'dp')
- grad_patch_weight: float32 [9, 768], P(None, 'dp')
- grad_query_weight: float32 [768, 768], P('dp', 'tensor')
- grad_query_bias: float32 [768], P('tensor')
- grad_key_weight: float32 [768, 768], P('dp', 'tensor')
- grad_value_weight: float32 [768, 768], P('dp', 'tensor')
- grad_value_bias: float32 [768], P('tensor')
- grad_out_weight: float32 [768, 768], P('tensor', 'dp')
- grad_out_bias: float32 [768], P('dp')
- grad_line_table: float32 [32, 12], P(None, 'tensor')
- grad_width_table: float32 [64, 12], P(None, 'tensor')
- grad_height_table: float32 [64, 12], P(None, 'tensor')
- grad_norm1_gain: float32 [768], P('dp')
- grad_norm1_shift: float32 [768], P('dp')
- grad_inner_weight: float32 [768, 3072], P('dp', 'tensor')
- grad_inner_bias: float32 [3072], P('tensor')
- grad_outer_weight: float32 [3072, 768], P('tensor', 'dp')
- grad_outer_bias: float32 [768], P('dp')
- grad_norm2_gain: float32 [768], P('dp')
- grad_norm2_shift: float32 [768], P('dp')
Inputs may be any that keep to these rules, and one draw needn't show every extreme that they name: `patch_counts`: each page has 49 or 196 patches; both occur in every draw.
All inputs are finite; a program needn't handle non-finite values.
Results may differ from a plain program's by a relative error of at most 0.014.
The roundings to bfloat16 on the way count: a program that leaves them out, or rounds other values in their place, can miss the bound.
Values sent between devices are 32-bit elements; how exact they have to be, the bound alone decides.
No kernel may reach another device: no remote copies, remote signals or barrier semaphores. Data moves between devices by JAX's collectives and lax.ppermute only.
A program may use at most 192 MiB of HBM per device.

v0:
```python
import jax
import jax.numpy as jnp
from jax import lax
from jax.sharding import PartitionSpec as P

HEADS = 12
TEXT = 512
GRID_SMALL = 7
GRID_LARGE = 14
BINS_1D = 32
BINS_2D = 64
BIN_WIDTH = 8


eps_norm = 1e-05
neg_fill = -1000000000.0
highest = lax.Precision.HIGHEST


def dense(left_side, right_side):
    return jnp.dot(left_side, right_side, preferred_element_type=jnp.float32)


def dense_back(left_side, right_side):
    return lax.dot_general(
        left_side, right_side, (((1,), (1,)), ((), ())), preferred_element_type=jnp.float32
    )


def contract_rows(left_side, right_side):
    return lax.dot_general(
        left_side, right_side, (((0,), (0,)), ((), ())), preferred_element_type=jnp.float32
    )


def layer_norm(values, gain_vec, shift_vec):
    centre = values - jnp.mean(values, axis=-1, keepdims=True)
    spread = jnp.mean(centre * centre, axis=-1, keepdims=True)
    return centre * lax.rsqrt(spread + eps_norm) * gain_vec + shift_vec


def exact_gelu(values):
    return jax.nn.gelu(values, approximate=False)


def grid_conv(grid_rows, patch_w, side):
    padded = jnp.pad(grid_rows, ((1, 1), (1, 1), (0, 0)))
    summed = jnp.zeros_like(grid_rows)
    for step_row in (-1, 0, 1):
        for step_col in (-1, 0, 1):
            tap_index = 3 * (step_row + 1) + step_col + 1
            summed = (
                summed
                + patch_w[tap_index]
                * padded[1 + step_row : 1 + step_row + side, 1 + step_col : 1 + step_col + side]
            )
    return summed


def patch_conv(patch_rows, patch_w, is_large):
    patches, width = patch_rows.shape
    large_part = grid_conv(
        patch_rows.reshape(GRID_LARGE, GRID_LARGE, width), patch_w, GRID_LARGE
    ).reshape(patches, width)
    few_rows = GRID_SMALL * GRID_SMALL
    small_part = grid_conv(
        patch_rows[:few_rows].reshape(GRID_SMALL, GRID_SMALL, width), patch_w, GRID_SMALL
    ).reshape(few_rows, width)
    small_part = jnp.pad(small_part, ((0, patches - few_rows), (0, 0)))
    return jnp.where(is_large, large_part, small_part)


def position_encoding(page_rows, text_w, patch_w, is_large, text_len):
    text_rows = page_rows[:text_len]
    padded = jnp.pad(text_rows, ((3, 3), (0, 0)))
    summed = jnp.zeros_like(text_rows)
    for dilate in range(3):
        for tap_index in range(3):
            offset = (tap_index - 1) * (dilate + 1)
            summed = summed + text_w[dilate, tap_index] * padded[3 + offset : 3 + offset + text_len]
    patch_part = patch_conv(page_rows[text_len:], patch_w, is_large)
    return jnp.concatenate([summed, patch_part], axis=0)


def plane_bucket(coordinate):
    half_plane = BINS_2D // 2
    differ = jnp.floor_divide(coordinate[None, :] - coordinate[:, None], BIN_WIDTH)
    return jnp.clip(differ, -half_plane, half_plane - 1) + half_plane


def bias_buckets(boxes_page, seq_len):
    position = jnp.arange(seq_len, dtype=jnp.int32)
    half_line = BINS_1D // 2
    line_bucket = (
        jnp.clip(position[None, :] - position[:, None], -half_line, half_line - 1) + half_line
    )
    return (line_bucket, plane_bucket(boxes_page[0]), plane_bucket(boxes_page[1]))


def row_block(seq_len):
    return max((size for size in range(1, min(64, seq_len) + 1) if seq_len % size == 0))


def selector_rows(bucket_page, start, block, dtype):
    bin_total = BINS_1D + 2 * BINS_2D
    bin_ids = jnp.arange(bin_total, dtype=jnp.int32)
    offset = 0
    hits = None
    for bucket, count in zip(bucket_page, (BINS_1D, BINS_2D, BINS_2D)):
        rows = lax.dynamic_slice_in_dim(bucket, start, block, 0)
        match = (rows + offset)[:, :, None] == bin_ids
        hits = match if hits is None else hits | match
        offset = offset + count
    return hits.astype(dtype)


def page_bias(bucket_page, table_low):
    seq_len = bucket_page[0].shape[0]
    heads = table_low.shape[1]
    block = row_block(seq_len)

    def fill(index, total):
        start = index * block
        selector = selector_rows(bucket_page, start, block, jnp.bfloat16)
        part = lax.dot_general(
            table_low, selector, (((0,), (2,)), ((), ())), preferred_element_type=jnp.float32
        )
        return lax.dynamic_update_slice_in_dim(total, part, start, 1)

    return lax.fori_loop(
        0, seq_len // block, fill, jnp.zeros((heads, seq_len, seq_len), jnp.float32)
    )


def table_sums(grad_scores, bucket_page):
    heads, seq_len, keys_count = grad_scores.shape
    block = row_block(seq_len)
    bin_total = BINS_1D + 2 * BINS_2D

    def accumulate(index, total):
        start = index * block
        selector = selector_rows(bucket_page, start, block, jnp.float32)
        grad_part = lax.dynamic_slice_in_dim(grad_scores, start, block, 1)
        return total + lax.dot_general(
            grad_part,
            selector,
            (((1, 2), (0, 1)), ((), ())),
            precision=highest,
            preferred_element_type=jnp.float32,
        )

    summed = lax.fori_loop(
        0, seq_len // block, accumulate, jnp.zeros((heads, bin_total), jnp.float32)
    )
    summed = jnp.transpose(summed)
    return (summed[:BINS_1D], summed[BINS_1D : BINS_1D + BINS_2D], summed[BINS_1D + BINS_2D :])


def per_device(
    page_tokens,
    patch_counts,
    token_boxes,
    text_weight,
    patch_weight,
    query_weight,
    query_bias,
    key_weight,
    value_weight,
    value_bias,
    out_weight,
    out_bias,
    line_table,
    width_table,
    height_table,
    norm1_gain,
    norm1_shift,
    inner_weight,
    inner_bias,
    outer_weight,
    outer_bias,
    norm2_gain,
    norm2_shift,
    cotangent,
):
    page_count, seq_len, model_width = page_tokens.shape
    text_len = TEXT
    head_dim = model_width // HEADS
    local_heads = query_weight.shape[1] // head_dim
    scale = head_dim ** (-0.5)
    row_count = page_count * seq_len
    live_rows = (jnp.arange(seq_len)[None, :] < text_len + patch_counts[:, None]).astype(
        jnp.float32
    )
    large_pages = patch_counts == GRID_LARGE * GRID_LARGE

    def page_buckets(boxes_page):
        return bias_buckets(boxes_page, seq_len)

    buckets = jax.vmap(page_buckets)(token_boxes)
    table_low = jnp.concatenate([line_table, width_table, height_table], axis=0)

    def encode_page(page_rows, is_large, text_w, patch_w):
        return position_encoding(page_rows, text_w, patch_w, is_large, text_len)

    def encode_all(rows_float, text_w, patch_w):
        return jax.vmap(encode_page, in_axes=(0, 0, None, None))(
            rows_float, large_pages, text_w, patch_w
        )

    inputs_float = page_tokens.astype(jnp.float32)
    encoding, encode_back = jax.vjp(
        encode_all, inputs_float, text_weight.astype(jnp.float32), patch_weight.astype(jnp.float32)
    )
    encoded = (inputs_float + encoding).reshape(row_count, model_width)
    encoded_low = encoded.astype(jnp.bfloat16)
    queries = (dense(encoded_low, query_weight) + query_bias.astype(jnp.float32)).astype(
        jnp.bfloat16
    )
    key_rows = dense(encoded_low, key_weight).astype(jnp.bfloat16)
    value_rows = (dense(encoded_low, value_weight) + value_bias.astype(jnp.float32)).astype(
        jnp.bfloat16
    )

    def page_scores(query_page, key_page, live_page, bias_page):
        shaped_query = query_page.reshape(seq_len, local_heads, head_dim)
        shaped_key = key_page.reshape(seq_len, local_heads, head_dim)
        raw_scores = jnp.einsum(
            "qhd,khd->hqk", shaped_query, shaped_key, preferred_element_type=jnp.float32
        )
        scores = raw_scores * scale + bias_page
        return jnp.where(live_page[None, None, :] > 0.5, scores, neg_fill)

    def attend(packed):
        query_page, key_page, value_page, live_page, bucket_page = packed
        bias_page = page_bias(bucket_page, table_low)
        scores = page_scores(query_page, key_page, live_page, bias_page)
        row_max = jnp.max(scores, axis=-1, keepdims=True)
        exp_scores = jnp.exp(scores - row_max)
        row_total = jnp.sum(exp_scores, axis=-1, keepdims=True)
        attn_probs = (exp_scores / row_total).astype(jnp.bfloat16)
        shaped_value = value_page.reshape(seq_len, local_heads, head_dim)
        mixture = jnp.einsum(
            "hqk,khd->qhd", attn_probs, shaped_value, preferred_element_type=jnp.float32
        )
        return (
            mixture.reshape(seq_len, local_heads * head_dim).astype(jnp.bfloat16),
            row_max + jnp.log(row_total),
            bias_page,
        )

    query_pages = queries.reshape(page_count, seq_len, -1)
    key_pages = key_rows.reshape(page_count, seq_len, -1)
    value_pages = value_rows.reshape(page_count, seq_len, -1)
    mixture, log_totals, biases = lax.map(
        attend, (query_pages, key_pages, value_pages, live_rows, buckets)
    )
    mixture_flat = mixture.reshape(row_count, -1)
    attended = lax.psum(dense(mixture_flat, out_weight), "tensor") + out_bias.astype(jnp.float32)
    hidden, norm1_back = jax.vjp(
        layer_norm,
        encoded + attended,
        norm1_gain.astype(jnp.float32),
        norm1_shift.astype(jnp.float32),
    )
    hidden_low = hidden.astype(jnp.bfloat16)
    inner_pre = dense(hidden_low, inner_weight) + inner_bias.astype(jnp.float32)
    activated, gelu_back = jax.vjp(exact_gelu, inner_pre)
    activated_low = activated.astype(jnp.bfloat16)
    outer_out = lax.psum(dense(activated_low, outer_weight), "tensor") + outer_bias.astype(
        jnp.float32
    )
    live_flat = live_rows.reshape(row_count, 1)

    def final_norm(values, gain_vec, shift_vec):
        return layer_norm(values, gain_vec, shift_vec) * live_flat

    layer_out, norm2_back = jax.vjp(
        final_norm,
        hidden + outer_out,
        norm2_gain.astype(jnp.float32),
        norm2_shift.astype(jnp.float32),
    )
    grad_res2, grad_gain2, grad_shift2 = norm2_back(
        cotangent.reshape(row_count, model_width).astype(jnp.float32)
    )
    grad_outer_bias = jnp.sum(grad_res2, axis=0)
    grad_res2_low = grad_res2.astype(jnp.bfloat16)
    grad_outer_weight = contract_rows(activated_low, grad_res2_low)
    (grad_inner,) = gelu_back(dense_back(grad_res2_low, outer_weight))
    grad_inner_bias = jnp.sum(grad_inner, axis=0)
    grad_inner_low = grad_inner.astype(jnp.bfloat16)
    grad_inner_weight = contract_rows(hidden_low, grad_inner_low)
    grad_hidden = grad_res2 + lax.psum(dense_back(grad_inner_low, inner_weight), "tensor")
    grad_res1, grad_gain1, grad_shift1 = norm1_back(grad_hidden)
    grad_out_bias = jnp.sum(grad_res1, axis=0)
    grad_res1_low = grad_res1.astype(jnp.bfloat16)
    grad_out_weight = contract_rows(mixture_flat, grad_res1_low)
    grad_mixture = dense_back(grad_res1_low, out_weight).astype(jnp.bfloat16)

    def attend_back(packed):
        query_page, key_page, value_page, live_page, bucket_page, bias_page, log_page, grad_page = (
            packed
        )
        scores = page_scores(query_page, key_page, live_page, bias_page)
        attn_probs = jnp.exp(scores - log_page)
        probs_low = attn_probs.astype(jnp.bfloat16)
        shaped_query = query_page.reshape(seq_len, local_heads, head_dim)
        shaped_key = key_page.reshape(seq_len, local_heads, head_dim)
        shaped_value = value_page.reshape(seq_len, local_heads, head_dim)
        shaped_grad = grad_page.reshape(seq_len, local_heads, head_dim)
        grad_value = jnp.einsum(
            "hqk,qhd->khd", probs_low, shaped_grad, preferred_element_type=jnp.float32
        )
        grad_probs = jnp.einsum(
            "qhd,khd->hqk", shaped_grad, shaped_value, preferred_element_type=jnp.float32
        )
        grad_scores = attn_probs * (
            grad_probs - jnp.sum(grad_probs * attn_probs, axis=-1, keepdims=True)
        )
        table_grads = table_sums(grad_scores, bucket_page)
        scores_low = grad_scores.astype(jnp.bfloat16)
        grad_query = (
            jnp.einsum("hqk,khd->qhd", scores_low, shaped_key, preferred_element_type=jnp.float32)
            * scale
        )
        grad_key = (
            jnp.einsum("hqk,qhd->khd", scores_low, shaped_query, preferred_element_type=jnp.float32)
            * scale
        )
        widths = local_heads * head_dim
        return (
            grad_query.reshape(seq_len, widths),
            grad_key.reshape(seq_len, widths),
            grad_value.reshape(seq_len, widths),
            table_grads,
        )

    grad_query, grad_key, grad_value, table_grads = lax.map(
        attend_back,
        (
            query_pages,
            key_pages,
            value_pages,
            live_rows,
            buckets,
            biases,
            log_totals,
            grad_mixture.reshape(page_count, seq_len, -1),
        ),
    )
    grad_line = jnp.sum(table_grads[0], axis=0)
    grad_width = jnp.sum(table_grads[1], axis=0)
    grad_height = jnp.sum(table_grads[2], axis=0)
    grad_query = grad_query.reshape(row_count, -1)
    grad_key = grad_key.reshape(row_count, -1)
    grad_value = grad_value.reshape(row_count, -1)
    grad_query_bias = jnp.sum(grad_query, axis=0)
    grad_value_bias = jnp.sum(grad_value, axis=0)
    query_low = grad_query.astype(jnp.bfloat16)
    key_low = grad_key.astype(jnp.bfloat16)
    value_low = grad_value.astype(jnp.bfloat16)
    grad_query_weight = contract_rows(encoded_low, query_low)
    grad_key_weight = contract_rows(encoded_low, key_low)
    grad_value_weight = contract_rows(encoded_low, value_low)
    back_terms = (
        dense_back(query_low, query_weight)
        + dense_back(key_low, key_weight)
        + dense_back(value_low, value_weight)
    )
    grad_encoded = grad_res1 + lax.psum(back_terms, "tensor")
    grad_encoded = grad_encoded.reshape(page_count, seq_len, model_width)
    grad_inputs, grad_text, grad_patch = encode_back(grad_encoded)
    input_grad = (grad_encoded + grad_inputs).astype(jnp.bfloat16)
    layer_output = layer_out.reshape(page_count, seq_len, model_width).astype(jnp.bfloat16)
    (
        sum_text,
        sum_patch,
        sum_query_w,
        sum_key_w,
        sum_value_w,
        sum_out_w,
        sum_out_b,
        sum_gain1,
        sum_shift1,
        sum_inner_w,
        sum_outer_w,
        sum_outer_b,
        sum_gain2,
        sum_shift2,
    ) = (
        lax.psum_scatter(grad_text, "dp", scatter_dimension=2, tiled=True),
        lax.psum_scatter(grad_patch, "dp", scatter_dimension=1, tiled=True),
        lax.psum_scatter(grad_query_weight, "dp", scatter_dimension=0, tiled=True),
        lax.psum_scatter(grad_key_weight, "dp", scatter_dimension=0, tiled=True),
        lax.psum_scatter(grad_value_weight, "dp", scatter_dimension=0, tiled=True),
        lax.psum_scatter(grad_out_weight, "dp", scatter_dimension=1, tiled=True),
        lax.psum_scatter(grad_out_bias, "dp", scatter_dimension=0, tiled=True),
        lax.psum_scatter(grad_gain1, "dp", scatter_dimension=0, tiled=True),
        lax.psum_scatter(grad_shift1, "dp", scatter_dimension=0, tiled=True),
        lax.psum_scatter(grad_inner_weight, "dp", scatter_dimension=0, tiled=True),
        lax.psum_scatter(grad_outer_weight, "dp", scatter_dimension=1, tiled=True),
        lax.psum_scatter(grad_outer_bias, "dp", scatter_dimension=0, tiled=True),
        lax.psum_scatter(grad_gain2, "dp", scatter_dimension=0, tiled=True),
        lax.psum_scatter(grad_shift2, "dp", scatter_dimension=0, tiled=True),
    )
    sum_query_b, sum_value_b, sum_line, sum_width, sum_height, sum_inner_b = lax.psum(
        (grad_query_bias, grad_value_bias, grad_line, grad_width, grad_height, grad_inner_bias),
        "dp",
    )
    return (
        layer_output,
        input_grad,
        sum_text,
        sum_patch,
        sum_query_w,
        sum_query_b,
        sum_key_w,
        sum_value_w,
        sum_value_b,
        sum_out_w,
        sum_out_b,
        sum_line,
        sum_width,
        sum_height,
        sum_gain1,
        sum_shift1,
        sum_inner_w,
        sum_inner_b,
        sum_outer_w,
        sum_outer_b,
        sum_gain2,
        sum_shift2,
    )


def solution(mesh):
    placed = (
        P("dp", None, None),
        P("dp"),
        P("dp", None, None),
        P(),
        P(),
        P(None, "tensor"),
        P("tensor"),
        P(None, "tensor"),
        P(None, "tensor"),
        P("tensor"),
        P("tensor", None),
        P(),
        P(None, "tensor"),
        P(None, "tensor"),
        P(None, "tensor"),
        P(),
        P(),
        P(None, "tensor"),
        P("tensor"),
        P("tensor", None),
        P(),
        P(),
        P(),
        P("dp", None, None),
    )
    return jax.shard_map(
        per_device,
        mesh=mesh,
        in_specs=placed,
        out_specs=(
            P("dp", None, None),
            P("dp", None, None),
            P(None, None, "dp"),
            P(None, "dp"),
            P("dp", "tensor"),
            P("tensor"),
            P("dp", "tensor"),
            P("dp", "tensor"),
            P("tensor"),
            P("tensor", "dp"),
            P("dp"),
            P(None, "tensor"),
            P(None, "tensor"),
            P(None, "tensor"),
            P("dp"),
            P("dp"),
            P("dp", "tensor"),
            P("tensor"),
            P("tensor", "dp"),
            P("dp"),
            P("dp"),
            P("dp"),
        ),
        check_vma=False,
    )
```

profile of v0, /device:TPU:0, one launch (start us, length us, event | category | flops | bytes accessed | tf_op | source)
XLA Modules:
  0.0 1123.1 jit_solution(12278521960262698997)
XLA Ops:
  57.3 129.0 %while.33 = (s32[]{:T(128)}, f32[6,708,708]{2,0,1:T(8,128)}, s32[708,708]{1,0:T(8,128)}, s32[708,708]{1,0:T(8,128)}, s32[708,708]{1,0:T(8,128)}, /*index=5*/bf16...) while((s32[]{:T(128)}, f32[6,708,708]{2,0,1:T(8,128)}, s32[708,708]{1,0:T(8,128)}, ...), condition=%wide.region_1.2_spmd, body=%wide.region_0.1_spmd.sunk | while | flops 113703392 | bytes 2955855 | solution.py:130
  186.3 16.4 %copy.79 = f32[6,708,708]{1,2,0:T(8,128)} copy(f32[6,708,708]{2,0,1:T(8,128)} %get-tuple-element.343) | data formatting | bytes 24060672 | tf_op jit(solution)/shard_map/while/body/eval_jaxpr/while | solution.py:130
  220.6 67.6 %all-reduce.73.cloned.1.call-done = f32[708,768]{1,0:T(8,128)} async-done(((f32[708,768]{1,0:T(8,128)}), f32[708,768]{1,0:T(8,128)}) %all-reduce.73.cloned.1.call-update) | async-done | bytes 2174992 | tf_op jit(solution)/shard_map/psum | solution.py:258
  291.4 12.8 %multiply_convert_fusion = (bf16[708,1536]{1,0:T(8,128)(2,1)S(1)}, f32[708,1536]{1,0:T(8,128)}, f32[708,1536]{1,0:T(8,128)}) fusion(f32[1536]{0:T(1024)S(1)} %convert_element_type.181, bf16[768,1536]{1,0:T(8,128)(2,1)S(1)} %copy-done, f32[708,768]{1,0:T(8,128)S(1)} %get-tuple-element.483, f32[768]{0:T(1024)S(1)} %convert_element_type.179, ...), kind=kOutput, calls=%fused_computation.53 | convolution fusion | flops 1744874496 | bytes 15427104 | tf_op jit(solution)/shard_map/dot_general | solution.py:21
  309.5 64.5 %all-reduce.75.cloned.1.call-done = f32[708,768]{1,0:T(8,128)} async-done(((f32[708,768]{1,0:T(8,128)}), f32[708,768]{1,0:T(8,128)}) %all-reduce.75.cloned.1.call-update) | async-done | bytes 2174992 | tf_op jit(solution)/shard_map/psum | solution.py:269
  393.2 64.9 %all-reduce.77.cloned.1.call-done = f32[708,768]{1,0:T(8,128)} async-done(((f32[708,768]{1,0:T(8,128)}), f32[708,768]{1,0:T(8,128)}) %all-reduce.77.cloned.1.call-update) | async-done | bytes 2174992 | tf_op jit(solution)/shard_map/psum | solution.py:293
  512.1 63.3 %all-reduce.79.cloned.1.call-done = f32[708,768]{1,0:T(8,128)} async-done(((f32[708,768]{1,0:T(8,128)}), f32[708,768]{1,0:T(8,128)}) %all-reduce.79.cloned.1.call-update) | async-done | bytes 2174992 | tf_op jit(solution)/shard_map/psum | solution.py:370
  629.0 17.2 %copy.87 = f32[6,708,708]{2,0,1:T(8,128)} copy(f32[6,708,708]{1,2,0:T(8,128)} %subtract_multiply_fusion) | data formatting | bytes 24060672
  646.2 245.7 %while.34 = (s32[]{:T(128)}, f32[6,160]{1,0:T(8,128)S(1)}, f32[6,708,708]{2,0,1:T(8,128)}, s32[708,708]{1,0:T(8,128)}, s32[708,708]{1,0:T(8,128)}, /*index=5*/s3...) while((s32[]{:T(128)}, f32[6,160]{1,0:T(8,128)S(1)}, ...), condition=%wide.region_55.56_spmd.clone, body=%wide.region_54.55_spmd.clone.sunk | while | flops 514716512 | bytes 2961633 | solution.py:152
  648.5 18.3 %fusion.170 = f32[6,160]{1,0:T(8,128)S(1)} fusion(s32[59,708]{1,0:T(8,128)S(1)} %get-tuple-element.621, s32[59,708]{1,0:T(8,128)S(1)} %get-tuple-element.622, s32[59,708]{1,0:T(8,128)S(1)} %constant_dynamic-slice_fusion.5, f32[6,708,708]{2,0,1:T(8,128)} %get-tuple-element.675, s32[]{:T(128)S(6)} %select_n.79, f32[6,160]{1,0:T(8,128)S(1)} %get-tuple-element.664, ...), kind=kOutput, calls=%fused_computation.26.clone.1 | convolution fusion | flops 514632960 | bytes 1958933 | tf_op jit(solution)/shard_map/while/body/eval_jaxpr/while/body/eval_jaxpr/dot_general | solution.py:144
  668.9 18.3 %fusion.170 = f32[6,160]{1,0:T(8,128)S(1)} fusion(s32[59,708]{1,0:T(8,128)S(1)} %get-tuple-element.621, s32[59,708]{1,0:T(8,128)S(1)} %get-tuple-element.622, s32[59,708]{1,0:T(8,128)S(1)} %constant_dynamic-slice_fusion.5, f32[6,708,708]{2,0,1:T(8,128)} %get-tuple-element.675, s32[]{:T(128)S(6)} %select_n.79, f32[6,160]{1,0:T(8,128)S(1)} %get-tuple-element.664, ...), kind=kOutput, calls=%fused_computation.26.clone.1 | convolution fusion | flops 514632960 | bytes 1958933 | tf_op jit(solution)/shard_map/while/body/eval_jaxpr/while/body/eval_jaxpr/dot_general | solution.py:144
  689.4 18.3 %fusion.170 = f32[6,160]{1,0:T(8,128)S(1)} fusion(s32[59,708]{1,0:T(8,128)S(1)} %get-tuple-element.621, s32[59,708]{1,0:T(8,128)S(1)} %get-tuple-element.622, s32[59,708]{1,0:T(8,128)S(1)} %constant_dynamic-slice_fusion.5, f32[6,708,708]{2,0,1:T(8,128)} %get-tuple-element.675, s32[]{:T(128)S(6)} %select_n.79, f32[6,160]{1,0:T(8,128)S(1)} %get-tuple-element.664, ...), kind=kOutput, calls=%fused_computation.26.clone.1 | convolution fusion | flops 514632960 | bytes 1958933 | tf_op jit(solution)/shard_map/while/body/eval_jaxpr/while/body/eval_jaxpr/dot_general | solution.py:144
  709.8 18.3 %fusion.170 = f32[6,160]{1,0:T(8,128)S(1)} fusion(s32[59,708]{1,0:T(8,128)S(1)} %get-tuple-element.621, s32[59,708]{1,0:T(8,128)S(1)} %get-tuple-element.622, s32[59,708]{1,0:T(8,128)S(1)} %constant_dynamic-slice_fusion.5, f32[6,708,708]{2,0,1:T(8,128)} %get-tuple-element.675, s32[]{:T(128)S(6)} %select_n.79, f32[6,160]{1,0:T(8,128)S(1)} %get-tuple-element.664, ...), kind=kOutput, calls=%fused_computation.26.clone.1 | convolution fusion | flops 514632960 | bytes 1958933 | tf_op jit(solution)/shard_map/while/body/eval_jaxpr/while/body/eval_jaxpr/dot_general | solution.py:144
  730.3 18.3 %fusion.170 = f32[6,160]{1,0:T(8,128)S(1)} fusion(s32[59,708]{1,0:T(8,128)S(1)} %get-tuple-element.621, s32[59,708]{1,0:T(8,128)S(1)} %get-tuple-element.622, s32[59,708]{1,0:T(8,128)S(1)} %constant_dynamic-slice_fusion.5, f32[6,708,708]{2,0,1:T(8,128)} %get-tuple-element.675, s32[]{:T(128)S(6)} %select_n.79, f32[6,160]{1,0:T(8,128)S(1)} %get-tuple-element.664, ...), kind=kOutput, calls=%fused_computation.26.clone.1 | convolution fusion | flops 514632960 | bytes 1958933 | tf_op jit(solution)/shard_map/while/body/eval_jaxpr/while/body/eval_jaxpr/dot_general | solution.py:144
  750.7 18.3 %fusion.170 = f32[6,160]{1,0:T(8,128)S(1)} fusion(s32[59,708]{1,0:T(8,128)S(1)} %get-tuple-element.621, s32[59,708]{1,0:T(8,128)S(1)} %get-tuple-element.622, s32[59,708]{1,0:T(8,128)S(1)} %constant_dynamic-slice_fusion.5, f32[6,708,708]{2,0,1:T(8,128)} %get-tuple-element.675, s32[]{:T(128)S(6)} %select_n.79, f32[6,160]{1,0:T(8,128)S(1)} %get-tuple-element.664, ...), kind=kOutput, calls=%fused_computation.26.clone.1 | convolution fusion | flops 514632960 | bytes 1958933 | tf_op jit(solution)/shard_map/while/body/eval_jaxpr/while/body/eval_jaxpr/dot_general | solution.py:144
  771.2 18.3 %fusion.170 = f32[6,160]{1,0:T(8,128)S(1)} fusion(s32[59,708]{1,0:T(8,128)S(1)} %get-tuple-element.621, s32[59,708]{1,0:T(8,128)S(1)} %get-tuple-element.622, s32[59,708]{1,0:T(8,128)S(1)} %constant_dynamic-slice_fusion.5, f32[6,708,708]{2,0,1:T(8,128)} %get-tuple-element.675, s32[]{:T(128)S(6)} %select_n.79, f32[6,160]{1,0:T(8,128)S(1)} %get-tuple-element.664, ...), kind=kOutput, calls=%fused_computation.26.clone.1 | convolution fusion | flops 514632960 | bytes 1958933 | tf_op jit(solution)/shard_map/while/body/eval_jaxpr/while/body/eval_jaxpr/dot_general | solution.py:144
  791.6 18.3 %fusion.170 = f32[6,160]{1,0:T(8,128)S(1)} fusion(s32[59,708]{1,0:T(8,128)S(1)} %get-tuple-element.621, s32[59,708]{1,0:T(8,128)S(1)} %get-tuple-element.622, s32[59,708]{1,0:T(8,128)S(1)} %constant_dynamic-slice_fusion.5, f32[6,708,708]{2,0,1:T(8,128)} %get-tuple-element.675, s32[]{:T(128)S(6)} %select_n.79, f32[6,160]{1,0:T(8,128)S(1)} %get-tuple-element.664, ...), kind=kOutput, calls=%fused_computation.26.clone.1 | convolution fusion | flops 514632960 | bytes 1958933 | tf_op jit(solution)/shard_map/while/body/eval_jaxpr/while/body/eval_jaxpr/dot_general | solution.py:144
  812.1 18.3 %fusion.170 = f32[6,160]{1,0:T(8,128)S(1)} fusion(s32[59,708]{1,0:T(8,128)S(1)} %get-tuple-element.621, s32[59,708]{1,0:T(8,128)S(1)} %get-tuple-element.622, s32[59,708]{1,0:T(8,128)S(1)} %constant_dynamic-slice_fusion.5, f32[6,708,708]{2,0,1:T(8,128)} %get-tuple-element.675, s32[]{:T(128)S(6)} %select_n.79, f32[6,160]{1,0:T(8,128)S(1)} %get-tuple-element.664, ...), kind=kOutput, calls=%fused_computation.26.clone.1 | convolution fusion | flops 514632960 | bytes 1958933 | tf_op jit(solution)/shard_map/while/body/eval_jaxpr/while/body/eval_jaxpr/dot_general | solution.py:144
  832.5 18.3 %fusion.170 = f32[6,160]{1,0:T(8,128)S(1)} fusion(s32[59,708]{1,0:T(8,128)S(1)} %get-tuple-element.621, s32[59,708]{1,0:T(8,128)S(1)} %get-tuple-element.622, s32[59,708]{1,0:T(8,128)S(1)} %constant_dynamic-slice_fusion.5, f32[6,708,708]{2,0,1:T(8,128)} %get-tuple-element.675, s32[]{:T(128)S(6)} %select_n.79, f32[6,160]{1,0:T(8,128)S(1)} %get-tuple-element.664, ...), kind=kOutput, calls=%fused_computation.26.clone.1 | convolution fusion | flops 514632960 | bytes 1958933 | tf_op jit(solution)/shard_map/while/body/eval_jaxpr/while/body/eval_jaxpr/dot_general | solution.py:144
  853.0 18.3 %fusion.170 = f32[6,160]{1,0:T(8,128)S(1)} fusion(s32[59,708]{1,0:T(8,128)S(1)} %get-tuple-element.621, s32[59,708]{1,0:T(8,128)S(1)} %get-tuple-element.622, s32[59,708]{1,0:T(8,128)S(1)} %constant_dynamic-slice_fusion.5, f32[6,708,708]{2,0,1:T(8,128)} %get-tuple-element.675, s32[]{:T(128)S(6)} %select_n.79, f32[6,160]{1,0:T(8,128)S(1)} %get-tuple-element.664, ...), kind=kOutput, calls=%fused_computation.26.clone.1 | convolution fusion | flops 514632960 | bytes 1958933 | tf_op jit(solution)/shard_map/while/body/eval_jaxpr/while/body/eval_jaxpr/dot_general | solution.py:144
  873.4 18.3 %fusion.170 = f32[6,160]{1,0:T(8,128)S(1)} fusion(s32[59,708]{1,0:T(8,128)S(1)} %get-tuple-element.621, s32[59,708]{1,0:T(8,128)S(1)} %get-tuple-element.622, s32[59,708]{1,0:T(8,128)S(1)} %constant_dynamic-slice_fusion.5, f32[6,708,708]{2,0,1:T(8,128)} %get-tuple-element.675, s32[]{:T(128)S(6)} %select_n.79, f32[6,160]{1,0:T(8,128)S(1)} %get-tuple-element.664, ...), kind=kOutput, calls=%fused_computation.26.clone.1 | convolution fusion | flops 514632960 | bytes 1958933 | tf_op jit(solution)/shard_map/while/body/eval_jaxpr/while/body/eval_jaxpr/dot_general | solution.py:144
  893.6 61.5 %all-reduce.67 = (f32[384]{0:T(512)}, f32[384]{0:T(512)}, f32[768]{0:T(1024)S(1)}, f32[32,6]{0,1:T(8,128)}, f32[64,6]{0,1:T(8,128)}, /*index=5*/f32[64,6]{0,1:T(...) all-reduce(f32[384]{0:T(512)S(1)} %reduce_sum.459, ...), channel_id=1, replica_groups=mesh['dp'=16,'tensor'=2] {'dp'}, use_global_device_ids=true, to_apply=%region_46.47 | all-reduce | flops 7872 | bytes 62976 | tf_op jit(solution)/shard_map/psum | solution.py:406
  973.2 63.5 %reduce-scatter.21.cloned.1.call-done = f32[48,1536]{1,0:T(8,128)} async-done(((f32[768,1536]{1,0:T(8,128)}), f32[48,1536]{1,0:T(8,128)}) %reduce-scatter.21.cloned.1.call-update) | async-done | bytes 294928 | tf_op jit(solution)/shard_map/reduce_scatter | solution.py:400
  1036.6 79.4 %reduce-scatter.23.cloned.1.call-done = f32[1536,48]{0,1:T(8,128)} async-done(((f32[1536,768]{0,1:T(8,128)}), f32[1536,48]{0,1:T(8,128)}) %reduce-scatter.23.cloned.1.call-update) | async-done | bytes 294928 | tf_op jit(solution)/shard_map/reduce_scatter | solution.py:401
  (467 shorter events, 374.3 us)
Async XLA Ops:
  7.2 284.2 %copy-start = (bf16[768,1536]{1,0:T(8,128)(2,1)S(1)}, bf16[768,1536]{1,0:T(8,128)(2,1)}, u32[]{:S(2)}) copy-start(bf16[768,1536]{1,0:T(8,128)(2,1)} %param.45) | copy-start | bytes 7077892
  7.2 281.0 %all-reduce.73.cloned.1.call-start = ((), (), s32[]{:S(2)}) async-start(), calls=%async_computation.8 | async-start | bytes 4374528 | tf_op jit(solution)/shard_map/psum | solution.py:258
  40.0 162.7 %copy-start.29 = (bf16[708,384]{0,1:T(8,128)(2,1)}, bf16[708,384]{0,1:T(8,128)(2,1)S(1)}, u32[]{:S(2)}) copy-start(bf16[708,384]{0,1:T(8,128)(2,1)S(1)} %copy.78) | copy-start | bytes 1631236
  220.5 153.5 %all-reduce.75.cloned.1.call-start = ((), (), s32[]{:S(2)}) async-start(), calls=%async_computation.9 | async-start | bytes 4374528 | tf_op jit(solution)/shard_map/psum | solution.py:269
  308.8 149.3 %all-reduce.77.cloned.1.call-start = ((), (), s32[]{:S(2)}) async-start(), calls=%async_computation.10 | async-start | bytes 4374528 | tf_op jit(solution)/shard_map/psum | solution.py:293
  392.9 182.4 %all-reduce.79.cloned.1.call-start = ((), (), s32[]{:S(2)}) async-start(), calls=%async_computation.11 | async-start | bytes 4374528 | tf_op jit(solution)/shard_map/psum | solution.py:370
  510.1 460.0 %reduce-scatter.27.cloned.1.call-start = ((), (), s32[]{:S(2)}) async-start(), calls=%async_computation.19 | async-start | bytes 417792
  598.0 373.6 %reduce-scatter.25.cloned.1.call-start = ((), (), s32[]{:S(2)}) async-start(), calls=%async_computation.18 | async-start | bytes 417792
  602.2 370.9 %reduce-scatter.19.cloned.1.call-start = ((), (), s32[]{:S(2)}) async-start(), calls=%async_computation.15 | async-start | bytes 1253376 | tf_op jit(solution)/shard_map/reduce_scatter | solution.py:396
  606.1 367.0 %reduce-scatter.17.cloned.1.call-start = ((), (), s32[]{:S(2)}) async-start(), calls=%async_computation.14 | async-start | bytes 1253376 | tf_op jit(solution)/shard_map/reduce_scatter | solution.py:395
  609.1 364.0 %reduce-scatter.13.cloned.1.call-start = ((), (), s32[]{:S(2)}) async-start(), calls=%async_computation.12 | async-start | bytes 1253376 | tf_op jit(solution)/shard_map/reduce_scatter | solution.py:393
  612.1 361.0 %reduce-scatter.15.cloned.1.call-start = ((), (), s32[]{:S(2)}) async-start(), calls=%async_computation.13 | async-start | bytes 1253376 | tf_op jit(solution)/shard_map/reduce_scatter | solution.py:394
  615.2 421.5 %reduce-scatter.21.cloned.1.call-start = ((), (), s32[]{:S(2)}) async-start(), calls=%async_computation.16 | async-start | bytes 5013504 | tf_op jit(solution)/shard_map/reduce_scatter | solution.py:400
  621.2 494.8 %reduce-scatter.23.cloned.1.call-start = ((), (), s32[]{:S(2)}) async-start(), calls=%async_computation.17 | async-start | bytes 5013504 | tf_op jit(solution)/shard_map/reduce_scatter | solution.py:401
  646.2 246.1 %copy-start.42 = (f32[1,7,7,768]{3,0,2,1:T(1,128)S(1)}, f32[1,7,7,768]{3,0,2,1:T(1,128)}, u32[]{:S(2)}) copy-start(f32[1,7,7,768]{3,0,2,1:T(1,128)} %copy-done.41) | copy-start | bytes 451588
  646.2 246.1 %copy-start.58 = (f32[768]{0:T(1024)S(1)}, f32[768]{0:T(1024)}, u32[]{:S(2)}) copy-start(f32[768]{0:T(1024)} %copy-done.57) | copy-start | bytes 9220
  646.2 246.1 %copy-start.60 = (f32[768]{0:T(1024)S(1)}, f32[768]{0:T(1024)}, u32[]{:S(2)}) copy-start(f32[768]{0:T(1024)} %copy-done.59) | copy-start | bytes 9220
  646.2 246.1 %copy-start.62 = (f32[768]{0:T(1024)S(1)}, f32[768]{0:T(1024)}, u32[]{:S(2)}) copy-start(f32[768]{0:T(1024)} %copy-done.61) | copy-start | bytes 9220
  646.2 246.1 %copy-start.64 = (f32[768]{0:T(1024)S(1)}, f32[768]{0:T(1024)}, u32[]{:S(2)}) copy-start(f32[768]{0:T(1024)} %copy-done.63) | copy-start | bytes 9220
  646.2 246.1 %copy-start.66 = (f32[768]{0:T(1024)S(1)}, f32[768]{0:T(1024)}, u32[]{:S(2)}) copy-start(f32[768]{0:T(1024)} %copy-done.65) | copy-start | bytes 9220
  646.2 246.1 %copy-start.68 = (f32[768]{0:T(1024)S(1)}, f32[768]{0:T(1024)}, u32[]{:S(2)}) copy-start(f32[768]{0:T(1024)} %copy-done.67) | copy-start | bytes 9220
  646.2 246.1 %copy-start.70 = (f32[768]{0:T(1024)S(1)}, f32[768]{0:T(1024)}, u32[]{:S(2)}) copy-start(f32[768]{0:T(1024)} %copy-done.69) | copy-start | bytes 9220
  646.2 246.9 %copy-start.44 = (f32[1,7,7,768]{3,0,2,1:T(1,128)S(1)}, f32[1,7,7,768]{3,0,2,1:T(1,128)}, u32[]{:S(2)}) copy-start(f32[1,7,7,768]{3,0,2,1:T(1,128)} %get-tuple-element.517) | copy-start | bytes 451588
  646.2 246.9 %copy-start.45 = (f32[1,7,7,768]{3,0,2,1:T(1,128)S(1)}, f32[1,7,7,768]{3,0,2,1:T(1,128)}, u32[]{:S(2)}) copy-start(f32[1,7,7,768]{3,0,2,1:T(1,128)} %get-tuple-element.518) | copy-start | bytes 451588
  (104 other events, 1241.1 us)
Sparse Core Ops, SparseCore 0:
  220.6 67.5 all-reduce.72
  308.9 65.0 all-reduce.74
  393.1 65.0 all-reduce.76
  510.3 65.0 all-reduce.78
  598.1 55.7 reduce-scatter.26
  657.7 54.5 reduce-scatter.24
  716.5 57.0 reduce-scatter.18
  777.8 57.1 reduce-scatter.16
  839.2 57.1 reduce-scatter.12
  900.4 57.1 reduce-scatter.14
  962.0 74.5 reduce-scatter.20
  1041.4 74.6 reduce-scatter.22
where the time goes:
time: 1130 us; the launch traced here: 1120 us
  matrix products  424 us (38%)
  waiting for transfers between devices  403 us (36%)
  local copies, waits for them, and re-layouts  114 us (10%)
  other arithmetic  101 us (9%)
  blocking collectives  61.5 us (5%)
  between operations  17.5 us (2%)
    dot_general x12, matrix products, accumulate(): lax.dot_general(grad_part, selector, (((1, 2), (0, 1)), ((), ())), precis...  220 us
    dot_general x12, matrix products, fill(): lax.dot_general(table_low, selector, (((0,), (2,)), ((), ())), preferred_...  104 us
    reduce_scatter x1, waiting for transfers between devices, per_device(): lax.psum_scatter(grad_outer_weight, 'dp', scatter_dimension=1, tiled=True)  79.4 us
    psum x1, waiting for transfers between devices, per_device(): lax.psum(dense(mixture_flat, out_weight), 'tensor')  67.6 us
    psum x1, waiting for transfers between devices, per_device(): lax.psum(dense_back(grad_inner_low, inner_weight), 'tensor')  64.9 us
    psum x1, waiting for transfers between devices, per_device(): lax.psum(dense(activated_low, outer_weight), 'tensor')  64.5 us
    reduce_scatter x1, waiting for transfers between devices, per_device(): lax.psum_scatter(grad_inner_weight, 'dp', scatter_dimension=0, tiled=True)  63.5 us
    psum x1, waiting for transfers between devices, per_device(): grad_encoded = grad_res1 + lax.psum(back_terms, 'tensor')  63.3 us
  transfers between devices with their start and end apart: 12, of which 6 were waited for; matrix products, arithmetic and copies ran while one was open for 27% of the time, Pallas kernels for 0%

commit v1 on v0

v1 whole, which is shorter than its diff:
```python
import functools

import jax
import jax.numpy as jnp
from jax import lax
from jax.experimental import pallas as pl
from jax.experimental.pallas import tpu as pltpu
from jax.sharding import PartitionSpec as P

HEADS = 12
TEXT = 512
GRID_SMALL = 7
GRID_LARGE = 14
BINS_1D = 32
BINS_2D = 64
BIN_WIDTH = 8

F32 = jnp.float32
BF16 = jnp.bfloat16
EPS = 1e-05
NEG = -1000000000.0
HIGHEST = lax.Precision.HIGHEST

D = 768
SEQ = 708
ROWS = 720
KEYS = 768
CHUNKS = ((0, 256), (256, 256), (512, 208))
ORDER = (2, 0, 1)
SUB = 128
PAIR = 128
HL = 6
DL = 384
FL = 1536
MARGIN = 16
MIB = 1024 * 1024


def vmem():
    return pl.BlockSpec(memory_space=pltpu.VMEM)


def anywhere():
    return pl.BlockSpec(memory_space=pl.ANY)


def hbm():
    return pl.BlockSpec(memory_space=pltpu.HBM)


def smem():
    return pl.BlockSpec(memory_space=pltpu.SMEM)


def params(mib):
    return pltpu.CompilerParams(vmem_limit_bytes=mib * MIB)


def sds(shape, dtype):
    return jax.ShapeDtypeStruct(shape, dtype)


TOKEN = jax.ShapeDtypeStruct((8, 128), jnp.float32)


class Order:
    def __init__(self):
        self.token = None

    def __call__(
        self, kernel, operands, in_specs, out_shape, out_specs, mib=10, us=1, after=(), **more
    ):
        operands, in_specs = list(operands), list(in_specs)
        count = len(operands)
        operands += list(after)
        in_specs += [anywhere()] * len(after)
        if self.token is not None:
            operands.append(self.token)
            grid = "grid" in more
            in_specs.append(pl.BlockSpec(TOKEN.shape, lambda *i: (0, 0)) if grid else vmem())
        has_token = self.token is not None
        outs = len(out_shape)

        def body(*refs):
            rest = list(refs)
            del rest[count : count + len(after) + has_token]
            at = count + outs
            rest[at][...] = jnp.zeros(TOKEN.shape, F32)
            del rest[at]
            kernel(*rest)

        token_spec = pl.BlockSpec(TOKEN.shape, lambda *i: (0, 0)) if "grid" in more else vmem()
        got = pl.pallas_call(
            body,
            out_shape=tuple(out_shape) + (TOKEN,),
            in_specs=in_specs,
            out_specs=tuple(out_specs) + (token_spec,),
            compiler_params=params(mib),
            cost_estimate=cost(us),
            **more,
        )(*operands)
        self.token = got[-1]
        return got[:-1]


def dot(a, b):
    return lax.dot_general(a, b, (((1,), (0,)), ((), ())), preferred_element_type=F32)


def dot_nt(a, b):
    return lax.dot_general(a, b, (((1,), (1,)), ((), ())), preferred_element_type=F32)


def dot_tn(a, b):
    return lax.dot_general(a, b, (((0,), (0,)), ((), ())), preferred_element_type=F32)


def cost(us):
    return pl.CostEstimate(flops=int(us * 1.0e6), bytes_accessed=int(us * 1.0e3), transcendentals=0)


def iota(shape, dim):
    return lax.broadcasted_iota(jnp.int32, shape, dim)


def first_lanes():
    return iota((1, PAIR), 1) < 64


def start_all(pairs, sems, first=0):
    copies = [
        pltpu.make_async_copy(src, dst, sems.at[first + i]) for i, (src, dst) in enumerate(pairs)
    ]
    for copy in copies:
        copy.start()
    return copies


def tables_kernel(
    where_ref, tab_ref, boxes_hbm, wo_hbm,
    z_ref, m_ref, o_ref, u_ref, r_ref, mine_ref, o_far, ur_far, r_far,
    box_scr, boxes_ref, wo_ref, ur_ref, sems,
):
    half = DL // 2
    rows = pl.ds(pl.multiple_of(where_ref[1] * half, half), half)
    copies = start_all(
        (
            (boxes_hbm, boxes_ref),
            (wo_hbm.at[rows, :], wo_ref),
        ),
        sems,
    )
    for copy in copies:
        copy.wait()
    mine_ref[...] = wo_ref[...].astype(F32)
    lane = iota((BINS_1D, 768), 1)
    bucket = jnp.where(lane < 640, jnp.clip(lane - 256, -16, 15) + 16, 0)
    line_pick = (bucket == iota((BINS_1D, 768), 0)).astype(BF16)
    line_base = dot(tab_ref[:, 0:BINS_1D], line_pick)
    lane = iota((BINS_2D, PAIR), 1)
    bucket = jnp.clip(lane - 64, -32, 31) + 32
    plane_pick = (bucket == iota((BINS_2D, PAIR), 0)).astype(BF16)
    bases = [
        dot(tab_ref[:, BINS_1D + 64 * plane : BINS_1D + 64 * plane + 64], plane_pick)
        for plane in range(2)
    ]
    first = first_lanes()
    zeros = jnp.zeros((64, PAIR), BF16)
    for h in range(HL):
        spread = jnp.broadcast_to(line_base[h : h + 1, :], (SUB, 768))
        rolled = pltpu.roll(spread, 0, 1, stride=1, stride_axis=0)
        z_ref[h] = rolled[:, :640]
        for plane in range(2):
            spread = jnp.broadcast_to(bases[plane][h : h + 1, :], (64, PAIR))
            for below in range(2):
                one = pltpu.roll(spread, 64 + below, 1, stride=1, stride_axis=0)
                both = jnp.where(first, one, pltpu.roll(one, 64, 1)).astype(BF16)
                start = h * 512 + plane * 256 + below * 128
                m_ref[plane * 64 : plane * 64 + 64, start : start + 128] = both
                m_ref[64 - plane * 64 : 128 - plane * 64, start : start + 128] = zeros
    box_scr[...] = jnp.full((8, KEYS), -1, jnp.int32)
    box_scr[0:2, 0:SEQ] = boxes_ref[...]
    row = iota((512, KEYS), 0)
    value = 8 * (row % 64) + row // 64
    for plane in range(2):
        o_ref[plane * 512 : plane * 512 + 512, :] = (
            value == box_scr[plane : plane + 1, :]
        ).astype(F32).astype(BF16)
    turned = jnp.transpose(box_scr[...].astype(F32))[0:ROWS, :].astype(jnp.int32)
    left = jnp.broadcast_to(turned[:, 0:1], (ROWS, PAIR))
    right = jnp.broadcast_to(turned[:, 1:2], (ROWS, PAIR))
    lane = iota((ROWS, PAIR), 1)
    both = jnp.where(lane < 64, left, right)
    r_ref[0] = left & 7
    r_ref[1] = right & 7
    upper = lax.shift_right_logical(both, 3)
    inner = lane & 63
    u_ref[...] = (upper == inner).astype(F32).astype(BF16)
    ur_ref[...] = (63 - upper == inner).astype(F32).astype(BF16)
    for copy in start_all(((o_ref, o_far), (ur_ref, ur_far), (r_ref, r_far)), sems):
        copy.wait()


def make_tables(order, where, tab, boxes, wo):
    return order(
        tables_kernel,
        (where, tab, boxes, wo),
        [smem(), vmem()] + [hbm()] * 2,
        (
            sds((HL, SUB, 640), F32),
            sds((128, HL * 512), BF16),
            sds((1024, KEYS), BF16),
            sds((ROWS, PAIR), BF16),
            sds((2, ROWS, PAIR), jnp.int32),
            sds((DL // 2, D), F32),
            sds((1024, KEYS), BF16),
            sds((ROWS, PAIR), BF16),
            sds((2, ROWS, PAIR), jnp.int32),
        ),
        [vmem()] * 6 + [hbm()] * 3,
        us=20000,
        scratch_shapes=[
            pltpu.VMEM((8, KEYS), jnp.int32),
            pltpu.VMEM(boxes.shape, jnp.int32),
            pltpu.VMEM((DL // 2, D), BF16),
            pltpu.VMEM((ROWS, PAIR), BF16),
            pltpu.SemaphoreType.DMA((5,)),
        ],
        name="bias_tables",
    )


def copy_kernel(src, dst, scr, sems):
    for pair in ((src, scr), (scr, dst)):
        copy = pltpu.make_async_copy(*pair, sems.at[0])
        copy.start()
        copy.wait()


def pass_on(order, x):
    return order(
        copy_kernel,
        (x,),
        [anywhere()],
        (sds(x.shape, x.dtype),),
        [anywhere()],
        scratch_shapes=[pltpu.VMEM(x.shape, x.dtype), pltpu.SemaphoreType.DMA((1,))],
        name="pass_on",
    )[0]


def text_taps(text_ref, cols):
    taps = {}
    for dilate in range(3):
        for tap in range(3):
            shift = (tap - 1) * (dilate + 1)
            row = text_ref[dilate, tap : tap + 1, cols].astype(F32)
            taps[shift] = row if shift not in taps else taps[shift] + row
    return taps


def text_conv_block(win, taps, sign):
    total = win[8:40] * (taps[0] + 1.0)
    for shift in (-3, -2, -1, 1, 2, 3):
        start = 8 + sign * shift
        total = total + win[start : start + 32] * taps[shift]
    return total


def grid_masks(side):
    place = iota((208, PAIR), 0)
    row = jnp.floor((place.astype(F32) + 0.5) * (1.0 / side)).astype(jnp.int32)
    col = place - row * side
    return (place < side * side, col >= 1, col <= side - 2)


def patch_conv_cols(win, patch_ref, cols, side, sign):
    live, has_left, has_right = grid_masks(side)
    total = None
    for ds in (-1, 0, 1):
        part = None
        for dr in (-1, 0, 1):
            tap = 3 * (dr + 1) + ds + 1
            start = MARGIN + sign * (dr * side + ds)
            term = win[start : start + 208] * patch_ref[tap : tap + 1, cols].astype(F32)
            part = term if part is None else part + term
        if ds * sign == -1:
            part = jnp.where(has_left, part, 0.0)
        if ds * sign == 1:
            part = jnp.where(has_right, part, 0.0)
        total = part if total is None else total + part
    return jnp.where(live, total, 0.0)


def fill_patches(patch_scr, source, count):
    zero = jnp.zeros((MARGIN, D), F32)
    patch_scr[0:MARGIN, :] = zero
    patch_scr[MARGIN + 208 : MARGIN + 208 + MARGIN, :] = zero
    live = iota((208, PAIR), 0) < count
    for c in range(D // PAIR):
        cols = slice(c * PAIR, c * PAIR + PAIR)
        patch_scr[MARGIN : MARGIN + 208, cols] = jnp.where(live, source(cols), 0.0)


def load_page(x_ref, count, text_scr, patch_scr, raw_scr):
    zero8 = jnp.zeros((8, D), F32)
    text_scr[0:8, :] = zero8
    text_scr[520:528, :] = zero8
    for b in range(TEXT // 64):
        text_scr[8 + 64 * b : 72 + 64 * b, :] = x_ref[64 * b : 64 * b + 64, :].astype(F32)
    raw_scr[...] = jnp.zeros((208, D), F32)
    raw_scr[0 : SEQ - TEXT, :] = x_ref[TEXT:SEQ, :].astype(F32)
    fill_patches(patch_scr, lambda cols: raw_scr[:, cols], count)


PAGE_SCRATCH = [
    pltpu.VMEM((528, D), F32),
    pltpu.VMEM((208 + 2 * MARGIN, D), F32),
    pltpu.VMEM((208, D), F32),
]


def by_grid(count, patches):
    large = count == GRID_LARGE * GRID_LARGE

    @pl.when(large)
    def _():
        patches(GRID_LARGE)

    @pl.when(jnp.logical_not(large))
    def _():
        patches(GRID_SMALL)


def encode_kernel(
    count_ref, x_hbm, text_ref, patch_ref, bias_ref, wq_hbm, wk_hbm, wv_hbm,
    q0, q1, q2, k_ref, v_ref,
    e0_far, e1_far, e2_far, l0_far, l1_far, l2_far, q0_far, q1_far, q2_far, k_far, v_far,
    text_scr, patch_scr, raw_scr, x_ref, wq_ref, wk_ref, wv_ref,
    e0, e1, e2, l0, l1, l2, sems,
):
    copies = start_all(
        ((x_hbm, x_ref), (wq_hbm, wq_ref), (wk_hbm, wk_ref), (wv_hbm, wv_ref)), sems
    )
    count = count_ref[0]
    copies[0].wait()
    load_page(x_ref, count, text_scr, patch_scr, raw_scr)

    for c in range(2):
        cols = slice(c * 384, c * 384 + 384)
        taps = text_taps(text_ref, cols)

        def one(b, carry, cols=cols, taps=taps, out=None, first=0):
            base = pl.multiple_of(b * 32, 32)
            win = text_scr[pl.ds(first + base, 48), cols]
            out[pl.ds(base, 32), cols] = text_conv_block(win, taps, 1)
            return carry

        lax.fori_loop(0, 8, functools.partial(one, out=e0, first=0), 0)
        lax.fori_loop(0, 8, functools.partial(one, out=e1, first=256), 0)

    def patches(side):
        for c in range(D // PAIR):
            cols = slice(c * PAIR, c * PAIR + PAIR)
            e2[:, cols] = raw_scr[:, cols] + patch_conv_cols(
                patch_scr[:, cols], patch_ref, cols, side, 1
            )

    by_grid(count, patches)
    far = start_all(((e0, e0_far), (e1, e1_far), (e2, e2_far)), sems, 4)
    for copy in copies[1:]:
        copy.wait()
    for i, ((start, rows), e, low, low_far, q, q_far) in enumerate(
        zip(
            CHUNKS, (e0, e1, e2), (l0, l1, l2), (l0_far, l1_far, l2_far), (q0, q1, q2),
            (q0_far, q1_far, q2_far),
        )
    ):
        enc = e[...].astype(BF16)
        low[...] = enc
        query = (dot(enc, wq_ref[...]) + bias_ref[0:1, :]).astype(BF16)
        q[...] = query * jnp.asarray(0.125, BF16)
        k_ref[start : start + rows, :] = dot(enc, wk_ref[...]).astype(BF16)
        value = dot(enc, wv_ref[...]) + bias_ref[1:2, :]
        v_ref[start : start + rows, :] = value.astype(BF16)
        far += start_all(((low, low_far), (q, q_far)), sems, 7 + 2 * i)
    k_ref[ROWS:KEYS, :] = jnp.zeros((KEYS - ROWS, DL), BF16)
    v_ref[ROWS:KEYS, :] = jnp.zeros((KEYS - ROWS, DL), BF16)
    far += start_all(((k_ref, k_far), (v_ref, v_far)), sems, 13)
    for copy in far:
        copy.wait()


def encode(order, count, x, text, patch, bias, wq, wk, wv):
    chunk = lambda width, dtype: tuple(sds((rows, width), dtype) for _, rows in CHUNKS)
    scratch = lambda width, dtype: [pltpu.VMEM((rows, width), dtype) for _, rows in CHUNKS]
    keys = (sds((KEYS, DL), BF16), sds((KEYS, DL), BF16))
    out = order(
        encode_kernel,
        (count, x, text, patch, bias, wq, wk, wv),
        [smem(), hbm()] + [vmem()] * 3 + [hbm()] * 3,
        chunk(DL, BF16) + keys + chunk(D, F32) + chunk(D, BF16) + chunk(DL, BF16) + keys,
        [vmem()] * 5 + [hbm()] * 11,
        scratch_shapes=PAGE_SCRATCH
        + [pltpu.VMEM((SEQ, D), BF16)]
        + [pltpu.VMEM((D, DL), BF16)] * 3
        + scratch(D, F32)
        + scratch(D, BF16)
        + [pltpu.SemaphoreType.DMA((15,))],
        mib=18,
        us=8000,
        name="encode_project",
    )
    return out[0:5], out[5:8], out[8:11], out[11:]


def bias_rows(e, r_col, k, rows):
    step = 2 * k + (iota((rows, PAIR), 1) >= 64).astype(jnp.int32)
    return jnp.where(step >= r_col, e[0], e[1]).astype(BF16)


def line_rows(z_ref, h, sub, rows):
    groups = [min(max(g - sub + 2, 0), 4) for g in range(KEYS // SUB)]
    return jnp.concatenate([z_ref[h, 0:rows, g * 128 : g * 128 + 128] for g in groups], axis=1)


def attend_kernel(
    start, rows, count_ref, q_ref, k_ref, v_ref, u_ref, r_ref, m_ref, o_ref, z_ref,
    p_hbm, mix_ref, low_far, p_scr, low_scr, sems,
):
    live = iota((1, KEYS), 1) < TEXT + count_ref[0]
    first = first_lanes()
    r_w = r_ref[0, start : start + rows, :]
    r_h = r_ref[1, start : start + rows, :]
    copies = []
    u = u_ref[start : start + rows, :]
    for pair in range(HL // 2):
        cols = slice(pair * PAIR, pair * PAIR + PAIR)
        q = q_ref[:, cols]
        k = k_ref[:, cols]
        v = v_ref[:, cols]
        mixed = []
        for half in range(2):
            h = 2 * pair + half
            mine = first if half == 0 else jnp.logical_not(first)
            qm = jnp.where(mine, q, jnp.zeros_like(q))
            e = dot(u, m_ref[:, h * 512 : h * 512 + 512])
            parts = [bias_rows((e[:, 0:128], e[:, 128:256]), r_w, kk, rows) for kk in range(4)]
            parts += [bias_rows((e[:, 256:384], e[:, 384:512]), r_h, kk, rows) for kk in range(4)]
            picked = jnp.concatenate(parts, axis=1)
            s = dot(picked, o_ref[...]) + dot_nt(qm, k)
            pieces = []
            for at in range(0, rows, SUB):
                size = min(SUB, rows - at)
                pieces.append(line_rows(z_ref, h, (start + at) // SUB, size))
            s = s + jnp.concatenate(pieces, axis=0)
            s = jnp.where(live, s, NEG)
            top = jnp.max(s, axis=1, keepdims=True)
            ex = jnp.exp(s - top)
            total = jnp.sum(ex, axis=1, keepdims=True)
            prob = (ex * (1.0 / total)).astype(BF16)
            p_scr[h] = prob
            copies.append(pltpu.make_async_copy(p_scr.at[h], p_hbm.at[h], sems.at[h]))
            copies[-1].start()
            mixed.append(dot(prob, v))
        low = jnp.where(first, mixed[0], mixed[1]).astype(BF16)
        low_scr[:, cols] = low
        mix_ref[:, cols] = low.astype(F32)
    copies.append(pltpu.make_async_copy(low_scr, low_far, sems.at[HL]))
    copies[-1].start()
    for copy in copies:
        copy.wait()


def attend(order, c, count, q, k, v, u, r, m, o, z):
    start, rows = CHUNKS[c]
    return order(
        functools.partial(attend_kernel, start, rows),
        (count, q, k, v, u, r, m, o, z),
        [smem()] + [vmem()] * 8,
        (sds((HL, rows, KEYS), BF16), sds((rows, DL), F32), sds((rows, DL), BF16)),
        (hbm(), vmem(), hbm()),
        scratch_shapes=[
            pltpu.VMEM((HL, rows, KEYS), BF16),
            pltpu.VMEM((rows, DL), BF16),
            pltpu.SemaphoreType.DMA((HL + 1,)),
        ],
        mib=14,
        name=f"attend_{c}",
    )


def feed_kernel(
    where_ref, own_ref, other_ref, enc_hbm, vec_ref, wo_ref, wo_a_ref, wo_b_ref, wi_ref, bi_ref,
    w2_ref, xhat_ref, rstd_ref, hlow_ref, act_ref, slope_ref, part_ref, enc_ref, sems,
):
    (copy,) = start_all(((enc_hbm, enc_ref),), sems)
    half = where_ref[0]
    core = where_ref[1]
    own = dot(own_ref[...].astype(BF16), wo_ref[...])
    other = other_ref[...].astype(BF16)
    low = jnp.where(core == 0, wo_a_ref[...], wo_b_ref[...]).astype(BF16)
    high = jnp.where(core == 0, wo_b_ref[...], wo_a_ref[...]).astype(BF16)
    other = dot(other, jnp.concatenate([low, high], axis=0))
    attended = jnp.where(half == 0, own, other) + jnp.where(half == 0, other, own)
    copy.wait()
    v = enc_ref[...] + (attended + vec_ref[0:1, :])
    centre = v - jnp.mean(v, axis=1, keepdims=True)
    rstd = lax.rsqrt(jnp.mean(centre * centre, axis=1, keepdims=True) + EPS)
    xhat = centre * rstd
    xhat_ref[...] = xhat
    rstd_ref[...] = jnp.broadcast_to(rstd, rstd_ref.shape)
    hlow = (xhat * vec_ref[1:2, :] + vec_ref[2:3, :]).astype(BF16)
    hlow_ref[...] = hlow
    total = None
    for n in range(FL // 512):
        cols = slice(n * 512, n * 512 + 512)
        pre = dot(hlow, wi_ref[:, cols]) + bi_ref[0:1, cols]
        gate = 0.5 + 0.5 * lax.erf(pre * 0.7071067811865476)
        slope_ref[:, cols] = gate + pre * (0.3989422804014327 * jnp.exp(-0.5 * pre * pre))
        act = (pre * gate).astype(BF16)
        act_ref[:, cols] = act
        term = dot(act, w2_ref[cols, :])
        total = term if total is None else total + term
    part_ref[...] = total


def feed(order, c, where, own, other, enc, vec, wo, wo_a, wo_b, wi, bi, w2):
    _, rows = CHUNKS[c]
    return order(
        feed_kernel,
        (where, own, other, enc, vec, wo, wo_a, wo_b, wi, bi, w2),
        [smem()] + [vmem()] * 2 + [hbm()] + [vmem()] * 7,
        (
            sds((rows, D), F32),
            sds((rows, 128), F32),
            sds((rows, D), BF16),
            sds((rows, FL), BF16),
            sds((rows, FL), F32),
            sds((rows, D), F32),
        ),
        [vmem()] * 6,
        scratch_shapes=[pltpu.VMEM((rows, D), F32), pltpu.SemaphoreType.DMA((1,))],
        name=f"feed_{c}",
    )


def norm_back(dy, xhat, rstd, gain):
    dxh = dy * gain
    return rstd * (
        dxh
        - jnp.mean(dxh, axis=1, keepdims=True)
        - xhat * jnp.mean(dxh * xhat, axis=1, keepdims=True)
    )


def col_sum(x):
    return jnp.sum(x, axis=0, keepdims=True)


def feed_back_kernel(
    start, rows, first, count_ref, own_ref, other_ref, xhat1_ref, cot_ref, vec_ref, w2_ref,
    slope_ref, wi_ref, *rest,
):
    if not first:
        rest = rest[1:]
    out_ref, dres_ref, g2_ref, g1_ref, part_ref, sums_ref = rest
    place = start + iota((rows, 1), 0)
    live = place < TEXT + count_ref[0]
    hidden = xhat1_ref[...] * vec_ref[1:2, :] + vec_ref[2:3, :]
    v = hidden + ((own_ref[...] + other_ref[...]) + vec_ref[3:4, :])
    centre = v - jnp.mean(v, axis=1, keepdims=True)
    rstd = lax.rsqrt(jnp.mean(centre * centre, axis=1, keepdims=True) + EPS)
    xhat = centre * rstd
    y = xhat * vec_ref[4:5, :] + vec_ref[5:6, :]
    out_ref[0:rows, :] = jnp.where(live, y, 0.0).astype(BF16)
    dy = jnp.where(live, cot_ref[0:rows, :].astype(F32), 0.0)
    sums_ref[...] = jnp.zeros(sums_ref.shape, F32)
    sums_ref[2:3, 0:D] = col_sum(dy * xhat)
    sums_ref[3:4, 0:D] = col_sum(dy)
    dres = norm_back(dy, xhat, rstd, vec_ref[4:5, :])
    dres_ref[...] = dres
    sums_ref[1:2, 0:D] = col_sum(dres)
    g2 = dres.astype(BF16)
    g2_ref[...] = g2
    total = None
    for n in range(FL // 512):
        cols = slice(n * 512, n * 512 + 512)
        d_inner = dot_nt(g2, w2_ref[cols, :]) * slope_ref[:, cols]
        sums_ref[0:1, cols] = col_sum(d_inner)
        g1 = d_inner.astype(BF16)
        g1_ref[:, cols] = g1
        term = dot_nt(g1, wi_ref[:, cols])
        total = term if total is None else total + term
    part_ref[...] = total


def feed_back(order, c, count, own, other, xhat1, cot, vec, w2, slope, wi, out_so_far):
    start, rows = CHUNKS[c]
    block = pl.BlockSpec((256, D), lambda i: (start // 256, 0))
    whole = lambda a: pl.BlockSpec(a.shape, lambda i: (0, 0))
    shapes = (
        sds((SEQ, D), BF16),
        sds((rows, D), F32),
        sds((rows, D), BF16),
        sds((rows, FL), BF16),
        sds((rows, D), F32),
        sds((8, FL), F32),
    )
    operands = [count, own, other, xhat1, cot, vec, w2, slope, wi]
    specs = [smem()] + [vmem()] * 3 + [block] + [vmem()] * 4
    aliases = {}
    if out_so_far is not None:
        operands.append(out_so_far)
        specs.append(anywhere())
        aliases = {9: 0}
    return order(
        functools.partial(feed_back_kernel, start, rows, out_so_far is None),
        operands,
        specs,
        shapes,
        [block] + [vmem()] * 5,
        grid=(1,),
        input_output_aliases=aliases,
        us=15000 if c == ORDER[0] else 1,
        name=f"feed_back_{c}",
    )


def store_slabs(slab, core, grad, keep_ref, send_ref):
    for i in range(D // (2 * slab)):
        even = grad[2 * i * slab : (2 * i + 1) * slab]
        odd = grad[(2 * i + 1) * slab : (2 * i + 2) * slab]
        keep_ref[i * slab : (i + 1) * slab, :] = jnp.where(core == 0, even, odd)
        send_ref[i * slab : (i + 1) * slab, :] = jnp.where(core == 0, odd, even)


def tn_sum(lefts, rights):
    total = None
    for left, right in zip(lefts, rights):
        term = dot_tn(left[...], right[...].astype(BF16))
        total = term if total is None else total + term
    return total


def put_grads(slab, where_ref, grad, outs):
    if slab is None:
        outs[0][...] = grad
    else:
        store_slabs(slab, where_ref[1], grad, *outs)


def chunk_grads_kernel(slab, has_total, where_ref, left_ref, right_ref, *refs):
    grad = dot_tn(left_ref[...], right_ref[...])
    if has_total:
        grad = refs[0][...] + grad
    put_grads(slab, where_ref, grad, refs[has_total:])


def chunk_grads(order, slab, where, left, right, total, last, name):
    width = right.shape[1]
    block = 512
    piece = lambda rows: pl.BlockSpec((rows, block), lambda i: (0, i))
    whole = pl.BlockSpec(left.shape, lambda i: (0, 0))
    apart = last and slab is not None
    rows, count = (D // 2, 2) if apart else (D, 1)
    operands, specs, aliases = [where, left, right], [smem(), whole, piece(right.shape[0])], {}
    if total is not None:
        operands.append(total)
        specs.append(piece(D))
        if not apart:
            aliases = {3: 0}
    return order(
        functools.partial(chunk_grads_kernel, slab if apart else None, total is not None),
        operands,
        specs,
        (sds((rows, width), F32),) * count,
        [piece(rows)] * count,
        grid=(width // block,),
        input_output_aliases=aliases,
        mib=16,
        name=name,
    )


def attention_grads_kernel(slab, where_ref, *refs):
    low, dq, (dk_ref, dv_ref), g0, mix = refs[0:3], refs[3:6], refs[6:8], refs[8:11], refs[11:14]
    outs = refs[14:]
    half = len(outs) // 2
    step = pl.program_id(0)
    chunks = lambda ref: [ref.at[start : start + rows] for start, rows in CHUNKS]
    todo = (
        (low, dq, outs[:half]),
        (low, chunks(dk_ref), outs[:half]),
        (low, chunks(dv_ref), outs[half:]),
        (g0, mix, outs[half:]),
    )
    for i, (lefts, rights, out) in enumerate(todo):

        @pl.when(step == i)
        def _(lefts=lefts, rights=rights, out=out):
            put_grads(slab, where_ref, tn_sum(lefts, rights), out)


def attention_grads(order, slab, where, enc_low, dq, dk, dv, g0, mix):
    operands = [*enc_low, *dq, dk, dv, *g0, *mix]
    rows, count = (D, 1) if slab is None else (D // 2, 2)
    return order(
        functools.partial(attention_grads_kernel, slab),
        (where, *operands),
        [smem()] + [pl.BlockSpec(a.shape, lambda i: (0, 0)) for a in operands],
        (sds((rows, D), F32),) * (2 * count),
        [pl.BlockSpec((rows, DL), lambda i: (0, jnp.minimum(i, 1)))] * count
        + [pl.BlockSpec((rows, DL), lambda i: (0, jnp.maximum(i - 2, 0)))] * count,
        grid=(4,),
        mib=24,
        name="attention_grads",
    )


SMALL = 40


def halve_kernel(slabs, high, where_bit, extra, where_ref, *refs):
    small_ref = None
    if extra == "first":
        small_ref, *refs = refs
    *pairs, own_ref, out_ref = refs
    mine = where_ref[where_bit]
    total = pairs[0].shape[0] - (SMALL if extra == "more" else 0)
    run = high * (total // slabs)
    at = 0
    for a_ref, b_ref in zip(pairs[0::2], pairs[1::2]):
        cols = slice(at, at + a_ref.shape[1])
        at += a_ref.shape[1]
        for i in range(slabs // (2 * high)):
            for ref, which in ((own_ref, mine), (out_ref, 1 - mine)):
                rows = pl.ds(pl.multiple_of((2 * i + which) * run, 8), run)
                ref[i * run : (i + 1) * run, cols] = a_ref[rows, :] + b_ref[rows, :]
    if extra is not None:
        small = small_ref[...] if extra == "first" else pairs[0][total:] + pairs[1][total:]
        own_ref[total // 2 :, :] = small
        out_ref[total // 2 :, :] = small


def halve(order, where, pairs, slabs, high, where_bit, first, width, name, small=None, extra=None):
    rows = pairs[0][0].shape[0]
    out_rows = rows // 2
    operands, specs = [where], [smem()]
    if extra == "first":
        out_rows = rows // 2 + SMALL
        operands.append(small)
        specs.append(vmem())
    if extra == "more":
        out_rows = (rows - SMALL) // 2 + SMALL
    if len(pairs) == 1 and extra is None:
        block = 512 if width % 512 == 0 and first % 512 == 0 else 384
        at = first // block
        specs += [pl.BlockSpec((rows, block), lambda i: (0, at + i))] * 2
        grid = (width // block,)
    else:
        block = width
        specs += [pl.BlockSpec(a.shape, lambda i: (0, 0)) for pair in pairs for a in pair]
        grid = (1,)
    half = pl.BlockSpec((out_rows, block), lambda i: (0, i))
    return order(
        functools.partial(halve_kernel, slabs, high, where_bit, extra),
        operands + [a for pair in pairs for a in pair],
        specs,
        (sds((out_rows, width), F32),) * 2,
        [half, half],
        grid=grid,
        mib=12,
        name=name,
    )


def norm_back_kernel(
    dres2_ref, own_ref, other_ref, xhat_ref, rstd_ref, vec_ref, wo_ref,
    dres1_far, g0_ref, dmix_ref, sums_ref, dres1_ref, sems,
):
    dhid = dres2_ref[...] + (own_ref[...] + other_ref[...])
    xhat = xhat_ref[...]
    sums_ref[...] = jnp.zeros(sums_ref.shape, F32)
    sums_ref[1:2, :] = col_sum(dhid * xhat)
    sums_ref[2:3, :] = col_sum(dhid)
    dres1 = norm_back(dhid, xhat, rstd_ref[:, 0:1], vec_ref[1:2, :])
    dres1_ref[...] = dres1
    (copy,) = start_all(((dres1_ref, dres1_far),), sems)
    sums_ref[0:1, :] = col_sum(dres1)
    g0 = dres1.astype(BF16)
    g0_ref[...] = g0
    dmix_ref[...] = dot_nt(g0, wo_ref[...]).astype(BF16)
    copy.wait()


def norm_one_back(order, c, dres2, own, other, xhat, rstd, vec, wo):
    _, rows = CHUNKS[c]
    return order(
        norm_back_kernel,
        (dres2, own, other, xhat, rstd, vec, wo),
        [vmem()] * 7,
        (sds((rows, D), F32), sds((rows, D), BF16), sds((rows, DL), BF16), sds((8, D), F32)),
        [hbm()] + [vmem()] * 3,
        scratch_shapes=[pltpu.VMEM((rows, D), F32), pltpu.SemaphoreType.DMA((1,))],
        us=20000 if c == ORDER[0] else 1,
        name=f"norm_back_{c}",
    )


def attend_back_kernel(
    start, rows, first, dmix_ref, p_hbm, q_ref, k_ref, v_ref, ur_ref, r_ref, o_ref, *rest,
):
    if not first:
        dk_in, dv_in, dm_in, dz_in = rest[:4]
        rest = rest[4:]
    dq_ref, dk_ref, dv_ref, dm_ref, dz_ref, p_scr, sems = rest
    copies = [pltpu.make_async_copy(p_hbm.at[h], p_scr.at[h], sems.at[h]) for h in range(HL)]
    for copy in copies:
        copy.start()
    if first:
        dz_ref[...] = jnp.zeros(dz_ref.shape, F32)
    else:
        dz_ref[...] = dz_in[...]

    lanes = first_lanes()
    r_w = r_ref[0, start : start + rows, :]
    r_h = r_ref[1, start : start + rows, :]
    upper = (iota((rows, PAIR), 1) >= 64).astype(jnp.int32)
    ur = ur_ref[start : start + rows, :]
    for pair in range(HL // 2):
        cols = slice(pair * PAIR, pair * PAIR + PAIR)
        q = q_ref[:, cols]
        k = k_ref[:, cols]
        v = v_ref[:, cols]
        dmix = dmix_ref[:, cols]
        dq_total = None
        dk_total = None if first else dk_in[:, cols]
        dv_total = None if first else dv_in[:, cols]
        for half in range(2):
            h = 2 * pair + half
            mine = lanes if half == 0 else jnp.logical_not(lanes)
            pick = lambda a: jnp.where(mine, a, jnp.zeros_like(a))
            dmix_m = pick(dmix)
            copies[h].wait()
            prob = p_scr[h]
            dprob = dot_nt(dmix_m, v)
            prob_f = prob.astype(F32)
            both = prob_f * dprob
            ds = both - prob_f * jnp.sum(both, axis=1, keepdims=True)
            low = ds.astype(BF16)
            dq = dot(low, pick(k))
            dk = dot_tn(low, pick(q))
            dv = dot_tn(prob, dmix_m)
            dq_total = dq if dq_total is None else dq_total + dq
            dk_total = dk if dk_total is None else dk_total + dk
            dv_total = dv if dv_total is None else dv_total + dv
            for at in range(0, rows, SUB):
                size = min(SUB, rows - at)
                sub = (start + at) // SUB
                sums = {}
                for g in range(KEYS // SUB):
                    group = min(max(g - sub + 2, 0), 4)
                    piece = ds[at : at + size, g * 128 : g * 128 + 128]
                    sums[group] = piece if group not in sums else sums[group] + piece
                for group, piece in sums.items():
                    dz_ref[h, 0:size, group * 128 : group * 128 + 128] += piece
            dbias = dot_nt(low, o_ref[...])
            parts = []
            for plane, r_col in ((0, r_w), (1, r_h)):
                same = None
                under = None
                for kk in range(4):
                    base = plane * 512 + kk * 128
                    piece = dbias[:, base : base + 128]
                    ok = (2 * kk + upper) >= r_col
                    yes = jnp.where(ok, piece, 0.0)
                    no = jnp.where(ok, 0.0, piece)
                    same = yes if same is None else same + yes
                    under = no if under is None else under + no
                parts += [same, under]
            dm = dot_tn(ur, jnp.concatenate(parts, axis=1).astype(BF16))
            at = slice(h * 512, h * 512 + 512)
            dm_ref[:, at] = dm if first else dm_in[:, at] + dm
        dq_ref[:, cols] = dq_total * 0.125
        dk_ref[:, cols] = dk_total
        dv_ref[:, cols] = dv_total


def attend_back(order, c, dmix, p, q, k, v, ur, r, o, carry):
    start, rows = CHUNKS[c]
    operands = [dmix, p, q, k, v, ur, r, o]
    aliases = {}
    if carry is not None:
        operands += list(carry)
        aliases = {8 + i: 1 + i for i in range(4)}
    return order(
        functools.partial(attend_back_kernel, start, rows, carry is None),
        operands,
        [vmem(), hbm()] + [vmem()] * (len(operands) - 2),
        (
            sds((rows, DL), F32),
            sds((KEYS, DL), F32),
            sds((KEYS, DL), F32),
            sds((128, HL * 512), F32),
            sds((HL, SUB, 640), F32),
        ),
        [vmem()] * 5,
        scratch_shapes=[pltpu.VMEM((HL, rows, KEYS), BF16), pltpu.SemaphoreType.DMA((HL,))],
        input_output_aliases=aliases,
        mib=14,
        name=f"attend_back_{c}",
    )


def table_sums_kernel(dm_ref, dz_ref, out_ref):
    lane = iota((PAIR, BINS_2D), 0)
    plane_bin = jnp.clip(lane - 64, -32, 31) + 32
    plane_pick = (plane_bin == iota((PAIR, BINS_2D), 1)).astype(F32)
    lane = iota((512, BINS_1D), 0)
    line_bin = jnp.clip(lane - 256, -16, 15) + 16
    line_pick = (line_bin == iota((512, BINS_1D), 1)).astype(F32)
    first = first_lanes()
    flip = (iota((SUB, SUB), 0) + iota((SUB, SUB), 1) == SUB - 1).astype(F32)
    bin_id = iota((1, BINS_1D), 1)
    exact = functools.partial(
        lax.dot_general,
        dimension_numbers=(((1,), (0,)), ((), ())),
        precision=HIGHEST,
        preferred_element_type=F32,
    )
    out_ref[...] = jnp.zeros(out_ref.shape, F32)
    for h in range(HL):
        z = dz_ref[h]
        left = jnp.sum(z[:, 0:128])
        right = jnp.sum(z[:, 512:640])
        band = jnp.concatenate([z[:, 128:512], jnp.zeros((SUB, 128), F32)], axis=1)
        band = pltpu.roll(exact(flip, band), 512 - 127 + 128, 1, stride=1, stride_axis=0)
        line = exact(col_sum(band), line_pick)
        line = line + jnp.where(bin_id == 0, left, 0.0) + jnp.where(bin_id == 31, right, 0.0)
        out_ref[h : h + 1, 0:BINS_1D] = line
        for plane in range(2):
            total = None
            for below in range(2):
                at = h * 512 + plane * 256 + below * 128
                g = dm_ref[plane * 64 : plane * 64 + 64, at : at + 128]
                g = jnp.where(first, g + pltpu.roll(g, 64, 1), 0.0)
                g = pltpu.roll(g, 1 - below, 1, stride=1, stride_axis=0)
                total = g if total is None else total + g
            summed = exact(col_sum(total), plane_pick)
            at = BINS_1D + plane * 64
            out_ref[h : h + 1, at : at + 64] = summed


def table_sums(order, dm, dz):
    return order(
        table_sums_kernel,
        (dm, dz),
        [vmem()] * 2,
        (sds((8, 256), F32),),
        [vmem()],
        name="table_sums",
    )[0]


def project_back_kernel(
    q0, q1, q2, dk_ref, dv_ref, wq_hbm, wk_hbm, wv_hbm, part_ref, bias_ref,
    wq_ref, wk_ref, wv_ref, sems,
):
    copies = [
        pltpu.make_async_copy(src, dst, sems.at[i])
        for i, (src, dst) in enumerate(
            zip((wq_hbm, wk_hbm, wv_hbm), (wq_ref, wk_ref, wv_ref))
        )
    ]
    for copy in copies:
        copy.start()
    sum_q = None
    sum_v = None
    for i, ((start, rows), dq) in enumerate(zip(CHUNKS, (q0, q1, q2))):
        query = dq[...]
        value = dv_ref[start : start + rows, :]
        sum_q = col_sum(query) if sum_q is None else sum_q + col_sum(query)
        sum_v = col_sum(value) if sum_v is None else sum_v + col_sum(value)
        query = query.astype(BF16)
        key = dk_ref[start : start + rows, :].astype(BF16)
        value = value.astype(BF16)
        if i == 0:
            for copy in copies:
                copy.wait()
        part_ref[start : start + rows, :] = (
            dot_nt(query, wq_ref[...]) + dot_nt(key, wk_ref[...]) + dot_nt(value, wv_ref[...])
        )
    bias_ref[...] = jnp.zeros(bias_ref.shape, F32)
    bias_ref[0:1, 0:DL] = sum_q
    bias_ref[0:1, DL:D] = sum_v


def project_back(order, dq, dk, dv, wq, wk, wv):
    return order(
        project_back_kernel,
        (*dq, dk, dv, wq, wk, wv),
        [vmem()] * 5 + [hbm()] * 3,
        (sds((ROWS, D), F32), sds((8, D), F32)),
        [vmem()] * 2,
        scratch_shapes=[pltpu.VMEM((D, DL), BF16)] * 3 + [pltpu.SemaphoreType.DMA((3,))],
        name="project_back",
    )


def taps_kernel(
    count_ref, x_hbm, pt, r0_far, r1_far, r2_far, out_ref,
    text_scr, patch_scr, raw_scr, x_ref, r0, r1, r2, sems,
):
    count = count_ref[0]
    copies = start_all(((x_hbm, x_ref), (r0_far, r0), (r1_far, r1), (r2_far, r2)), sems)
    copies[0].wait()
    load_page(x_ref, count, text_scr, patch_scr, raw_scr)
    for copy in copies[1:]:
        copy.wait()
    out_ref[...] = jnp.zeros(out_ref.shape, F32)
    shifts = tuple(range(-3, 4))
    for c in range(2):
        cols = slice(c * 384, c * 384 + 384)

        def one(b, sums, cols=cols, res=None, first=0):
            base = pl.multiple_of(b * 32, 32)
            win = text_scr[pl.ds(first + base, 48), cols]
            grad = pt[pl.ds(first + base, 32), cols] + 0.5 * res[pl.ds(base, 32), cols]
            out = []
            for shift, total in zip(shifts, sums):
                prod = grad * win[8 + shift : 40 + shift]
                out.append(total + jnp.sum(prod.reshape(4, 8, 384), axis=0))
            return tuple(out)

        sums = tuple(jnp.zeros((8, 384), F32) for _ in shifts)
        sums = lax.fori_loop(0, 8, functools.partial(one, res=r0, first=0), sums)
        sums = lax.fori_loop(0, 8, functools.partial(one, res=r1, first=256), sums)
        for dilate in range(3):
            for tap in range(3):
                row = 3 * dilate + tap
                total = sums[3 + (tap - 1) * (dilate + 1)]
                out_ref[row : row + 1, cols] = col_sum(total)

    def patches(side):
        live, has_left, has_right = grid_masks(side)
        for c in range(D // PAIR):
            cols = slice(c * PAIR, c * PAIR + PAIR)
            win = patch_scr[:, cols]
            grad = jnp.where(live, pt[TEXT:ROWS, cols] + 0.5 * r2[:, cols], 0.0)
            for ds in (-1, 0, 1):
                masked = grad
                if ds == -1:
                    masked = jnp.where(has_left, grad, 0.0)
                if ds == 1:
                    masked = jnp.where(has_right, grad, 0.0)
                for dr in (-1, 0, 1):
                    row = 9 + 3 * (dr + 1) + ds + 1
                    at = MARGIN + dr * side + ds
                    out_ref[row : row + 1, cols] = col_sum(masked * win[at : at + 208])

    by_grid(count, patches)


def tap_sums(order, count, x, part, res):
    return order(
        taps_kernel,
        (count, x, part, *res),
        [smem(), hbm(), vmem()] + [hbm()] * 3,
        (sds((24, D), F32),),
        [vmem()],
        scratch_shapes=PAGE_SCRATCH
        + [pltpu.VMEM((SEQ, D), BF16)]
        + [pltpu.VMEM((rows, D), F32) for _, rows in CHUNKS]
        + [pltpu.SemaphoreType.DMA((4,))],
        mib=14,
        name="tap_sums",
    )[0]


def decode_text_kernel(text_ref, p, s, r0, r1, out_ref, text_scr):
    zero8 = jnp.zeros((8, D), F32)
    text_scr[0:8, :] = zero8
    text_scr[520:528, :] = zero8
    for r, at in ((r0, 0), (r1, 256)):
        for b in range(4):
            res = r[64 * b : 64 * b + 64, :]
            rows = slice(at + 64 * b, at + 64 * b + 64)
            text_scr[8 + at + 64 * b : 72 + at + 64 * b, :] = res + (p[rows, :] + s[rows, :])
    for c in range(2):
        cols = slice(c * 384, c * 384 + 384)
        taps = text_taps(text_ref, cols)

        def one(b, carry, cols=cols, taps=taps):
            base = pl.multiple_of(b * 32, 32)
            win = text_scr[pl.ds(base, 48), cols]
            out_ref[pl.ds(base, 32), cols] = text_conv_block(win, taps, -1).astype(BF16)
            return carry

        lax.fori_loop(0, TEXT // 32, one, 0)


def decode_kernel(
    count_ref, text_ref, patch_ref, p, s, r0_far, r1_far, r2_far, out_ref,
    text_scr, patch_scr, raw_scr, r0, r1, r2, sems,
):
    for copy in start_all(((r0_far, r0), (r1_far, r1), (r2_far, r2)), sems):
        copy.wait()
    decode_text_kernel(text_ref, p, s, r0, r1, out_ref, text_scr)
    count = count_ref[0]
    raw_scr[...] = r2[...] + (p[TEXT:ROWS, :] + s[TEXT:ROWS, :])
    fill_patches(patch_scr, lambda cols: raw_scr[:, cols], count)

    def patches(side):
        for c in range(D // PAIR):
            cols = slice(c * PAIR, c * PAIR + PAIR)
            total = raw_scr[:, cols] + patch_conv_cols(patch_scr[:, cols], patch_ref, cols, side, -1)
            out_ref[TEXT:SEQ, cols] = total[0 : SEQ - TEXT].astype(BF16)

    by_grid(count, patches)


def decode(order, count, text_w, patch_w, part, other, res):
    return order(
        decode_kernel,
        (count, text_w, patch_w, part, other, *res),
        [smem()] + [vmem()] * 4 + [hbm()] * 3,
        (sds((SEQ, D), BF16),),
        [vmem()],
        scratch_shapes=PAGE_SCRATCH
        + [pltpu.VMEM((rows, D), F32) for _, rows in CHUNKS]
        + [pltpu.SemaphoreType.DMA((3,))],
        mib=14,
        name="decode",
    )[0]


def swap_tensor(x):
    return lax.ppermute(x, "tensor", [(0, 1), (1, 0)])


def swap_dp(x, bit, dp):
    return lax.ppermute(x, "dp", [(i, i ^ bit) for i in range(dp)])


def swap_core(parts, dp):
    return (parts[0], swap_dp(parts[1], 1, dp)) if len(parts) == 2 else parts


class Scatter:
    def __init__(self, order, dp, where, pair, bits, name, first, width):
        self.order, self.dp, self.where, self.bits, self.name = order, dp, where, bits, name
        self.window = (first, width)
        self.pairs = [pair]
        self.left = list(range(1, dp.bit_length() - 1))

    def join(self, other):
        self.pairs += other.pairs
        self.window = (self.window[0], self.window[1] + other.window[1])

    def step(self, small=None, extra=None):
        if len(self.pairs[0]) == 1:
            return
        bit = self.bits[0]
        self.bits = self.bits[1:]
        at = self.left.index(bit)
        own, out = halve(
            self.order, self.where, self.pairs, 2 ** len(self.left), 2**at, 1 + bit, *self.window,
            f"{self.name}_{bit}", small, extra,
        )
        self.window = (0, self.window[1])
        self.left.remove(bit)
        self.pairs = [(own, swap_dp(out, 2**bit, self.dp))]

    def total(self):
        if len(self.pairs[0]) == 1:
            first, width = self.window
            whole = self.pairs[0][0][:, first : first + width]
            return lax.psum_scatter(whole, "dp", scatter_dimension=0, tiled=True)
        return self.pairs[0][0] + self.pairs[0][1]


def total_kernel(turned, a0, a1, out):
    both = a0[...] + a1[...]
    out[...] = jnp.transpose(both) if turned else both


def total_of(order, part, turned, name):
    pair = part.pairs[0]
    shape = pair[0].shape[::-1] if turned else pair[0].shape
    return order(
        functools.partial(total_kernel, turned), pair, [vmem()] * 2, (sds(shape, F32),), [vmem()],
        name=name,
    )[0]


def attention_totals_kernel(a0, a1, b0, b1, q_ref, k_ref, v_ref, o_ref, small_ref):
    both = a0[...] + a1[...]
    slab = q_ref.shape[0]
    q_ref[...] = both[0:slab, 0:DL]
    k_ref[...] = both[0:slab, DL:D]
    small_ref[...] = both[slab:]
    both = b0[...] + b1[...]
    v_ref[...] = both[:, 0:DL]
    o_ref[...] = jnp.transpose(both[:, DL:D])


def attention_totals(order, query_key, value_out, slab):
    pairs = [a for part in (query_key, value_out) for a in part.pairs[0]]
    plain = sds((slab, DL), F32)
    return order(
        attention_totals_kernel, pairs, [vmem()] * 4,
        (plain, plain, plain, sds((DL, slab), F32), sds((SMALL, D), F32)), [vmem()] * 5,
        name="attention_totals",
    )


def gather_small_kernel(taps, a0, a1, a2, f0, f1, f2, bias, tab, out):
    out[...] = jnp.zeros(out.shape, F32)
    out[0:18, :] = taps[0:18, :]
    out[18:21, :] = (a0[...] + a1[...] + a2[...])[0:3]
    feed_sums = f0[...] + f1[...] + f2[...]
    out[21:24, :] = feed_sums[1:4, 0:D]
    out[24:25, :] = bias[0:1, :]
    out[25:26, :] = feed_sums[0:1, 0:D]
    out[26:27, :] = feed_sums[0:1, D:]
    out[27 : 27 + HL, 0:256] = tab[0:HL, :]


def gather_small(order, *rest):
    return order(
        gather_small_kernel, rest, [vmem()] * 9, (sds((SMALL, D), F32),), [vmem()],
        name="gather_small",
    )[0]


def finish_kernel(
    place_ref, own, core, other, both,
    text, patch, out_b, gain1, shift1, outer_b, gain2, shift2,
    query_b, value_b, inner_b, line, width, height,
):
    small = own[...] + core[...]
    slab = patch.shape[1]
    turn = lambda a: pltpu.roll(a, lax.rem(D - place_ref[0] * slab, D), 1)[:, 0:slab]
    shard = turn(small[0:24])
    taps = shard + turn(other[...] + both[...])
    for i in range(3):
        text[i] = taps[3 * i : 3 * i + 3]
    patch[...] = taps[9:18]
    for i, ref in enumerate((out_b, gain1, shift1, outer_b, gain2, shift2)):
        ref[...] = shard[18 + i]
    query_b[...] = small[24, 0:DL]
    value_b[...] = small[24, DL:D]
    inner_b[0:D] = small[25]
    inner_b[D:FL] = small[26]
    tables = jnp.transpose(small[24:40, 0:256])
    line[...] = tables[0:32, 3 : 3 + HL]
    width[...] = tables[32:96, 3 : 3 + HL]
    height[...] = tables[96:160, 3 : 3 + HL]


def finish(order, place, own, core, other, both, slab):
    f = lambda *shape: sds(shape, F32)
    shapes = (f(3, 3, slab), f(9, slab)) + (f(slab),) * 6
    shapes += (f(DL), f(DL), f(FL), f(32, HL), f(64, HL), f(64, HL))
    return order(
        finish_kernel, (place, own, core, other, both), [smem()] + [vmem()] * 4, shapes,
        [vmem()] * 14, name="finish",
    )


def swap_both(x, dp):
    pairs = [(2 * i + t, 2 * (i ^ 1) + (t ^ 1)) for i in range(dp) for t in range(2)]
    return lax.ppermute(x, ("dp", "tensor"), pairs)


def per_device(
    dp,
    page_tokens,
    patch_counts,
    token_boxes,
    text_weight,
    patch_weight,
    query_weight,
    query_bias,
    key_weight,
    value_weight,
    value_bias,
    out_weight,
    out_bias,
    line_table,
    width_table,
    height_table,
    norm1_gain,
    norm1_shift,
    inner_weight,
    inner_bias,
    outer_weight,
    outer_bias,
    norm2_gain,
    norm2_shift,
    cotangent,
):
    place = lax.axis_index("dp")
    half = lax.axis_index("tensor")
    core = place % 2
    bits = [(place // 2**i) % 2 for i in range(4)]
    where = jnp.stack([half] + bits).astype(jnp.int32)
    x = page_tokens.reshape(SEQ, D)
    cot = cotangent.reshape(SEQ, D)
    slab = D // dp if dp == 16 else None
    order = Order()

    z, m, o, u, r, wo_mine, o_far, ur_far, r_far = make_tables(
        order,
        where,
        jnp.concatenate([jnp.transpose(a) for a in (line_table, width_table, height_table)], axis=1),
        token_boxes.reshape(2, SEQ),
        out_weight,
    )
    wo_a = swap_tensor(wo_mine)
    row = lax.broadcasted_iota(jnp.int32, (8, 1), 0)
    bias = jnp.where(row == 0, query_bias[None, :], value_bias[None, :]).astype(F32)
    (q0, q1, q2, k, v), enc, enc_low, far = encode(
        order, patch_counts, x, text_weight, patch_weight, bias,
        query_weight, key_weight, value_weight,
    )
    q = (q0, q1, q2)
    q_far, k_far, v_far = far[0:3], far[3], far[4]

    vec = jnp.zeros((8, 1), F32)
    for i, a in enumerate(
        (out_bias, norm1_gain, norm1_shift, outer_bias, norm2_gain, norm2_shift)
    ):
        vec = jnp.where(row == i, a[None, :].astype(F32), vec)
    bi = jnp.broadcast_to(inner_bias[None, :].astype(F32), (8, FL))
    probs, mix, mix_low, mix_other = ([None] * 3 for _ in range(4))
    xhat, rstd, hlow, act, slope, outer, outer_other = ([None] * 3 for _ in range(7))

    def attention_of(c):
        p, a, low = attend(order, c, patch_counts, q[c], k, v, u, r, m, o, z)
        probs[c], mix[c], mix_low[c], mix_other[c] = p, a, low, swap_tensor(a)

    def feed_of(c):
        got = feed(
            order, c, where, mix[c], mix_other[c], enc[c], vec, out_weight, wo_a, wo_b,
            inner_weight, bi, outer_weight,
        )
        for keep, a in zip((xhat, rstd, hlow, act, slope, outer), got):
            keep[c] = a
        outer_other[c] = swap_tensor(got[5])

    attention_of(ORDER[0])
    wo_a = pass_on(order, wo_a)
    wo_b = swap_dp(wo_a, 1, dp)
    attention_of(ORDER[1])
    feed_of(ORDER[0])
    attention_of(ORDER[2])
    feed_of(ORDER[1])
    feed_of(ORDER[2])
    layer_out, inner_grad, outer_grad = None, None, None
    dres2, g2, g1, dhid, dhid_other, sums2 = ([None] * 3 for _ in range(6))
    for c in ORDER:
        got = feed_back(
            order, c, patch_counts, outer[c], outer_other[c], xhat[c], cot, vec, outer_weight,
            slope[c], inner_weight, layer_out,
        )
        layer_out = got[0]
        for keep, a in zip((dres2, g2, g1, dhid, sums2), got[1:]):
            keep[c] = a
        dhid_other[c] = swap_tensor(got[4])
        last = c == ORDER[2]
        inner_grad = chunk_grads(
            order, slab, where, hlow[c], g1[c], inner_grad, last, f"inner_grads_{c}"
        )
        outer_grad = chunk_grads(
            order, slab, where, g2[c], act[c], outer_grad, last, f"outer_grads_{c}"
        )
        if not last:
            inner_grad, outer_grad = inner_grad[0], outer_grad[0]
    scatter = functools.partial(Scatter, order, dp, where)
    x_first, z_first = (1, 2, 3), (2, 3, 1)
    inner_pair, outer_pair = swap_core(inner_grad, dp), swap_core(outer_grad, dp)
    inner = scatter(inner_pair, x_first, "inner", 0, D)
    inner_b = scatter(inner_pair, x_first, "inner_b", D, D)
    outer_a = scatter(outer_pair, x_first, "outer_a", 0, 512)
    outer_b = scatter(outer_pair, z_first, "outer_b", 512, 1024)
    carry = None
    dres1, g0, dq, sums1 = ([None] * 3 for _ in range(4))
    for c in ORDER:
        got = norm_one_back(
            order, c, dres2[c], dhid[c], dhid_other[c], xhat[c], rstd[c], vec, out_weight
        )
        dres1[c], g0[c], _, sums1[c] = got
        if c == ORDER[0]:
            inner.step()
            outer_b.step()
            inner_b.step()
        if c == ORDER[1]:
            outer_a.step()
            inner.step()
            outer_b.step()
        if c == ORDER[2]:
            inner_b.step()
            inner.step()
            outer_b.step()
        dq[c], *carry = attend_back(
            order, c, got[2], probs[c], q_far[c], k_far, v_far, ur_far, r_far, o_far, carry
        )
    dk, dv, dm, dz = carry
    outer_a.step()
    inner_b.step()
    if dp == 16:
        total_inner = total_of(order, inner, False, "inner_total")
        total_outer_b = total_of(order, outer_b, True, "outer_b_total")
    got = attention_grads(order, slab, where, enc_low, dq, dk, dv, g0, mix_low)
    half_way = len(got) // 2
    query_key = scatter(swap_core(got[:half_way], dp), x_first, "query_key", 0, D)
    value_out = scatter(swap_core(got[half_way:], dp), z_first, "value_out", 0, D)
    part, bias_sums = project_back(order, dq, dk, dv, query_weight, key_weight, value_weight)
    part_other = swap_tensor(part)
    tables = table_sums(order, dm, dz)
    taps = tap_sums(order, patch_counts, x, part, dres1)
    small = gather_small(order, taps, *sums1, *sums2, bias_sums, tables)
    outer_a.step()
    if dp == 16:
        total_inner_b = total_of(order, inner_b, False, "inner_b_total")
    query_key.step(small, "first")
    value_out.step()
    query_key.step(None, "more")
    value_out.step()
    if dp == 16:
        total_outer_a = total_of(order, outer_a, True, "outer_a_total")
    query_key.step(None, "more")
    value_out.step()
    input_grad = decode(order, patch_counts, text_weight, patch_weight, part, part_other, dres1)
    if dp == 16:
        inner_total = jnp.concatenate([total_inner, total_inner_b], axis=1)
        sum_outer = jnp.concatenate([total_outer_a, total_outer_b], axis=0)
        grad_q, grad_k, grad_v, grad_o, small = attention_totals(
            order, query_key, value_out, slab
        )
    else:
        grad_q, grad_k = jnp.split(query_key.total(), 2, axis=1)
        grad_v, grad_o = jnp.split(value_out.total(), 2, axis=1)
        grad_o = jnp.transpose(grad_o)
        inner_total = jnp.concatenate([inner.total(), inner_b.total()], axis=1)
        sum_outer = jnp.concatenate([outer_a.total(), outer_b.total()], axis=1)
        sum_outer = jnp.transpose(sum_outer)
        bit = 2
        while bit < dp:
            small = small + swap_dp(small, bit, dp)
            bit *= 2
    small = finish(
        order, jnp.reshape(place, (1,)).astype(jnp.int32), small, swap_dp(small, 1, dp),
        swap_tensor(small[0:24]), swap_both(small[0:24], dp), D // dp,
    )
    text, patch, out_b, gain1, shift1, outer_b, gain2, shift2 = small[:8]
    query_b, value_b, inner_b, line, width, height = small[8:]
    return (
        layer_out.reshape(1, SEQ, D),
        input_grad.reshape(1, SEQ, D),
        text,
        patch,
        grad_q,
        query_b,
        grad_k,
        grad_v,
        value_b,
        grad_o,
        out_b,
        line,
        width,
        height,
        gain1,
        shift1,
        inner_total,
        inner_b,
        sum_outer,
        outer_b,
        gain2,
        shift2,
    )


def solution(mesh):
    placed = (
        P("dp", None, None),
        P("dp"),
        P("dp", None, None),
        P(),
        P(),
        P(None, "tensor"),
        P("tensor"),
        P(None, "tensor"),
        P(None, "tensor"),
        P("tensor"),
        P("tensor", None),
        P(),
        P(None, "tensor"),
        P(None, "tensor"),
        P(None, "tensor"),
        P(),
        P(),
        P(None, "tensor"),
        P("tensor"),
        P("tensor", None),
        P(),
        P(),
        P(),
        P("dp", None, None),
    )
    return jax.shard_map(
        functools.partial(per_device, mesh.shape["dp"]),
        mesh=mesh,
        in_specs=placed,
        out_specs=(
            P("dp", None, None),
            P("dp", None, None),
            P(None, None, "dp"),
            P(None, "dp"),
            P("dp", "tensor"),
            P("tensor"),
            P("dp", "tensor"),
            P("dp", "tensor"),
            P("tensor"),
            P("tensor", "dp"),
            P("dp"),
            P(None, "tensor"),
            P(None, "tensor"),
            P(None, "tensor"),
            P("dp"),
            P("dp"),
            P("dp", "tensor"),
            P("tensor"),
            P("tensor", "dp"),
            P("dp"),
            P("dp"),
            P("dp"),
        ),
        check_vma=False,
    )
```

time: 1130 us -> 275 us (0.24)
  matrix products: 424 us -> 0 us
  waiting for transfers between devices: 403 us -> 65.2 us
  Pallas kernels: 0 us -> 145 us
  local copies, waits for them, and re-layouts: 114 us -> 13.7 us
  other arithmetic: 101 us -> 3.44 us
  blocking collectives: 61.5 us -> 0 us
  starting transfers between devices: 1.08 us -> 41.1 us
  between operations: 17.5 us -> 2.72 us
    dot_general x48 -> x0, matrix products: 424 us -> none  [the longest x12 220 us: accumulate(): lax.dot_general(grad_part, selector, (((1, 2), (0, 1)), ((), ())), precis...]
    psum x4 -> x0, waiting for transfers between devices: 260 us -> none  [the longest x1 67.6 us: per_device(): lax.psum(dense(mixture_flat, out_weight), 'tensor')]
    pallas_call x0 -> x54, Pallas kernels: none -> 145 us  [__call__(): pl.pallas_call(body, out_shape=tuple(out_shape) + (TOKEN,), in_specs=in_s...]
    reduce_scatter x6 -> x0, waiting for transfers between devices: 143 us -> none  [the longest x1 79.4 us: per_device(): lax.psum_scatter(grad_outer_weight, 'dp', scatter_dimension=1, tiled=True)]
    ppermute x0 -> x37, waiting for transfers between devices: none -> 65.2 us  [the longest x12 34 us: swap_tensor(): return lax.ppermute(x, 'tensor', [(0, 1), (1, 0)])]
    psum x1 -> x0, blocking collectives: 61.5 us -> none  [per_device(): lax.psum((grad_query_bias, grad_value_bias, grad_line, grad_width, grad_h...]
    add x30 -> x0, other arithmetic: 43.4 us -> none  [the longest x24 26.3 us: selector_rows(): match = (rows + offset)[:, :, None] == bin_ids]
    ppermute x0 -> x37, starting transfers between devices: none -> 41.1 us  [the longest x24 24.9 us: swap_dp(): return lax.ppermute(x, 'dp', [(i, i ^ bit) for i in range(dp)])]
  transfers between devices with their start and end apart: 12 -> 37, of which waited for: 6 -> 11; matrix products, arithmetic and copies ran while one was open for 27% -> 2% of each run, Pallas kernels for 0% -> 48%
where the time goes in v1:
time: 275 us; the launch traced here: 271 us
  Pallas kernels  145 us (53%)
  waiting for transfers between devices  65.2 us (24%)
  starting transfers between devices  41.1 us (15%)
  local copies, waits for them, and re-layouts  13.7 us (5%)
  other arithmetic  3.44 us (1%)
    pallas_call x54, Pallas kernels, __call__(): pl.pallas_call(body, out_shape=tuple(out_shape) + (TOKEN,), in_specs=in_s...  145 us
    ppermute x12, waiting for transfers between devices, swap_tensor(): return lax.ppermute(x, 'tensor', [(0, 1), (1, 0)])  34 us
    ppermute x24, waiting for transfers between devices, swap_dp(): return lax.ppermute(x, 'dp', [(i, i ^ bit) for i in range(dp)])  31.2 us
    ppermute x24, starting transfers between devices, swap_dp(): return lax.ppermute(x, 'dp', [(i, i ^ bit) for i in range(dp)])  24.9 us
    ppermute x12, starting transfers between devices, swap_tensor(): return lax.ppermute(x, 'tensor', [(0, 1), (1, 0)])  16.2 us
    unnamed x102, local copies, waits for them, and re-layouts  11.1 us
  transfers between devices with their start and end apart: 37, of which 11 were waited for; matrix products, arithmetic and copies ran while one was open for 2% of the time, Pallas kernels for 48%

profile of v1, /device:TPU:0, one launch (start us, length us, event | category | flops | bytes accessed | tf_op | source)
XLA Modules:
  0.0 271.4 jit_solution(728821535456358239)
XLA Ops:
  3.4 3.8 %bias_tables.1 = (f32[6,128,640]{2,1,0:T(8,128)S(1)}, bf16[128,3072]{1,0:T(8,128)(2,1)S(1)}, bf16[1024,768]{1,0:T(8,128)(2,1)S(1)}, bf16[720,128]{1,0:T(8,128)(2...) custom-call(s32[5]{0:T(128)S(1)} %stack.23.refs_0_, ...), custom_call_target="tpu_custom_call" | custom-call | flops 20000000000 | bytes 20000000 | tf_op jit(solution)/shard_map/bias_tables/pallas_call | solution.py:93
  7.3 3.0 %collective-permute-start.1 = (f32[192,768]{1,0:T(8,128)S(1)}, f32[192,768]{1,0:T(8,128)S(1)}, u32[]{:S(2)}, u32[]{:S(2)}) collective-permute-start(f32[192,768]{1,0:T(8,128)S(1)} %get-tuple-element.263), channel_id=1, source_target_pairs={{0,1},{1,0},{2,3},{3,2},{4,5},{5,4},{6,7},{7,6},{8,9},{9,8},{10,11... | collective-permute-start | bytes 1769480 | tf_op jit(solution)/shard_map/ppermute | solution.py:1139
  11.1 8.3 %encode_project.1 = (bf16[256,384]{1,0:T(8,128)(2,1)S(1)}, bf16[256,384]{1,0:T(8,128)(2,1)S(1)}, bf16[208,384]{1,0:T(8,128)(2,1)S(1)}, bf16[768,384]{1,0:T(8,128...) custom-call(s32[1]{0:T(128)S(6)} %copy.81.refs_0_, ...), custom_call_target="tpu_custom_call" | custom-call | flops 8000000000 | bytes 8000000 | tf_op jit(solution)/shard_map/encode_project/pallas_call | solution.py:93
  19.5 7.6 %attend_2.1 = (bf16[6,208,768]{2,1,0:T(8,128)(2,1)S(1)}, f32[208,384]{1,0:T(8,128)S(1)}, bf16[208,384]{1,0:T(8,128)(2,1)S(1)}, f32[8,128]{1,0:T(8,128)S(1)}) custom-call(s32[1]{0:T(128)S(6)} %copy.81.refs_0_, bf16[208,384]{1,0:T(8,128)(2,1)S(1)} %get-tuple-element.259.refs_1_, bf16[768,384]{1,0:T(8,128)(2,1)S(1)} %get-tuple-element.252.refs_2_, ...), custom_call_target="tpu_custom_call" | custom-call | flops 1000000 | bytes 1000 | tf_op jit(solution)/shard_map/attend_2/pallas_call | solution.py:93
  27.8 9.2 %attend_0.1 = (bf16[6,256,768]{2,1,0:T(8,128)(2,1)S(1)}, f32[256,384]{1,0:T(8,128)S(1)}, bf16[256,384]{1,0:T(8,128)(2,1)S(1)}, f32[8,128]{1,0:T(8,128)S(1)}) custom-call(s32[1]{0:T(128)S(6)} %copy.81.refs_0_, bf16[256,384]{1,0:T(8,128)(2,1)S(1)} %get-tuple-element.266.refs_1_, bf16[768,384]{1,0:T(8,128)(2,1)S(1)} %get-tuple-element.252.refs_2_, ...), custom_call_target="tpu_custom_call" | custom-call | flops 1000000 | bytes 1000 | tf_op jit(solution)/shard_map/attend_0/pallas_call | solution.py:93
  37.5 3.1 %feed_2.1 = (f32[208,768]{1,0:T(8,128)S(1)}, f32[208,128]{1,0:T(8,128)S(1)}, bf16[208,768]{1,0:T(8,128)(2,1)S(1)}, bf16[208,1536]{1,0:T(8,128)(2,1)S(1)}, f32[20...) custom-call(s32[5]{0:T(128)S(1)} %stack.23.refs_0_, f32[208,384]{1,0:T(8,128)S(1)} %get-tuple-element.261.refs_1_, ...), custom_call_target="tpu_custom_call" | custom-call | flops 1000000 | bytes 1000 | tf_op jit(solution)/shard_map/feed_2/pallas_call | solution.py:93
  42.7 9.1 %attend_1.1 = (bf16[6,256,768]{2,1,0:T(8,128)(2,1)S(1)}, f32[256,384]{1,0:T(8,128)S(1)}, bf16[256,384]{1,0:T(8,128)(2,1)S(1)}, f32[8,128]{1,0:T(8,128)S(1)}) custom-call(s32[1]{0:T(128)S(6)} %copy.81.refs_0_, bf16[256,384]{1,0:T(8,128)(2,1)S(1)} %get-tuple-element.251.refs_1_, bf16[768,384]{1,0:T(8,128)(2,1)S(1)} %get-tuple-element.252.refs_2_, ...), custom_call_target="tpu_custom_call" | custom-call | flops 1000000 | bytes 1000 | tf_op jit(solution)/shard_map/attend_1/pallas_call | solution.py:93
  53.5 12.8 %collective-permute-done.4.refs_2_ = f32[256,384]{1,0:T(8,128)S(1)} collective-permute-done((f32[256,384]{1,0:T(8,128)S(1)}, f32[256,384]{1,0:T(8,128)S(1)}, u32[]{:S(2)}, u32[]{:S(2)}) %collective-permute-start.4) | collective-permute-done | bytes 393248 | tf_op jit(solution)/shard_map/ppermute | solution.py:1139
  66.3 3.5 %feed_0.1 = (f32[256,768]{1,0:T(8,128)S(1)}, f32[256,128]{1,0:T(8,128)S(1)}, bf16[256,768]{1,0:T(8,128)(2,1)S(1)}, bf16[256,1536]{1,0:T(8,128)(2,1)S(1)}, f32[25...) custom-call(s32[5]{0:T(128)S(1)} %stack.23.refs_0_, f32[256,384]{1,0:T(8,128)S(1)} %get-tuple-element.272.refs_1_, ...), custom_call_target="tpu_custom_call" | custom-call | flops 1000000 | bytes 1000 | tf_op jit(solution)/shard_map/feed_0/pallas_call | solution.py:93
  71.6 3.1 %collective-permute-done.3.refs_2_ = f32[256,384]{1,0:T(8,128)S(1)} collective-permute-done((f32[256,384]{1,0:T(8,128)S(1)}, f32[256,384]{1,0:T(8,128)S(1)}, u32[]{:S(2)}, u32[]{:S(2)}) %collective-permute-start.3) | collective-permute-done | bytes 393248 | tf_op jit(solution)/shard_map/ppermute | solution.py:1139
  74.7 3.3 %feed_1.1 = (f32[256,768]{1,0:T(8,128)S(1)}, f32[256,128]{1,0:T(8,128)S(1)}, bf16[256,768]{1,0:T(8,128)(2,1)S(1)}, bf16[256,1536]{1,0:T(8,128)(2,1)S(1)}, f32[25...) custom-call(s32[5]{0:T(128)S(1)} %stack.23.refs_0_, f32[256,384]{1,0:T(8,128)S(1)} %get-tuple-element.270.refs_1_, ...), custom_call_target="tpu_custom_call" | custom-call | flops 1000000 | bytes 1000 | tf_op jit(solution)/shard_map/feed_1/pallas_call | solution.py:93
  79.8 3.3 %feed_back_2.1 = (bf16[708,768]{1,0:T(8,128)(2,1)}, f32[208,768]{1,0:T(8,128)S(1)}, bf16[208,768]{1,0:T(8,128)(2,1)S(1)}, bf16[208,1536]{1,0:T(8,128)(2,1)S(1)},...) custom-call(s32[1]{0:T(128)S(6)} %copy.81.refs_0_, f32[208,768]{1,0:T(8,128)S(1)} %get-tuple-element.282.refs_1_, ...), custom_call_target="tpu_custom_call" | custom-call | flops 15000000512 | bytes 15000000 | tf_op jit(solution)/shard_map/feed_back_2/pallas_call | solution.py:93
  87.7 3.9 %collective-permute-done.6.refs_2_ = f32[256,768]{1,0:T(8,128)S(1)} collective-permute-done((f32[256,768]{1,0:T(8,128)S(1)}, f32[256,768]{1,0:T(8,128)S(1)}, u32[]{:S(2)}, u32[]{:S(2)}) %collective-permute-start.6) | collective-permute-done | bytes 786464 | tf_op jit(solution)/shard_map/ppermute | solution.py:1139
  98.7 9.7 %collective-permute-done.5.refs_2_ = f32[256,768]{1,0:T(8,128)S(1)} collective-permute-done((f32[256,768]{1,0:T(8,128)S(1)}, f32[256,768]{1,0:T(8,128)S(1)}, u32[]{:S(2)}, u32[]{:S(2)}) %collective-permute-start.5) | collective-permute-done | bytes 786464 | tf_op jit(solution)/shard_map/ppermute | solution.py:1139
  110.8 3.9 %inner_grads_1.1 = (f32[384,1536]{1,0:T(8,128)S(1)}, f32[384,1536]{1,0:T(8,128)}, f32[8,128]{1,0:T(8,128)S(1)}) custom-call(s32[5]{0:T(128)S(1)} %stack.23.refs_0_, bf16[256,768]{1,0:T(8,128)(2,1)S(1)} %get-tuple-element.314.refs_1_, bf16[256,1536]{1,0:T(8,128)(2,1)S(1)} %get-tuple-element.315.refs_2_, f32[768,1536]{1,0:T(8,128)S(1)} %get-tuple-element.316.refs_3_, ...), custom_call_target="tpu_custom_call" | custom-call | flops 1000000 | bytes 1000 | tf_op jit(solution)/shard_map/inner_grads_1/pallas_call | solution.py:93
  132.6 9.2 %attend_back_2.1 = (f32[208,384]{1,0:T(8,128)S(1)}, f32[768,384]{1,0:T(8,128)S(1)}, f32[768,384]{1,0:T(8,128)S(1)}, f32[128,3072]{1,0:T(8,128)S(1)}, f32[6,128,640]{2,1,0:T(8,128)S(1)}, /*index=5*/f32[8,128]{1,0:T(8,128)S(1)}) custom-call(bf16[208,384]{1,0:T(8,128)(2,1)S(1)} %get-tuple-element.320.refs_0_, ...), custom_call_target="tpu_custom_call" | custom-call | flops 1000000 | bytes 1000 | tf_op jit(solution)/shard_map/attend_back_2/pallas_call | solution.py:93
  151.0 10.8 %attend_back_0.1 = (f32[256,384]{1,0:T(8,128)S(1)}, f32[768,384]{1,0:T(8,128)S(1)}, f32[768,384]{1,0:T(8,128)S(1)}, f32[128,3072]{1,0:T(8,128)S(1)}, f32[6,128,640]{2,1,0:T(8,128)S(1)}, /*index=5*/f32[8,128]{1,0:T(8,128)S(1)}) custom-call(bf16[256,384]{1,0:T(8,128)(2,1)S(1)} %get-tuple-element., ...), custom_call_target="tpu_custom_call", output_to_operand_aliasing={{1}: (8, {}), {2}: (9, {}), {3}: (10, {}), {4}: (11, {})} | custom-call | flops 1000000 | bytes 1000 | tf_op jit(solution)/shard_map/attend_back_0/pallas_call | solution.py:93
  167.1 10.8 %attend_back_1.1 = (f32[256,384]{1,0:T(8,128)S(1)}, f32[768,384]{1,0:T(8,128)S(1)}, f32[768,384]{1,0:T(8,128)S(1)}, f32[128,3072]{1,0:T(8,128)S(1)}, f32[6,128,640]{2,1,0:T(8,128)S(1)}, /*index=5*/f32[8,128]{1,0:T(8,128)S(1)}) custom-call(bf16[256,384]{1,0:T(8,128)(2,1)S(1)} %get-tuple-element., ...), custom_call_target="tpu_custom_call", output_to_operand_aliasing={{1}: (8, {}), {2}: (9, {}), {3}: (10, {}), {4}: (11, {})} | custom-call | flops 1000000 | bytes 1000 | tf_op jit(solution)/shard_map/attend_back_1/pallas_call | solution.py:93
  180.0 4.4 %attention_grads.1 = (f32[384,768]{1,0:T(8,128)S(1)}, f32[384,768]{1,0:T(8,128)S(1)}, f32[384,768]{1,0:T(8,128)S(1)}, f32[384,768]{1,0:T(8,128)S(1)}, f32[8,128]{1,0:T(8,128)S(1)}) custom-call(s32[5]{0:T(128)S(1)} %stack.23.refs_0_, bf16[256,768]{1,0:T(8,128)(2,1)S(1)} %get-tuple-element.378.refs_1_, bf16[256,768]{1,0:T(8,128)(2,1)S(1)} %get-tuple-element.379.refs_2_, ...), custom_call_target="tpu_custom_call" | custom-call | flops 1000000 | bytes 1000 | tf_op jit(solution)/shard_map/attention_grads/pallas_call | solution.py:93
  192.3 3.9 %table_sums.1 = (f32[8,256]{1,0:T(8,128)S(1)}, f32[8,128]{1,0:T(8,128)S(1)}) custom-call(f32[128,3072]{1,0:T(8,128)S(1)} %get-tuple-element.407.refs_0_, f32[6,128,640]{2,1,0:T(8,128)S(1)} %get-tuple-element.408.refs_1_, f32[8,128]{1,0:T(8,128)S(1)} %get-tuple-element.409.refs_2_), custom_call_target="tpu_custom_call" | custom-call | flops 1000000 | bytes 1000 | tf_op jit(solution)/shard_map/table_sums/pallas_call | solution.py:93
  196.2 3.4 %tap_sums.1 = (f32[24,768]{1,0:T(8,128)S(1)}, f32[8,128]{1,0:T(8,128)S(1)}) custom-call(s32[1]{0:T(128)S(6)} %copy.81.refs_0_, bf16[708,768]{1,0:T(8,128)(2,1)S(1)} %bitcast.18, f32[720,768]{1,0:T(8,128)S(1)} %get-tuple-element.401.refs_2_.refs_3_, f32[256,768]{1,0:T(8,128)S(1)} %get-tuple-element.402.refs_3_.refs_5_, ...), custom_call_target="tpu_custom_call" | custom-call | flops 1000000 | bytes 1000 | tf_op jit(solution)/shard_map/tap_sums/pallas_call | solution.py:93
  205.8 13.3 %collective-permute-done.28.refs_2_ = f32[232,768]{1,0:T(8,128)S(1)} collective-permute-done((f32[232,768]{1,0:T(8,128)S(1)}, f32[232,768]{1,0:T(8,128)S(1)}, u32[]{:S(2)}, u32[]{:S(2)}) %collective-permute-start.28) | collective-permute-done | bytes 712736 | tf_op jit(solution)/shard_map/ppermute | solution.py:1143
  225.2 16.0 %collective-permute-done.31.refs_1_ = f32[48,512]{1,0:T(8,128)S(1)} collective-permute-done((f32[48,512]{1,0:T(8,128)S(1)}, f32[48,512]{1,0:T(8,128)S(1)}, u32[]{:S(2)}, u32[]{:S(2)}) %collective-permute-start.31) | collective-permute-done | bytes 98336 | tf_op jit(solution)/shard_map/ppermute | solution.py:1143
  254.9 6.5 %decode.1 = (bf16[708,768]{1,0:T(8,128)(2,1)}, f32[8,128]{1,0:T(8,128)S(1)}) custom-call(s32[1]{0:T(128)S(6)} %copy.81.refs_0_, bf16[3,3,768]{2,1,0:T(4,128)(2,1)S(1)} %copy-done.36, bf16[9,768]{1,0:T(8,128)(2,1)S(1)} %copy-done.34, f32[720,768]{1,0:T(8,128)S(1)} %get-tuple-element.401.refs_2_.refs_3_, f32[720,768]{1,0:T(8,128)} %collective-permute-done.22.refs_4_, ...), custom_call_target="tpu_custom_call" | custom-call | flops 1000000 | bytes 1000 | tf_op jit(solution)/shard_map/decode/pallas_call | solution.py:93
  (226 shorter events, 102.7 us)
Async XLA Ops:
  7.3 19.9 %collective-permute-start.1 = (f32[192,768]{1,0:T(8,128)S(1)}, f32[192,768]{1,0:T(8,128)S(1)}, u32[]{:S(2)}, u32[]{:S(2)}) collective-permute-start(f32[192,768]{1,0:T(8,128)S(1)} %get-tuple-element.263), channel_id=1, source_target_pairs={{0,1},{1,0},{2,3},{3,2},{4,5},{5,4},{6,7},{7,6},{8,9},{9,8},{10,11... | collective-permute-start | bytes 1769480 | tf_op jit(solution)/shard_map/ppermute | solution.py:1139
  40.6 39.2 %collective-permute-start.7 = (f32[208,768]{1,0:T(8,128)S(1)}, f32[208,768]{1,0:T(8,128)S(1)}, u32[]{:S(2)}, u32[]{:S(2)}) collective-permute-start(f32[208,768]{1,0:T(8,128)S(1)} %get-tuple-element.282.refs_1_), channel_id=1, source_target_pairs={{0,1},{1,0},{2,3},{3,2},{4,5},{5,4},{6,7},{7,6},{8,9},{9,8},{10,11... | collective-permute-start | bytes 1916936 | tf_op jit(solution)/shard_map/ppermute | solution.py:1139
  42.3 23.9 %collective-permute-start.4 = (f32[256,384]{1,0:T(8,128)S(1)}, f32[256,384]{1,0:T(8,128)S(1)}, u32[]{:S(2)}, u32[]{:S(2)}) collective-permute-start(f32[256,384]{1,0:T(8,128)S(1)} %get-tuple-element.272.refs_1_), channel_id=1, source_target_pairs={{0,1},{1,0},{2,3},{3,2},{4,5},{5,4},{6,7},{7,6},{8,9},{9,8},{10,11... | collective-permute-start | bytes 1179656 | tf_op jit(solution)/shard_map/ppermute | solution.py:1139
  51.8 23.0 %collective-permute-start.3 = (f32[256,384]{1,0:T(8,128)S(1)}, f32[256,384]{1,0:T(8,128)S(1)}, u32[]{:S(2)}, u32[]{:S(2)}) collective-permute-start(f32[256,384]{1,0:T(8,128)S(1)} %get-tuple-element.270.refs_1_), channel_id=1, source_target_pairs={{0,1},{1,0},{2,3},{3,2},{4,5},{5,4},{6,7},{7,6},{8,9},{9,8},{10,11... | collective-permute-start | bytes 1179656 | tf_op jit(solution)/shard_map/ppermute | solution.py:1139
  69.8 21.8 %collective-permute-start.6 = (f32[256,768]{1,0:T(8,128)S(1)}, f32[256,768]{1,0:T(8,128)S(1)}, u32[]{:S(2)}, u32[]{:S(2)}) collective-permute-start(f32[256,768]{1,0:T(8,128)S(1)} %get-tuple-element.279.refs_1_), channel_id=1, source_target_pairs={{0,1},{1,0},{2,3},{3,2},{4,5},{5,4},{6,7},{7,6},{8,9},{9,8},{10,11... | collective-permute-start | bytes 2359304 | tf_op jit(solution)/shard_map/ppermute | solution.py:1139
  78.0 30.4 %collective-permute-start.5 = (f32[256,768]{1,0:T(8,128)S(1)}, f32[256,768]{1,0:T(8,128)S(1)}, u32[]{:S(2)}, u32[]{:S(2)}) collective-permute-start(f32[256,768]{1,0:T(8,128)S(1)} %get-tuple-element.276.refs_1_), channel_id=1, source_target_pairs={{0,1},{1,0},{2,3},{3,2},{4,5},{5,4},{6,7},{7,6},{8,9},{9,8},{10,11... | collective-permute-start | bytes 2359304 | tf_op jit(solution)/shard_map/ppermute | solution.py:1139
  83.1 39.0 %collective-permute-start.9 = (f32[208,768]{1,0:T(8,128)}, f32[208,768]{1,0:T(8,128)S(1)}, u32[]{:S(2)}, u32[]{:S(2)}) collective-permute-start(f32[208,768]{1,0:T(8,128)} %get-tuple-element.309.refs_1_), channel_id=1, source_target_pairs={{0,1},{1,0},{2,3},{3,2},{4,5},{5,4},{6,7},{7,6},{8,9},{9,8},{10,11... | collective-permute-start | bytes 1916936 | tf_op jit(solution)/shard_map/ppermute | solution.py:1139
  117.7 24.1 %collective-permute-start.8 = (f32[256,768]{1,0:T(8,128)S(1)}, f32[256,768]{1,0:T(8,128)S(1)}, u32[]{:S(2)}, u32[]{:S(2)}) collective-permute-start(f32[256,768]{1,0:T(8,128)S(1)} %get-tuple-element.306.refs_1_), channel_id=1, source_target_pairs={{0,1},{1,0},{2,3},{3,2},{4,5},{5,4},{6,7},{7,6},{8,9},{9,8},{10,11... | collective-permute-start | bytes 2359304 | tf_op jit(solution)/shard_map/ppermute | solution.py:1139
  126.2 18.8 %collective-permute-start.12 = (f32[192,1024]{1,0:T(8,128)S(1)}, f32[192,1024]{1,0:T(8,128)S(1)}, u32[]{:S(2)}, u32[]{:S(2)}) collective-permute-start(f32[192,1024]{1,0:T(8,128)S(1)} %get-tuple-element.345), channel_id=1, source_target_pairs={{0,8},{2,10},{4,12},{6,14},{8,0},{10,2},{12,4},{14,6},{16,24},{18,... | collective-permute-start | bytes 2359304 | tf_op jit(solution)/shard_map/ppermute | solution.py:1143
  128.0 16.3 %collective-permute-start.13 = (f32[192,768]{1,0:T(8,128)S(1)}, f32[192,768]{1,0:T(8,128)S(1)}, u32[]{:S(2)}, u32[]{:S(2)}) collective-permute-start(f32[192,768]{1,0:T(8,128)S(1)} %get-tuple-element.347), channel_id=1, source_target_pairs={{0,4},{2,6},{4,0},{6,2},{8,12},{10,14},{12,8},{14,10},{16,20},{18,... | collective-permute-start | bytes 1769480 | tf_op jit(solution)/shard_map/ppermute | solution.py:1143
  129.5 32.2 %collective-permute-start.14 = (f32[256,768]{1,0:T(8,128)S(1)}, f32[256,768]{1,0:T(8,128)S(1)}, u32[]{:S(2)}, u32[]{:S(2)}) collective-permute-start(f32[256,768]{1,0:T(8,128)S(1)} %get-tuple-element.354.refs_1_), channel_id=1, source_target_pairs={{0,1},{1,0},{2,3},{3,2},{4,5},{5,4},{6,7},{7,6},{8,9},{9,8},{10,11... | collective-permute-start | bytes 2359304 | tf_op jit(solution)/shard_map/ppermute | solution.py:1139
  132.0 30.8 %collective-permute-start.17 = (f32[192,768]{1,0:T(8,128)S(1)}, f32[192,768]{1,0:T(8,128)S(1)}, u32[]{:S(2)}, u32[]{:S(2)}) collective-permute-start(f32[192,768]{1,0:T(8,128)S(1)} %get-tuple-element.369), channel_id=1, source_target_pairs={{0,4},{2,6},{4,0},{6,2},{8,12},{10,14},{12,8},{14,10},{16,20},{18,... | collective-permute-start | bytes 1769480 | tf_op jit(solution)/shard_map/ppermute | solution.py:1143
  145.9 19.5 %collective-permute-start.15 = (f32[96,1024]{1,0:T(8,128)S(1)}, f32[96,1024]{1,0:T(8,128)S(1)}, u32[]{:S(2)}, u32[]{:S(2)}) collective-permute-start(f32[96,1024]{1,0:T(8,128)S(1)} %get-tuple-element.365), channel_id=1, source_target_pairs={{0,16},{2,18},{4,20},{6,22},{8,24},{10,26},{12,28},{14,30},{16,0},... | collective-permute-start | bytes 1179656 | tf_op jit(solution)/shard_map/ppermute | solution.py:1143
  148.0 16.7 %collective-permute-start.16 = (f32[96,768]{1,0:T(8,128)S(1)}, f32[96,768]{1,0:T(8,128)S(1)}, u32[]{:S(2)}, u32[]{:S(2)}) collective-permute-start(f32[96,768]{1,0:T(8,128)S(1)} %get-tuple-element.367), channel_id=1, source_target_pairs={{0,8},{2,10},{4,12},{6,14},{8,0},{10,2},{12,4},{14,6},{16,24},{18,... | collective-permute-start | bytes 884744 | tf_op jit(solution)/shard_map/ppermute | solution.py:1143
  148.9 29.1 %collective-permute-start.21 = (f32[192,512]{1,0:T(8,128)S(1)}, f32[192,512]{1,0:T(8,128)S(1)}, u32[]{:S(2)}, u32[]{:S(2)}) collective-permute-start(f32[192,512]{1,0:T(8,128)S(1)} %get-tuple-element.394), channel_id=1, source_target_pairs={{0,4},{2,6},{4,0},{6,2},{8,12},{10,14},{12,8},{14,10},{16,20},{18,... | collective-permute-start | bytes 1179656 | tf_op jit(solution)/shard_map/ppermute | solution.py:1143
  184.4 17.0 %collective-permute-start.24 = (f32[384,768]{1,0:T(8,128)S(1)}, f32[384,768]{1,0:T(8,128)S(1)}, u32[]{:S(2)}, u32[]{:S(2)}) collective-permute-start(f32[384,768]{1,0:T(8,128)S(1)} %get-tuple-element.423), channel_id=1, source_target_pairs={{0,2},{2,0},{4,6},{6,4},{8,10},{10,8},{12,14},{14,12},{16,18},{18,... | collective-permute-start | bytes 3538952 | tf_op jit(solution)/shard_map/ppermute | solution.py:1143
  184.5 19.3 %collective-permute-start.23 = (f32[384,768]{1,0:T(8,128)S(1)}, f32[384,768]{1,0:T(8,128)S(1)}, u32[]{:S(2)}, u32[]{:S(2)}) collective-permute-start(f32[384,768]{1,0:T(8,128)S(1)} %get-tuple-element.406), channel_id=1, source_target_pairs={{0,2},{2,0},{4,6},{6,4},{8,10},{10,8},{12,14},{14,12},{16,18},{18,... | collective-permute-start | bytes 3538952 | tf_op jit(solution)/shard_map/ppermute | solution.py:1143
  187.7 64.3 %collective-permute-start.22 = (f32[720,768]{1,0:T(8,128)S(1)}, f32[720,768]{1,0:T(8,128)}, u32[]{:S(2)}, u32[]{:S(2)}) collective-permute-start(f32[720,768]{1,0:T(8,128)S(1)} %get-tuple-element.401.refs_2_.refs_3_), channel_id=1, source_target_pairs={{0,1},{1,0},{2,3},{3,2},{4,5},{5,4},{6,7},{7,6},{8,9},{9,8},{10,11... | collective-permute-start | bytes 6635528 | tf_op jit(solution)/shard_map/ppermute | solution.py:1139
  202.7 16.4 %collective-permute-start.28 = (f32[232,768]{1,0:T(8,128)S(1)}, f32[232,768]{1,0:T(8,128)S(1)}, u32[]{:S(2)}, u32[]{:S(2)}) collective-permute-start(f32[232,768]{1,0:T(8,128)S(1)} %get-tuple-element.435), channel_id=1, source_target_pairs={{0,4},{2,6},{4,0},{6,2},{8,12},{10,14},{12,8},{14,10},{16,20},{18,... | collective-permute-start | bytes 2138120 | tf_op jit(solution)/shard_map/ppermute | solution.py:1143
  204.6 16.3 %collective-permute-start.27 = (f32[192,768]{1,0:T(8,128)S(1)}, f32[192,768]{1,0:T(8,128)S(1)}, u32[]{:S(2)}, u32[]{:S(2)}) collective-permute-start(f32[192,768]{1,0:T(8,128)S(1)} %get-tuple-element.433), channel_id=1, source_target_pairs={{0,8},{2,10},{4,12},{6,14},{8,0},{10,2},{12,4},{14,6},{16,24},{18,... | collective-permute-start | bytes 1769480 | tf_op jit(solution)/shard_map/ppermute | solution.py:1143
  219.7 21.6 %collective-permute-start.30 = (f32[136,768]{1,0:T(8,128)S(1)}, f32[136,768]{1,0:T(8,128)S(1)}, u32[]{:S(2)}, u32[]{:S(2)}) collective-permute-start(f32[136,768]{1,0:T(8,128)S(1)} %get-tuple-element.441), channel_id=1, source_target_pairs={{0,8},{2,10},{4,12},{6,14},{8,0},{10,2},{12,4},{14,6},{16,24},{18,... | collective-permute-start | bytes 1253384 | tf_op jit(solution)/shard_map/ppermute | solution.py:1143
  222.3 22.6 %collective-permute-start.29 = (f32[96,768]{1,0:T(8,128)}, f32[96,768]{1,0:T(8,128)}, u32[]{:S(2)}, u32[]{:S(2)}) collective-permute-start(f32[96,768]{1,0:T(8,128)} %get-tuple-element.439), channel_id=1, source_target_pairs={{0,16},{2,18},{4,20},{6,22},{8,24},{10,26},{12,28},{14,30},{16,0},... | collective-permute-start | bytes 884744 | tf_op jit(solution)/shard_map/ppermute | solution.py:1143
  223.6 17.7 %collective-permute-start.31 = (f32[48,512]{1,0:T(8,128)S(1)}, f32[48,512]{1,0:T(8,128)S(1)}, u32[]{:S(2)}, u32[]{:S(2)}) collective-permute-start(f32[48,512]{1,0:T(8,128)S(1)} %get-tuple-element.443), channel_id=1, source_target_pairs={{0,16},{2,18},{4,20},{6,22},{8,24},{10,26},{12,28},{14,30},{16,0},... | collective-permute-start | bytes 294920 | tf_op jit(solution)/shard_map/ppermute | solution.py:1143
  244.1 17.4 %collective-permute-start.32 = (f32[88,768]{1,0:T(8,128)}, f32[88,768]{1,0:T(8,128)}, u32[]{:S(2)}, u32[]{:S(2)}) collective-permute-start(f32[88,768]{1,0:T(8,128)} %get-tuple-element.450), channel_id=1, source_target_pairs={{0,16},{2,18},{4,20},{6,22},{8,24},{10,26},{12,28},{14,30},{16,0},... | collective-permute-start | bytes 811016 | tf_op jit(solution)/shard_map/ppermute | solution.py:1143
  (62 other events, 526.0 us)

commit v2 on v1

--- a/solution.py
+++ b/solution.py
@@ -68,63 +68,52 @@
         self.token = None
 
     def __call__(
-        self, kernel, operands, in_specs, out_shape, out_specs, mib=10, us=1, after=(), **more
+        self, kernel, operands, in_specs, out_shape, out_specs, mib=10, us=1, out=(), into=(),
+        scratch_shapes=(), **more,
     ):
         operands, in_specs = list(operands), list(in_specs)
-        count = len(operands)
-        operands += list(after)
-        in_specs += [anywhere()] * len(after)
-        if self.token is not None:
+        count, outs, moved = len(operands), len(out_shape), len(out) + len(into)
+        operands += [*out, *into]
+        in_specs += [vmem()] * len(out) + [hbm()] * len(into)
+        has_token = self.token is not None
+        grid = "grid" in more
+        token_spec = pl.BlockSpec(TOKEN.shape, lambda *i: (0, 0)) if grid else vmem()
+        if has_token:
             operands.append(self.token)
-            grid = "grid" in more
-            in_specs.append(pl.BlockSpec(TOKEN.shape, lambda *i: (0, 0)) if grid else vmem())
-        has_token = self.token is not None
-        outs = len(out_shape)
+            in_specs.append(token_spec)
+        shapes = [sds(a.shape, a.dtype) for a in (*out, *into)]
+        specs = [hbm()] * len(out) + [vmem()] * len(into)
+        scratch_shapes = list(scratch_shapes)
+        if moved:
+            scratch_shapes.append(pltpu.SemaphoreType.DMA((moved,)))
 
         def body(*refs):
             rest = list(refs)
-            del rest[count : count + len(after) + has_token]
+            sources = rest[count : count + moved]
+            del rest[count : count + moved + has_token]
             at = count + outs
-            rest[at][...] = jnp.zeros(TOKEN.shape, F32)
-            del rest[at]
+            targets = rest[at : at + moved]
+            rest[at + moved][...] = jnp.zeros(TOKEN.shape, F32)
+            del rest[at : at + moved + 1]
+            copies = start_all(zip(sources, targets), rest.pop()) if moved else []
             kernel(*rest)
-
-        token_spec = pl.BlockSpec(TOKEN.shape, lambda *i: (0, 0)) if "grid" in more else vmem()
+            for copy in copies:
+                copy.wait()
+
         got = pl.pallas_call(
             body,
-            out_shape=tuple(out_shape) + (TOKEN,),
+            out_shape=tuple(out_shape) + tuple(shapes) + (TOKEN,),
             in_specs=in_specs,
-            out_specs=tuple(out_specs) + (token_spec,),
+            out_specs=tuple(out_specs) + tuple(specs) + (token_spec,),
+            scratch_shapes=scratch_shapes,
             compiler_params=params(mib),
             cost_estimate=cost(us),
             **more,
         )(*operands)
         self.token = got[-1]
+        if moved:
+            return got[:outs], got[outs:-1]
         return got[:-1]
-
-
-def dot(a, b):
-    return lax.dot_general(a, b, (((1,), (0,)), ((), ())), preferred_element_type=F32)
-
-
-def dot_nt(a, b):
-    return lax.dot_general(a, b, (((1,), (1,)), ((), ())), preferred_element_type=F32)
-
-
-def dot_tn(a, b):
-    return lax.dot_general(a, b, (((0,), (0,)), ((), ())), preferred_element_type=F32)
-
-
-def cost(us):
-    return pl.CostEstimate(flops=int(us * 1.0e6), bytes_accessed=int(us * 1.0e3), transcendentals=0)
-
-
-def iota(shape, dim):
-    return lax.broadcasted_iota(jnp.int32, shape, dim)
-
-
-def first_lanes():
-    return iota((1, PAIR), 1) < 64
 
 
 def start_all(pairs, sems, first=0):
@@ -136,10 +125,34 @@
     return copies
 
 
+def dot(a, b):
+    return lax.dot_general(a, b, (((1,), (0,)), ((), ())), preferred_element_type=F32)
+
+
+def dot_nt(a, b):
+    return lax.dot_general(a, b, (((1,), (1,)), ((), ())), preferred_element_type=F32)
+
+
+def dot_tn(a, b):
+    return lax.dot_general(a, b, (((0,), (0,)), ((), ())), preferred_element_type=F32)
+
+
+def cost(us):
+    return pl.CostEstimate(flops=int(us * 1.0e6), bytes_accessed=int(us * 1.0e3), transcendentals=0)
+
+
+def iota(shape, dim):
+    return lax.broadcasted_iota(jnp.int32, shape, dim)
+
+
+def first_lanes():
+    return iota((1, PAIR), 1) < 64
+
+
 def tables_kernel(
     where_ref, tab_ref, boxes_hbm, wo_hbm,
-    z_ref, m_ref, o_ref, u_ref, r_ref, mine_ref, o_far, ur_far, r_far,
-    box_scr, boxes_ref, wo_ref, ur_ref, sems,
+    z_ref, m_ref, o_ref, u_ref, r_ref, mine_ref, ur_ref,
+    box_scr, boxes_ref, wo_ref, sems,
 ):
     half = DL // 2
     rows = pl.ds(pl.multiple_of(where_ref[1] * half, half), half)
@@ -197,8 +210,6 @@
     inner = lane & 63
     u_ref[...] = (upper == inner).astype(F32).astype(BF16)
     ur_ref[...] = (63 - upper == inner).astype(F32).astype(BF16)
-    for copy in start_all(((o_ref, o_far), (ur_ref, ur_far), (r_ref, r_far)), sems):
-        copy.wait()
 
 
 def make_tables(order, where, tab, boxes, wo):
@@ -213,18 +224,15 @@
             sds((ROWS, PAIR), BF16),
             sds((2, ROWS, PAIR), jnp.int32),
             sds((DL // 2, D), F32),
-            sds((1024, KEYS), BF16),
             sds((ROWS, PAIR), BF16),
-            sds((2, ROWS, PAIR), jnp.int32),
         ),
-        [vmem()] * 6 + [hbm()] * 3,
+        [vmem()] * 7,
         us=20000,
         scratch_shapes=[
             pltpu.VMEM((8, KEYS), jnp.int32),
             pltpu.VMEM(boxes.shape, jnp.int32),
             pltpu.VMEM((DL // 2, D), BF16),
-            pltpu.VMEM((ROWS, PAIR), BF16),
-            pltpu.SemaphoreType.DMA((5,)),
+            pltpu.SemaphoreType.DMA((2,)),
         ],
         name="bias_tables",
     )
@@ -334,10 +342,8 @@
 
 def encode_kernel(
     count_ref, x_hbm, text_ref, patch_ref, bias_ref, wq_hbm, wk_hbm, wv_hbm,
-    q0, q1, q2, k_ref, v_ref,
-    e0_far, e1_far, e2_far, l0_far, l1_far, l2_far, q0_far, q1_far, q2_far, k_far, v_far,
-    text_scr, patch_scr, raw_scr, x_ref, wq_ref, wk_ref, wv_ref,
-    e0, e1, e2, l0, l1, l2, sems,
+    q0, q1, q2, k_ref, v_ref, e0, e1, e2, l0, l1, l2,
+    text_scr, patch_scr, raw_scr, x_ref, wq_ref, wk_ref, wv_ref, sems,
 ):
     copies = start_all(
         ((x_hbm, x_ref), (wq_hbm, wq_ref), (wk_hbm, wk_ref), (wv_hbm, wv_ref)), sems
@@ -356,8 +362,8 @@
             out[pl.ds(base, 32), cols] = text_conv_block(win, taps, 1)
             return carry
 
-        lax.fori_loop(0, 8, functools.partial(one, out=e0, first=0), 0)
-        lax.fori_loop(0, 8, functools.partial(one, out=e1, first=256), 0)
+        for (first, rows), out in zip(CHUNKS, (e0, e1)):
+            lax.fori_loop(0, rows // 32, functools.partial(one, out=out, first=first), 0)
 
     def patches(side):
         for c in range(D // PAIR):
@@ -367,15 +373,9 @@
             )
 
     by_grid(count, patches)
-    far = start_all(((e0, e0_far), (e1, e1_far), (e2, e2_far)), sems, 4)
     for copy in copies[1:]:
         copy.wait()
-    for i, ((start, rows), e, low, low_far, q, q_far) in enumerate(
-        zip(
-            CHUNKS, (e0, e1, e2), (l0, l1, l2), (l0_far, l1_far, l2_far), (q0, q1, q2),
-            (q0_far, q1_far, q2_far),
-        )
-    ):
+    for (start, rows), e, low, q in zip(CHUNKS, (e0, e1, e2), (l0, l1, l2), (q0, q1, q2)):
         enc = e[...].astype(BF16)
         low[...] = enc
         query = (dot(enc, wq_ref[...]) + bias_ref[0:1, :]).astype(BF16)
@@ -383,35 +383,29 @@
         k_ref[start : start + rows, :] = dot(enc, wk_ref[...]).astype(BF16)
         value = dot(enc, wv_ref[...]) + bias_ref[1:2, :]
         v_ref[start : start + rows, :] = value.astype(BF16)
-        far += start_all(((low, low_far), (q, q_far)), sems, 7 + 2 * i)
     k_ref[ROWS:KEYS, :] = jnp.zeros((KEYS - ROWS, DL), BF16)
     v_ref[ROWS:KEYS, :] = jnp.zeros((KEYS - ROWS, DL), BF16)
-    far += start_all(((k_ref, k_far), (v_ref, v_far)), sems, 13)
-    for copy in far:
-        copy.wait()
-
-
-def encode(order, count, x, text, patch, bias, wq, wk, wv):
+
+
+def encode(order, count, x, text, patch, bias, wq, wk, wv, out):
     chunk = lambda width, dtype: tuple(sds((rows, width), dtype) for _, rows in CHUNKS)
-    scratch = lambda width, dtype: [pltpu.VMEM((rows, width), dtype) for _, rows in CHUNKS]
     keys = (sds((KEYS, DL), BF16), sds((KEYS, DL), BF16))
-    out = order(
+    got, far = order(
         encode_kernel,
         (count, x, text, patch, bias, wq, wk, wv),
         [smem(), hbm()] + [vmem()] * 3 + [hbm()] * 3,
-        chunk(DL, BF16) + keys + chunk(D, F32) + chunk(D, BF16) + chunk(DL, BF16) + keys,
-        [vmem()] * 5 + [hbm()] * 11,
+        chunk(DL, BF16) + keys + chunk(D, F32) + chunk(D, BF16),
+        [vmem()] * 11,
         scratch_shapes=PAGE_SCRATCH
         + [pltpu.VMEM((SEQ, D), BF16)]
         + [pltpu.VMEM((D, DL), BF16)] * 3
-        + scratch(D, F32)
-        + scratch(D, BF16)
-        + [pltpu.SemaphoreType.DMA((15,))],
-        mib=18,
+        + [pltpu.SemaphoreType.DMA((4,))],
+        mib=12,
         us=8000,
+        out=out,
         name="encode_project",
     )
-    return out[0:5], out[5:8], out[8:11], out[11:]
+    return got[0:5], got[5:8], got[8:11], far
 
 
 def bias_rows(e, r_col, k, rows):
@@ -426,13 +420,12 @@
 
 def attend_kernel(
     start, rows, count_ref, q_ref, k_ref, v_ref, u_ref, r_ref, m_ref, o_ref, z_ref,
-    p_hbm, mix_ref, low_far, p_scr, low_scr, sems,
+    p_ref, mix_ref, low_ref,
 ):
     live = iota((1, KEYS), 1) < TEXT + count_ref[0]
     first = first_lanes()
     r_w = r_ref[0, start : start + rows, :]
     r_h = r_ref[1, start : start + rows, :]
-    copies = []
     u = u_ref[start : start + rows, :]
     for pair in range(HL // 2):
         cols = slice(pair * PAIR, pair * PAIR + PAIR)
@@ -459,33 +452,22 @@
             ex = jnp.exp(s - top)
             total = jnp.sum(ex, axis=1, keepdims=True)
             prob = (ex * (1.0 / total)).astype(BF16)
-            p_scr[h] = prob
-            copies.append(pltpu.make_async_copy(p_scr.at[h], p_hbm.at[h], sems.at[h]))
-            copies[-1].start()
+            p_ref[h] = prob
             mixed.append(dot(prob, v))
         low = jnp.where(first, mixed[0], mixed[1]).astype(BF16)
-        low_scr[:, cols] = low
+        low_ref[:, cols] = low
         mix_ref[:, cols] = low.astype(F32)
-    copies.append(pltpu.make_async_copy(low_scr, low_far, sems.at[HL]))
-    copies[-1].start()
-    for copy in copies:
-        copy.wait()
-
-
-def attend(order, c, count, q, k, v, u, r, m, o, z):
+
+
+def attend(order, c, count, q, k, v, u, r, m, o, z, out):
     start, rows = CHUNKS[c]
     return order(
         functools.partial(attend_kernel, start, rows),
         (count, q, k, v, u, r, m, o, z),
         [smem()] + [vmem()] * 8,
         (sds((HL, rows, KEYS), BF16), sds((rows, DL), F32), sds((rows, DL), BF16)),
-        (hbm(), vmem(), hbm()),
-        scratch_shapes=[
-            pltpu.VMEM((HL, rows, KEYS), BF16),
-            pltpu.VMEM((rows, DL), BF16),
-            pltpu.SemaphoreType.DMA((HL + 1,)),
-        ],
-        mib=14,
+        [vmem()] * 3,
+        out=out,
         name=f"attend_{c}",
     )
 
@@ -525,7 +507,7 @@
     part_ref[...] = total
 
 
-def feed(order, c, where, own, other, enc, vec, wo, wo_a, wo_b, wi, bi, w2):
+def feed(order, c, where, own, other, enc, vec, wo, wo_a, wo_b, wi, bi, w2, out):
     _, rows = CHUNKS[c]
     return order(
         feed_kernel,
@@ -541,6 +523,7 @@
         ),
         [vmem()] * 6,
         scratch_shapes=[pltpu.VMEM((rows, D), F32), pltpu.SemaphoreType.DMA((1,))],
+        out=out,
         name=f"feed_{c}",
     )
 
@@ -597,7 +580,8 @@
 
 def feed_back(order, c, count, own, other, xhat1, cot, vec, w2, slope, wi, out_so_far):
     start, rows = CHUNKS[c]
-    block = pl.BlockSpec((256, D), lambda i: (start // 256, 0))
+    high = 256 if start == TEXT else rows
+    block = pl.BlockSpec((high, D), lambda i: (start // high, 0))
     whole = lambda a: pl.BlockSpec(a.shape, lambda i: (0, 0))
     shapes = (
         sds((SEQ, D), BF16),
@@ -683,93 +667,94 @@
     )
 
 
+SPLIT = 1024
+
+
 def attention_grads_kernel(slab, where_ref, *refs):
     low, dq, (dk_ref, dv_ref), g0, mix = refs[0:3], refs[3:6], refs[6:8], refs[8:11], refs[11:14]
-    outs = refs[14:]
-    half = len(outs) // 2
-    step = pl.program_id(0)
     chunks = lambda ref: [ref.at[start : start + rows] for start, rows in CHUNKS]
-    todo = (
-        (low, dq, outs[:half]),
-        (low, chunks(dk_ref), outs[:half]),
-        (low, chunks(dv_ref), outs[half:]),
-        (g0, mix, outs[half:]),
-    )
-    for i, (lefts, rights, out) in enumerate(todo):
-
-        @pl.when(step == i)
-        def _(lefts=lefts, rights=rights, out=out):
-            put_grads(slab, where_ref, tn_sum(lefts, rights), out)
+    todo = ((low, dq), (low, chunks(dk_ref)), (low, chunks(dv_ref)), (g0, mix))
+    for i, (lefts, rights) in enumerate(todo):
+        grad = tn_sum(lefts, rights)
+        first, last = i * DL, i * DL + DL
+        for part, (low_end, high_end) in enumerate(((0, SPLIT), (SPLIT, 4 * DL))):
+            begin, end = max(first, low_end), min(last, high_end)
+            if begin < end:
+                cols = slice(begin - low_end, end - low_end)
+                outs = [ref.at[:, cols] for ref in refs[14 + 2 * part : 16 + 2 * part]]
+                store_slabs(slab, where_ref[1], grad[:, begin - first : end - first], *outs)
 
 
 def attention_grads(order, slab, where, enc_low, dq, dk, dv, g0, mix):
     operands = [*enc_low, *dq, dk, dv, *g0, *mix]
-    rows, count = (D, 1) if slab is None else (D // 2, 2)
+    widths = (SPLIT, SPLIT, 4 * DL - SPLIT, 4 * DL - SPLIT)
     return order(
         functools.partial(attention_grads_kernel, slab),
         (where, *operands),
-        [smem()] + [pl.BlockSpec(a.shape, lambda i: (0, 0)) for a in operands],
-        (sds((rows, D), F32),) * (2 * count),
-        [pl.BlockSpec((rows, DL), lambda i: (0, jnp.minimum(i, 1)))] * count
-        + [pl.BlockSpec((rows, DL), lambda i: (0, jnp.maximum(i - 2, 0)))] * count,
-        grid=(4,),
-        mib=24,
+        [smem()] + [vmem()] * len(operands),
+        [sds((D // 2, width), F32) for width in widths],
+        [vmem()] * 4,
         name="attention_grads",
     )
 
 
-SMALL = 40
-
-
-def halve_kernel(slabs, high, where_bit, extra, where_ref, *refs):
-    small_ref = None
-    if extra == "first":
-        small_ref, *refs = refs
-    *pairs, own_ref, out_ref = refs
+def plain_grads_kernel(*refs):
+    low, dq, (dk_ref, dv_ref), g0, mix = refs[0:3], refs[3:6], refs[6:8], refs[8:11], refs[11:14]
+    chunks = lambda ref: [ref.at[start : start + rows] for start, rows in CHUNKS]
+    todo = ((low, dq), (low, chunks(dk_ref)), (low, chunks(dv_ref)), (g0, mix))
+    for i, (lefts, rights) in enumerate(todo):
+        refs[14][:, i * DL : i * DL + DL] = tn_sum(lefts, rights)
+
+
+def plain_grads(order, enc_low, dq, dk, dv, g0, mix):
+    operands = [*enc_low, *dq, dk, dv, *g0, *mix]
+    return order(
+        plain_grads_kernel, operands, [vmem()] * len(operands), (sds((D, 4 * DL), F32),), [vmem()],
+        name="plain_grads",
+    )
+
+
+def halve_kernel(slabs, high, where_bit, count, extra, where_ref, *refs):
+    *smalls, a_ref, b_ref, own_ref, out_ref = refs
     mine = where_ref[where_bit]
-    total = pairs[0].shape[0] - (SMALL if extra == "more" else 0)
+    total = a_ref.shape[0] - (extra if count == 0 else 0)
     run = high * (total // slabs)
-    at = 0
-    for a_ref, b_ref in zip(pairs[0::2], pairs[1::2]):
-        cols = slice(at, at + a_ref.shape[1])
-        at += a_ref.shape[1]
-        for i in range(slabs // (2 * high)):
-            for ref, which in ((own_ref, mine), (out_ref, 1 - mine)):
-                rows = pl.ds(pl.multiple_of((2 * i + which) * run, 8), run)
-                ref[i * run : (i + 1) * run, cols] = a_ref[rows, :] + b_ref[rows, :]
-    if extra is not None:
-        small = small_ref[...] if extra == "first" else pairs[0][total:] + pairs[1][total:]
-        own_ref[total // 2 :, :] = small
-        out_ref[total // 2 :, :] = small
-
-
-def halve(order, where, pairs, slabs, high, where_bit, first, width, name, small=None, extra=None):
-    rows = pairs[0][0].shape[0]
-    out_rows = rows // 2
-    operands, specs = [where], [smem()]
-    if extra == "first":
-        out_rows = rows // 2 + SMALL
-        operands.append(small)
-        specs.append(vmem())
-    if extra == "more":
-        out_rows = (rows - SMALL) // 2 + SMALL
-    if len(pairs) == 1 and extra is None:
+    for i in range(slabs // (2 * high)):
+        for ref, which in ((own_ref, mine), (out_ref, 1 - mine)):
+            rows = pl.ds(pl.multiple_of((2 * i + which) * run, 8), run)
+            ref[i * run : (i + 1) * run, :] = a_ref[rows, :] + b_ref[rows, :]
+    if extra == 0:
+        return
+    width = D
+    small = a_ref[total:, 0:width] + b_ref[total:, 0:width] if count == 0 else smalls[0][...]
+    for ref in smalls[1:]:
+        small = small + ref[...]
+    for ref in (own_ref, out_ref):
+        ref[total // 2 :, 0:width] = small
+        if ref.shape[1] > width:
+            rest = (extra, ref.shape[1] - width)
+            ref[total // 2 :, width:] = jnp.zeros(rest, F32)
+
+
+def halve(order, where, pair, slabs, high, where_bit, first, width, name, smalls=(), extra=0):
+    rows = pair[0].shape[0]
+    total = rows - (0 if smalls else extra)
+    if extra == 0:
         block = 512 if width % 512 == 0 and first % 512 == 0 else 384
-        at = first // block
-        specs += [pl.BlockSpec((rows, block), lambda i: (0, at + i))] * 2
-        grid = (width // block,)
     else:
         block = width
-        specs += [pl.BlockSpec(a.shape, lambda i: (0, 0)) for pair in pairs for a in pair]
-        grid = (1,)
+    at = first // block
+    out_rows = total // 2 + extra
     half = pl.BlockSpec((out_rows, block), lambda i: (0, i))
     return order(
-        functools.partial(halve_kernel, slabs, high, where_bit, extra),
-        operands + [a for pair in pairs for a in pair],
-        specs,
+        functools.partial(halve_kernel, slabs, high, where_bit, len(smalls), extra),
+        [where, *smalls, *pair],
+        [smem()]
+        + [pl.BlockSpec(a.shape, lambda i: (0, 0)) for a in smalls]
+        + [pl.BlockSpec((rows, block), lambda i: (0, at + i))] * 2,
         (sds((out_rows, width), F32),) * 2,
         [half, half],
-        grid=grid,
+        grid=(width // block,),
         mib=12,
         name=name,
     )
@@ -809,15 +794,12 @@
 
 
 def attend_back_kernel(
-    start, rows, first, dmix_ref, p_hbm, q_ref, k_ref, v_ref, ur_ref, r_ref, o_ref, *rest,
+    start, rows, first, dmix_ref, p_ref, q_ref, k_ref, v_ref, ur_ref, r_ref, o_ref, *rest,
 ):
     if not first:
         dk_in, dv_in, dm_in, dz_in = rest[:4]
         rest = rest[4:]
-    dq_ref, dk_ref, dv_ref, dm_ref, dz_ref, p_scr, sems = rest
-    copies = [pltpu.make_async_copy(p_hbm.at[h], p_scr.at[h], sems.at[h]) for h in range(HL)]
-    for copy in copies:
-        copy.start()
+    dq_ref, dk_ref, dv_ref, dm_ref, dz_ref = rest
     if first:
         dz_ref[...] = jnp.zeros(dz_ref.shape, F32)
     else:
@@ -828,66 +810,74 @@
     r_h = r_ref[1, start : start + rows, :]
     upper = (iota((rows, PAIR), 1) >= 64).astype(jnp.int32)
     ur = ur_ref[start : start + rows, :]
-    for pair in range(HL // 2):
-        cols = slice(pair * PAIR, pair * PAIR + PAIR)
-        q = q_ref[:, cols]
-        k = k_ref[:, cols]
-        v = v_ref[:, cols]
-        dmix = dmix_ref[:, cols]
-        dq_total = None
-        dk_total = None if first else dk_in[:, cols]
-        dv_total = None if first else dv_in[:, cols]
-        for half in range(2):
-            h = 2 * pair + half
-            mine = lanes if half == 0 else jnp.logical_not(lanes)
-            pick = lambda a: jnp.where(mine, a, jnp.zeros_like(a))
-            dmix_m = pick(dmix)
-            copies[h].wait()
-            prob = p_scr[h]
-            dprob = dot_nt(dmix_m, v)
-            prob_f = prob.astype(F32)
-            both = prob_f * dprob
-            ds = both - prob_f * jnp.sum(both, axis=1, keepdims=True)
-            low = ds.astype(BF16)
-            dq = dot(low, pick(k))
-            dk = dot_tn(low, pick(q))
-            dv = dot_tn(prob, dmix_m)
-            dq_total = dq if dq_total is None else dq_total + dq
-            dk_total = dk if dk_total is None else dk_total + dk
-            dv_total = dv if dv_total is None else dv_total + dv
-            for at in range(0, rows, SUB):
-                size = min(SUB, rows - at)
-                sub = (start + at) // SUB
-                sums = {}
-                for g in range(KEYS // SUB):
-                    group = min(max(g - sub + 2, 0), 4)
-                    piece = ds[at : at + size, g * 128 : g * 128 + 128]
-                    sums[group] = piece if group not in sums else sums[group] + piece
-                for group, piece in sums.items():
-                    dz_ref[h, 0:size, group * 128 : group * 128 + 128] += piece
-            dbias = dot_nt(low, o_ref[...])
-            parts = []
-            for plane, r_col in ((0, r_w), (1, r_h)):
-                same = None
-                under = None
-                for kk in range(4):
-                    base = plane * 512 + kk * 128
-                    piece = dbias[:, base : base + 128]
-                    ok = (2 * kk + upper) >= r_col
-                    yes = jnp.where(ok, piece, 0.0)
-                    no = jnp.where(ok, 0.0, piece)
-                    same = yes if same is None else same + yes
-                    under = no if under is None else under + no
-                parts += [same, under]
-            dm = dot_tn(ur, jnp.concatenate(parts, axis=1).astype(BF16))
-            at = slice(h * 512, h * 512 + 512)
-            dm_ref[:, at] = dm if first else dm_in[:, at] + dm
-        dq_ref[:, cols] = dq_total * 0.125
-        dk_ref[:, cols] = dk_total
-        dv_ref[:, cols] = dv_total
-
-
-def attend_back(order, c, dmix, p, q, k, v, ur, r, o, carry):
+    pick = lambda h, a: jnp.where(
+        lanes if h % 2 == 0 else jnp.logical_not(lanes), a, jnp.zeros_like(a)
+    )
+    pair_cols = lambda h: slice(h // 2 * PAIR, h // 2 * PAIR + PAIR)
+
+    def dprob_of(h):
+        return dot_nt(pick(h, dmix_ref[:, pair_cols(h)]), v_ref[:, pair_cols(h)])
+
+    def back_of(h, dprob):
+        cols = pair_cols(h)
+        prob = p_ref[h]
+        prob_f = prob.astype(F32)
+        both = prob_f * dprob
+        ds = both - prob_f * jnp.sum(both, axis=1, keepdims=True)
+        low = ds.astype(BF16)
+        dq = dot(low, pick(h, k_ref[:, cols]))
+        dk = dot_tn(low, pick(h, q_ref[:, cols]))
+        dv = dot_tn(prob, pick(h, dmix_ref[:, cols]))
+        dbias = dot_nt(low, o_ref[...])
+        for at in range(0, rows, SUB):
+            size = min(SUB, rows - at)
+            sub = (start + at) // SUB
+            sums = {}
+            for g in range(KEYS // SUB):
+                group = min(max(g - sub + 2, 0), 4)
+                piece = ds[at : at + size, g * 128 : g * 128 + 128]
+                sums[group] = piece if group not in sums else sums[group] + piece
+            for group, piece in sums.items():
+                dz_ref[h, 0:size, group * 128 : group * 128 + 128] += piece
+        return dq, dk, dv, dbias
+
+    def table_of(h, dbias):
+        parts = []
+        for plane, r_col in ((0, r_w), (1, r_h)):
+            same = None
+            under = None
+            for kk in range(4):
+                base = plane * 512 + kk * 128
+                piece = dbias[:, base : base + 128]
+                ok = (2 * kk + upper) >= r_col
+                yes = jnp.where(ok, piece, 0.0)
+                no = jnp.where(ok, 0.0, piece)
+                same = yes if same is None else same + yes
+                under = no if under is None else under + no
+            parts += [same, under]
+        dm = dot_tn(ur, jnp.concatenate(parts, axis=1).astype(BF16))
+        at = slice(h * 512, h * 512 + 512)
+        dm_ref[:, at] = dm if first else dm_in[:, at] + dm
+
+    dprob = dprob_of(0)
+    totals = None
+    for h in range(HL):
+        following = dprob_of(h + 1) if h + 1 < HL else None
+        dq, dk, dv, dbias = back_of(h, dprob)
+        dprob = following
+        cols = pair_cols(h)
+        if h % 2 == 0:
+            totals = (dq, dk, dv)
+        else:
+            dq_ref[:, cols] = (totals[0] + dq) * 0.125
+            dk = totals[1] + dk
+            dv = totals[2] + dv
+            dk_ref[:, cols] = dk if first else dk_in[:, cols] + dk
+            dv_ref[:, cols] = dv if first else dv_in[:, cols] + dv
+        table_of(h, dbias)
+
+
+def attend_back(order, c, dmix, p, q, k, v, ur, r, o, carry, into):
     start, rows = CHUNKS[c]
     operands = [dmix, p, q, k, v, ur, r, o]
     aliases = {}
@@ -897,7 +887,7 @@
     return order(
         functools.partial(attend_back_kernel, start, rows, carry is None),
         operands,
-        [vmem(), hbm()] + [vmem()] * (len(operands) - 2),
+        [vmem()] * len(operands),
         (
             sds((rows, DL), F32),
             sds((KEYS, DL), F32),
@@ -906,9 +896,8 @@
             sds((HL, SUB, 640), F32),
         ),
         [vmem()] * 5,
-        scratch_shapes=[pltpu.VMEM((HL, rows, KEYS), BF16), pltpu.SemaphoreType.DMA((HL,))],
         input_output_aliases=aliases,
-        mib=14,
+        into=into,
         name=f"attend_back_{c}",
     )
 
@@ -1004,6 +993,7 @@
         (sds((ROWS, D), F32), sds((8, D), F32)),
         [vmem()] * 2,
         scratch_shapes=[pltpu.VMEM((D, DL), BF16)] * 3 + [pltpu.SemaphoreType.DMA((3,))],
+        us=15000,
         name="project_back",
     )
 
@@ -1034,13 +1024,12 @@
             return tuple(out)
 
         sums = tuple(jnp.zeros((8, 384), F32) for _ in shifts)
-        sums = lax.fori_loop(0, 8, functools.partial(one, res=r0, first=0), sums)
-        sums = lax.fori_loop(0, 8, functools.partial(one, res=r1, first=256), sums)
-        for dilate in range(3):
-            for tap in range(3):
-                row = 3 * dilate + tap
-                total = sums[3 + (tap - 1) * (dilate + 1)]
-                out_ref[row : row + 1, cols] = col_sum(total)
+        for (first, rows), res in zip(CHUNKS, (r0, r1)):
+            sums = lax.fori_loop(
+                0, rows // 32, functools.partial(one, res=res, first=first), sums
+            )
+        for row, total in enumerate(sums):
+            out_ref[row : row + 1, cols] = col_sum(total)
 
     def patches(side):
         live, has_left, has_right = grid_masks(side)
@@ -1055,7 +1044,7 @@
                 if ds == 1:
                     masked = jnp.where(has_right, grad, 0.0)
                 for dr in (-1, 0, 1):
-                    row = 9 + 3 * (dr + 1) + ds + 1
+                    row = 7 + 3 * (dr + 1) + ds + 1
                     at = MARGIN + dr * side + ds
                     out_ref[row : row + 1, cols] = col_sum(masked * win[at : at + 208])
 
@@ -1067,7 +1056,7 @@
         taps_kernel,
         (count, x, part, *res),
         [smem(), hbm(), vmem()] + [hbm()] * 3,
-        (sds((24, D), F32),),
+        (sds((16, D), F32),),
         [vmem()],
         scratch_shapes=PAGE_SCRATCH
         + [pltpu.VMEM((SEQ, D), BF16)]
@@ -1082,11 +1071,11 @@
     zero8 = jnp.zeros((8, D), F32)
     text_scr[0:8, :] = zero8
     text_scr[520:528, :] = zero8
-    for r, at in ((r0, 0), (r1, 256)):
-        for b in range(4):
+    for r, (at, rows) in zip((r0, r1), CHUNKS):
+        for b in range(rows // 64):
             res = r[64 * b : 64 * b + 64, :]
-            rows = slice(at + 64 * b, at + 64 * b + 64)
-            text_scr[8 + at + 64 * b : 72 + at + 64 * b, :] = res + (p[rows, :] + s[rows, :])
+            here = slice(at + 64 * b, at + 64 * b + 64)
+            text_scr[8 + at + 64 * b : 72 + at + 64 * b, :] = res + (p[here, :] + s[here, :])
     for c in range(2):
         cols = slice(c * 384, c * 384 + 384)
         taps = text_taps(text_ref, cols)
@@ -1101,10 +1090,11 @@
 
 
 def decode_kernel(
-    count_ref, text_ref, patch_ref, p, s, r0_far, r1_far, r2_far, out_ref,
-    text_scr, patch_scr, raw_scr, r0, r1, r2, sems,
+    count_ref, text_ref, patch_ref, p_far, s_far, r0_far, r1_far, r2_far, out_ref,
+    text_scr, patch_scr, raw_scr, p, s, r0, r1, r2, sems,
 ):
-    for copy in start_all(((r0_far, r0), (r1_far, r1), (r2_far, r2)), sems):
+    pairs = ((p_far, p), (s_far, s), (r0_far, r0), (r1_far, r1), (r2_far, r2))
+    for copy in start_all(pairs, sems):
         copy.wait()
     decode_text_kernel(text_ref, p, s, r0, r1, out_ref, text_scr)
     count = count_ref[0]
@@ -1124,13 +1114,15 @@
     return order(
         decode_kernel,
         (count, text_w, patch_w, part, other, *res),
-        [smem()] + [vmem()] * 4 + [hbm()] * 3,
+        [smem()] + [vmem()] * 2 + [hbm()] * 5,
         (sds((SEQ, D), BF16),),
-        [vmem()],
+        whole_blocks((sds((SEQ, D), BF16),)),
+        grid=(1,),
         scratch_shapes=PAGE_SCRATCH
+        + [pltpu.VMEM((ROWS, D), F32)] * 2
         + [pltpu.VMEM((rows, D), F32) for _, rows in CHUNKS]
-        + [pltpu.SemaphoreType.DMA((3,))],
-        mib=14,
+        + [pltpu.SemaphoreType.DMA((5,))],
+        mib=18,
         name="decode",
     )[0]
 
@@ -1151,86 +1143,120 @@
     def __init__(self, order, dp, where, pair, bits, name, first, width):
         self.order, self.dp, self.where, self.bits, self.name = order, dp, where, bits, name
         self.window = (first, width)
-        self.pairs = [pair]
+        self.pair = pair
         self.left = list(range(1, dp.bit_length() - 1))
-
-    def join(self, other):
-        self.pairs += other.pairs
-        self.window = (self.window[0], self.window[1] + other.window[1])
-
-    def step(self, small=None, extra=None):
-        if len(self.pairs[0]) == 1:
+        self.extra = 0
+
+    def step(self, *smalls):
+        if len(self.pair) == 1:
             return
         bit = self.bits[0]
         self.bits = self.bits[1:]
         at = self.left.index(bit)
+        if smalls:
+            self.extra = smalls[0].shape[0]
         own, out = halve(
-            self.order, self.where, self.pairs, 2 ** len(self.left), 2**at, 1 + bit, *self.window,
-            f"{self.name}_{bit}", small, extra,
+            self.order, self.where, self.pair, 2 ** len(self.left), 2**at, 1 + bit, *self.window,
+            f"{self.name}_{bit}", smalls, self.extra,
         )
         self.window = (0, self.window[1])
         self.left.remove(bit)
-        self.pairs = [(own, swap_dp(out, 2**bit, self.dp))]
+        self.pair = (own, swap_dp(out, 2**bit, self.dp))
 
     def total(self):
-        if len(self.pairs[0]) == 1:
-            first, width = self.window
-            whole = self.pairs[0][0][:, first : first + width]
-            return lax.psum_scatter(whole, "dp", scatter_dimension=0, tiled=True)
-        return self.pairs[0][0] + self.pairs[0][1]
-
-
-def total_kernel(turned, a0, a1, out):
+        first, width = self.window
+        whole = self.pair[0][:, first : first + width]
+        return lax.psum_scatter(whole, "dp", scatter_dimension=0, tiled=True)
+
+
+def whole_blocks(shapes):
+    return [pl.BlockSpec(a.shape, lambda i, n=len(a.shape): (0,) * n) for a in shapes]
+
+
+EARLY = 8
+LATE = 24
+
+
+def total_of(order, part, name):
+    pair = part.pair
+    shapes = (sds(pair[0].shape, F32),)
+    return order(
+        add_kernel, pair, whole_blocks(pair), shapes, whole_blocks(shapes), grid=(1,), name=name
+    )[0]
+
+
+def add_kernel(a, b, out):
+    out[...] = a[...] + b[...]
+
+
+def add_here(order, a, b, name):
+    return order(
+        add_kernel, (a, b), [vmem()] * 2, (sds(a.shape, F32),), [vmem()], name=name
+    )[0]
+
+
+def last_totals_kernel(
+    a0, a1, b0, b1, oa, ob, ia, ib, late, late_other,
+    q_ref, k_ref, v_ref, o_ref, outer_ref, inner_ref, small_ref,
+):
+    slab = q_ref.shape[0]
     both = a0[...] + a1[...]
-    out[...] = jnp.transpose(both) if turned else both
-
-
-def total_of(order, part, turned, name):
-    pair = part.pairs[0]
-    shape = pair[0].shape[::-1] if turned else pair[0].shape
-    return order(
-        functools.partial(total_kernel, turned), pair, [vmem()] * 2, (sds(shape, F32),), [vmem()],
-        name=name,
-    )[0]
-
-
-def attention_totals_kernel(a0, a1, b0, b1, q_ref, k_ref, v_ref, o_ref, small_ref):
-    both = a0[...] + a1[...]
-    slab = q_ref.shape[0]
     q_ref[...] = both[0:slab, 0:DL]
     k_ref[...] = both[0:slab, DL:D]
-    small_ref[...] = both[slab:]
+    v_ref[:, 0 : SPLIT - D] = both[0:slab, D:SPLIT]
+    small_ref[0:LATE, :] = late[...] + late_other[...]
     both = b0[...] + b1[...]
-    v_ref[...] = both[:, 0:DL]
-    o_ref[...] = jnp.transpose(both[:, DL:D])
-
-
-def attention_totals(order, query_key, value_out, slab):
-    pairs = [a for part in (query_key, value_out) for a in part.pairs[0]]
+    v_ref[:, SPLIT - D : DL] = both[:, 0 : D + DL - SPLIT]
+    o_ref[...] = both[:, D + DL - SPLIT :]
+    outer_ref[:, 0:D] = oa[0:slab, :]
+    outer_ref[:, D:FL] = ob[...]
+    inner_ref[:, 0:D] = ia[...]
+    inner_ref[:, D:FL] = ib[...]
+    small_ref[LATE : LATE + EARLY, :] = oa[slab:, :]
+
+
+def last_totals(order, part_a, part_b, *rest):
+    *rest, slab = rest
+    operands = [*part_a.pair, *part_b.pair, *rest]
     plain = sds((slab, DL), F32)
-    return order(
-        attention_totals_kernel, pairs, [vmem()] * 4,
-        (plain, plain, plain, sds((DL, slab), F32), sds((SMALL, D), F32)), [vmem()] * 5,
-        name="attention_totals",
-    )
-
-
-def gather_small_kernel(taps, a0, a1, a2, f0, f1, f2, bias, tab, out):
+    wide = sds((slab, FL), F32)
+    shapes = (plain,) * 4 + (wide, wide, sds((LATE + EARLY, D), F32))
+    return order(
+        last_totals_kernel, operands, whole_blocks(operands), shapes, whole_blocks(shapes),
+        grid=(1,), name="last_totals",
+    )
+
+
+def gather_early_kernel(f0, f1, f2, out):
+    sums = f0[...] + f1[...] + f2[...]
     out[...] = jnp.zeros(out.shape, F32)
-    out[0:18, :] = taps[0:18, :]
-    out[18:21, :] = (a0[...] + a1[...] + a2[...])[0:3]
-    feed_sums = f0[...] + f1[...] + f2[...]
-    out[21:24, :] = feed_sums[1:4, 0:D]
-    out[24:25, :] = bias[0:1, :]
-    out[25:26, :] = feed_sums[0:1, 0:D]
-    out[26:27, :] = feed_sums[0:1, D:]
-    out[27 : 27 + HL, 0:256] = tab[0:HL, :]
-
-
-def gather_small(order, *rest):
-    return order(
-        gather_small_kernel, rest, [vmem()] * 9, (sds((SMALL, D), F32),), [vmem()],
-        name="gather_small",
+    out[0:1, :] = sums[0:1, 0:D]
+    out[1:2, :] = sums[0:1, D:FL]
+    out[2:5, :] = sums[1:4, 0:D]
+
+
+def gather_early(order, sums, into):
+    (early,), moved = order(
+        gather_early_kernel, sums, [vmem()] * 3, (sds((EARLY, D), F32),), [vmem()], into=into,
+        name="gather_early",
+    )
+    return early, moved
+
+
+def gather_late_kernel(taps, a0, a1, a2, bias, tab, out):
+    out[...] = jnp.zeros(out.shape, F32)
+    out[0:16, :] = taps[0:16, :]
+    out[16:19, :] = (a0[...] + a1[...] + a2[...])[0:3]
+    out[19:20, :] = bias[0:1, :]
+    for h in range(HL):
+        at = 256 * (h % 3)
+        out[20 + h // 3 : 21 + h // 3, at : at + 256] = tab[h : h + 1, :]
+
+
+def gather_late(order, *rest):
+    return order(
+        gather_late_kernel, rest, [vmem()] * 6, (sds((LATE, D), F32),), [vmem()],
+        name="gather_late",
     )[0]
 
 
@@ -1242,30 +1268,34 @@
     small = own[...] + core[...]
     slab = patch.shape[1]
     turn = lambda a: pltpu.roll(a, lax.rem(D - place_ref[0] * slab, D), 1)[:, 0:slab]
-    shard = turn(small[0:24])
-    taps = shard + turn(other[...] + both[...])
-    for i in range(3):
-        text[i] = taps[3 * i : 3 * i + 3]
-    patch[...] = taps[9:18]
-    for i, ref in enumerate((out_b, gain1, shift1, outer_b, gain2, shift2)):
-        ref[...] = shard[18 + i]
-    query_b[...] = small[24, 0:DL]
-    value_b[...] = small[24, DL:D]
-    inner_b[0:D] = small[25]
-    inner_b[D:FL] = small[26]
-    tables = jnp.transpose(small[24:40, 0:256])
-    line[...] = tables[0:32, 3 : 3 + HL]
-    width[...] = tables[32:96, 3 : 3 + HL]
-    height[...] = tables[96:160, 3 : 3 + HL]
+    shard = turn(small)
+    taps = shard[0:16] + turn(other[...] + both[...])
+    for dilate in range(3):
+        for tap in range(3):
+            text[dilate, tap] = taps[3 + (tap - 1) * (dilate + 1)]
+    patch[...] = taps[7:16]
+    rows = (16, 17, 18, LATE + 2, LATE + 3, LATE + 4)
+    for i, ref in zip(rows, (out_b, gain1, shift1, outer_b, gain2, shift2)):
+        ref[...] = shard[i]
+    query_b[...] = small[19, 0:DL]
+    value_b[...] = small[19, DL:D]
+    inner_b[0:D] = small[LATE]
+    inner_b[D:FL] = small[LATE + 1]
+    for h in range(HL):
+        row, at = 20 + h // 3, 256 * (h % 3)
+        line[h : h + 1, :] = small[row : row + 1, at : at + 32]
+        width[h : h + 1, :] = small[row : row + 1, at + 32 : at + 96]
+        height[h : h + 1, :] = small[row : row + 1, at + 96 : at + 160]
 
 
 def finish(order, place, own, core, other, both, slab):
     f = lambda *shape: sds(shape, F32)
     shapes = (f(3, 3, slab), f(9, slab)) + (f(slab),) * 6
-    shapes += (f(DL), f(DL), f(FL), f(32, HL), f(64, HL), f(64, HL))
-    return order(
-        finish_kernel, (place, own, core, other, both), [smem()] + [vmem()] * 4, shapes,
-        [vmem()] * 14, name="finish",
+    shapes += (f(DL), f(DL), f(FL), f(HL, 32), f(HL, 64), f(HL, 64))
+    return order(
+        finish_kernel, (place, own, core, other, both),
+        [smem()] + whole_blocks((own, core, other, both)), shapes, whole_blocks(shapes), grid=(1,),
+        name="finish",
     )
 
 
@@ -1311,7 +1341,7 @@
     slab = D // dp if dp == 16 else None
     order = Order()
 
-    z, m, o, u, r, wo_mine, o_far, ur_far, r_far = make_tables(
+    z, m, o, u, r, wo_mine, ur = make_tables(
         order,
         where,
         jnp.concatenate([jnp.transpose(a) for a in (line_table, width_table, height_table)], axis=1),
@@ -1321,12 +1351,11 @@
     wo_a = swap_tensor(wo_mine)
     row = lax.broadcasted_iota(jnp.int32, (8, 1), 0)
     bias = jnp.where(row == 0, query_bias[None, :], value_bias[None, :]).astype(F32)
-    (q0, q1, q2, k, v), enc, enc_low, far = encode(
+    (q0, q1, q2, k, v), enc, enc_low, (o_far, ur_far, r_far) = encode(
         order, patch_counts, x, text_weight, patch_weight, bias,
-        query_weight, key_weight, value_weight,
+        query_weight, key_weight, value_weight, (o, ur, r),
     )
     q = (q0, q1, q2)
-    q_far, k_far, v_far = far[0:3], far[3], far[4]
 
     vec = jnp.zeros((8, 1), F32)
     for i, a in enumerate(
@@ -1337,26 +1366,32 @@
     probs, mix, mix_low, mix_other = ([None] * 3 for _ in range(4))
     xhat, rstd, hlow, act, slope, outer, outer_other = ([None] * 3 for _ in range(7))
 
-    def attention_of(c):
-        p, a, low = attend(order, c, patch_counts, q[c], k, v, u, r, m, o, z)
-        probs[c], mix[c], mix_low[c], mix_other[c] = p, a, low, swap_tensor(a)
-
-    def feed_of(c):
+    def attention_of(c, out):
+        (p, a, low), far = attend(order, c, patch_counts, q[c], k, v, u, r, m, o, z, out)
+        mix[c], mix_other[c] = a, swap_tensor(a)
+        return (p, low), far
+
+    def feed_of(c, out=()):
         got = feed(
             order, c, where, mix[c], mix_other[c], enc[c], vec, out_weight, wo_a, wo_b,
-            inner_weight, bi, outer_weight,
+            inner_weight, bi, outer_weight, out,
         )
+        far = None
+        if out:
+            got, far = got
         for keep, a in zip((xhat, rstd, hlow, act, slope, outer), got):
             keep[c] = a
         outer_other[c] = swap_tensor(got[5])
-
-    attention_of(ORDER[0])
+        return far
+
+    near, far = attention_of(ORDER[0], (*enc, *enc_low, q0, q1, q2, k, v))
+    enc, enc_low, q_far, k_far, v_far = far[0:3], far[3:6], far[6:9], far[9], far[10]
     wo_a = pass_on(order, wo_a)
     wo_b = swap_dp(wo_a, 1, dp)
-    attention_of(ORDER[1])
+    near, (probs[ORDER[0]], mix_low[ORDER[0]]) = attention_of(ORDER[1], near)
     feed_of(ORDER[0])
-    attention_of(ORDER[2])
-    feed_of(ORDER[1])
+    near, (probs[ORDER[1]], mix_low[ORDER[1]]) = attention_of(ORDER[2], near)
+    probs[ORDER[2]], mix_low[ORDER[2]] = feed_of(ORDER[1], near)
     feed_of(ORDER[2])
     layer_out, inner_grad, outer_grad = None, None, None
     dres2, g2, g1, dhid, dhid_other, sums2 = ([None] * 3 for _ in range(6))
@@ -1383,8 +1418,9 @@
     inner_pair, outer_pair = swap_core(inner_grad, dp), swap_core(outer_grad, dp)
     inner = scatter(inner_pair, x_first, "inner", 0, D)
     inner_b = scatter(inner_pair, x_first, "inner_b", D, D)
-    outer_a = scatter(outer_pair, x_first, "outer_a", 0, 512)
-    outer_b = scatter(outer_pair, z_first, "outer_b", 512, 1024)
+    outer_a = scatter(outer_pair, x_first, "outer_a", 0, D)
+    outer_b = scatter(outer_pair, z_first, "outer_b", D, D)
+    early, (prob,) = gather_early(order, sums2, (probs[ORDER[0]],))
     carry = None
     dres1, g0, dq, sums1 = ([None] * 3 for _ in range(4))
     for c in ORDER:
@@ -1397,63 +1433,76 @@
             outer_b.step()
             inner_b.step()
         if c == ORDER[1]:
-            outer_a.step()
+            outer_a.step(early)
             inner.step()
             outer_b.step()
         if c == ORDER[2]:
             inner_b.step()
             inner.step()
             outer_b.step()
-        dq[c], *carry = attend_back(
-            order, c, got[2], probs[c], q_far[c], k_far, v_far, ur_far, r_far, o_far, carry
+        into = [probs[after] for after in ORDER[ORDER.index(c) + 1 :][:1]]
+        got = attend_back(
+            order, c, got[2], prob, q_far[c], k_far, v_far, ur_far, r_far, o_far, carry, into
         )
+        if into:
+            got, (prob,) = got
+        dq[c], *carry = got
     dk, dv, dm, dz = carry
+    if dp == 16:
+        total_outer_b = total_of(order, outer_b, "outer_b_total")
+        total_inner = total_of(order, inner, "inner_total")
     outer_a.step()
     inner_b.step()
+    operands = (enc_low, dq, dk, dv, g0, mix_low)
     if dp == 16:
-        total_inner = total_of(order, inner, False, "inner_total")
-        total_outer_b = total_of(order, outer_b, True, "outer_b_total")
-    got = attention_grads(order, slab, where, enc_low, dq, dk, dv, g0, mix_low)
-    half_way = len(got) // 2
-    query_key = scatter(swap_core(got[:half_way], dp), x_first, "query_key", 0, D)
-    value_out = scatter(swap_core(got[half_way:], dp), z_first, "value_out", 0, D)
+        got = attention_grads(order, slab, where, *operands)
+        first_pair, second_pair = swap_core(got[0:2], dp), swap_core(got[2:4], dp)
+    else:
+        first_pair = second_pair = plain_grads(order, *operands)
+    rest = 0 if dp == 16 else SPLIT
+    part_a = scatter(first_pair, x_first, "part_a", 0, SPLIT)
+    part_b = scatter(second_pair, z_first, "part_b", rest, 4 * DL - SPLIT)
     part, bias_sums = project_back(order, dq, dk, dv, query_weight, key_weight, value_weight)
     part_other = swap_tensor(part)
+    part_a.step()
+    part_b.step()
     tables = table_sums(order, dm, dz)
     taps = tap_sums(order, patch_counts, x, part, dres1)
-    small = gather_small(order, taps, *sums1, *sums2, bias_sums, tables)
+    late = gather_late(order, taps, *sums1, bias_sums, tables)
+    late_other = swap_dp(late, 2, dp)
     outer_a.step()
     if dp == 16:
-        total_inner_b = total_of(order, inner_b, False, "inner_b_total")
-    query_key.step(small, "first")
-    value_out.step()
-    query_key.step(None, "more")
-    value_out.step()
+        total_inner_b = total_of(order, inner_b, "inner_b_total")
+    part_b.step()
+    part_a.step()
     if dp == 16:
-        total_outer_a = total_of(order, outer_a, True, "outer_a_total")
-    query_key.step(None, "more")
-    value_out.step()
+        late = add_here(order, late, late_other, "late_2")
+        late_other = swap_dp(late, 4, dp)
+    part_a.step()
+    part_b.step()
+    if dp == 16:
+        late = add_here(order, late, late_other, "late_4")
+        late_other = swap_dp(late, 8, dp)
     input_grad = decode(order, patch_counts, text_weight, patch_weight, part, part_other, dres1)
     if dp == 16:
-        inner_total = jnp.concatenate([total_inner, total_inner_b], axis=1)
-        sum_outer = jnp.concatenate([total_outer_a, total_outer_b], axis=0)
-        grad_q, grad_k, grad_v, grad_o, small = attention_totals(
-            order, query_key, value_out, slab
+        total_outer_a = total_of(order, outer_a, "outer_a_total")
+        grad_q, grad_k, grad_v, grad_o, sum_outer, inner_total, small = last_totals(
+            order, part_a, part_b, total_outer_a, total_outer_b, total_inner, total_inner_b,
+            late, late_other, slab,
         )
     else:
-        grad_q, grad_k = jnp.split(query_key.total(), 2, axis=1)
-        grad_v, grad_o = jnp.split(value_out.total(), 2, axis=1)
-        grad_o = jnp.transpose(grad_o)
         inner_total = jnp.concatenate([inner.total(), inner_b.total()], axis=1)
         sum_outer = jnp.concatenate([outer_a.total(), outer_b.total()], axis=1)
-        sum_outer = jnp.transpose(sum_outer)
+        both = jnp.concatenate([part_a.total(), part_b.total()], axis=1)
+        grad_q, grad_k, grad_v, grad_o = jnp.split(both, 4, axis=1)
+        small = jnp.concatenate([late, early], axis=0)
         bit = 2
         while bit < dp:
             small = small + swap_dp(small, bit, dp)
             bit *= 2
     small = finish(
         order, jnp.reshape(place, (1,)).astype(jnp.int32), small, swap_dp(small, 1, dp),
-        swap_tensor(small[0:24]), swap_both(small[0:24], dp), D // dp,
+        swap_tensor(small[0:16]), swap_both(small[0:16], dp), D // dp,
     )
     text, patch, out_b, gain1, shift1, outer_b, gain2, shift2 = small[:8]
     query_b, value_b, inner_b, line, width, height = small[8:]
@@ -1467,16 +1516,16 @@
         grad_k,
         grad_v,
         value_b,
-        grad_o,
+        jnp.transpose(grad_o),
         out_b,
-        line,
-        width,
-        height,
+        jnp.transpose(line),
+        jnp.transpose(width),
+        jnp.transpose(height),
         gain1,
         shift1,
         inner_total,
         inner_b,
-        sum_outer,
+        jnp.transpose(sum_outer),
         outer_b,
         gain2,
         shift2,

time: 275 us -> 252 us (0.916)
  Pallas kernels: 145 us -> 126 us
  waiting for transfers between devices: 65.2 us -> 77.2 us
  local copies, waits for them, and re-layouts: 13.7 us -> 1.97 us
    pallas_call x54 -> x57, Pallas kernels: 145 us -> 126 us  [__call__(): pl.pallas_call(body, out_shape=tuple(out_shape) + tuple(shapes) + (TOKEN,...]
    ppermute x12, waiting for transfers between devices: 34 us -> 44.2 us  [swap_tensor(): return lax.ppermute(x, 'tensor', [(0, 1), (1, 0)])]
    unnamed x102 -> x46, local copies, waits for them, and re-layouts: 11.1 us -> 1.87 us
    ppermute x12, starting transfers between devices: 16.2 us -> 12.1 us  [swap_tensor(): return lax.ppermute(x, 'tensor', [(0, 1), (1, 0)])]
    ppermute x24 -> x27, starting transfers between devices: 24.9 us -> 26 us  [swap_dp(): return lax.ppermute(x, 'dp', [(i, i ^ bit) for i in range(dp)])]
    ppermute x24 -> x27, waiting for transfers between devices: 31.2 us -> 32 us  [swap_dp(): return lax.ppermute(x, 'dp', [(i, i ^ bit) for i in range(dp)])]
  transfers between devices with their start and end apart: 37 -> 40, of which waited for: 11 -> 16; matrix products, arithmetic and copies ran while one was open for 2% -> 0% of each run, Pallas kernels for 48% -> 46%
where the time goes in v2:
time: 252 us; the launch traced here: 247 us
  Pallas kernels  126 us (50%)
  waiting for transfers between devices  77.2 us (31%)
  starting transfers between devices  38.5 us (15%)
  between operations  2.56 us (1%)
    pallas_call x57, Pallas kernels, __call__(): pl.pallas_call(body, out_shape=tuple(out_shape) + tuple(shapes) + (TOKEN,...  126 us
    ppermute x12, waiting for transfers between devices, swap_tensor(): return lax.ppermute(x, 'tensor', [(0, 1), (1, 0)])  44.2 us
    ppermute x27, waiting for transfers between devices, swap_dp(): return lax.ppermute(x, 'dp', [(i, i ^ bit) for i in range(dp)])  32 us
    ppermute x27, starting transfers between devices, swap_dp(): return lax.ppermute(x, 'dp', [(i, i ^ bit) for i in range(dp)])  26 us
    ppermute x12, starting transfers between devices, swap_tensor(): return lax.ppermute(x, 'tensor', [(0, 1), (1, 0)])  12.1 us
  transfers between devices with their start and end apart: 40, of which 16 were waited for; matrix products, arithmetic and copies ran while one was open for 0% of the time, Pallas kernels for 46%

profile of v2, /device:TPU:0, one launch (start us, length us, event | category | flops | bytes accessed | tf_op | source)
XLA Modules:
  0.0 247.4 jit_solution(1790937700253232048)
XLA Ops:
  10.3 6.4 %encode_project.1 = (bf16[256,384]{1,0:T(8,128)(2,1)S(1)}, bf16[256,384]{1,0:T(8,128)(2,1)S(1)}, bf16[208,384]{1,0:T(8,128)(2,1)S(1)}, bf16[768,384]{1,0:T(8,128...) custom-call(s32[1]{0:T(128)S(6)} %copy.70.refs_0_, ...), custom_call_target="tpu_custom_call" | custom-call | flops 8000000000 | bytes 8000000 | tf_op jit(solution)/shard_map/encode_project/pallas_call | solution.py:103
  16.8 8.8 %attend_2.1 = (bf16[6,208,768]{2,1,0:T(8,128)(2,1)S(1)}, f32[208,384]{1,0:T(8,128)S(1)}, bf16[208,384]{1,0:T(8,128)(2,1)S(1)}, f32[256,768]{1,0:T(8,128)S(1)}, f...) custom-call(s32[1]{0:T(128)S(6)} %copy.70.refs_0_, ...), custom_call_target="tpu_custom_call" | custom-call | flops 1000000 | bytes 1000 | tf_op jit(solution)/shard_map/attend_2/pallas_call | solution.py:103
  26.3 7.7 %attend_0.1 = (bf16[6,256,768]{2,1,0:T(8,128)(2,1)S(1)}, f32[256,384]{1,0:T(8,128)S(1)}, bf16[256,384]{1,0:T(8,128)(2,1)S(1)}, bf16[6,208,768]{2,1,0:T(8,128)(2,...) custom-call(s32[1]{0:T(128)S(6)} %copy.70.refs_0_, bf16[256,384]{1,0:T(8,128)(2,1)S(1)} %get-tuple-element.284.refs_15_.refs_1_, ...), custom_call_target="tpu_custom_call" | custom-call | flops 1000000 | bytes 1000 | tf_op jit(solution)/shard_map/attend_0/pallas_call | solution.py:103
  36.0 3.3 %feed_2.1 = (f32[208,768]{1,0:T(8,128)S(1)}, f32[208,128]{1,0:T(8,128)S(1)}, bf16[208,768]{1,0:T(8,128)(2,1)S(1)}, bf16[208,1536]{1,0:T(8,128)(2,1)S(1)}, f32[20...) custom-call(s32[5]{0:T(128)S(1)} %stack.23.refs_0_, f32[208,384]{1,0:T(8,128)S(1)} %get-tuple-element.300.refs_1_, ...), custom_call_target="tpu_custom_call" | custom-call | flops 1000000 | bytes 1000 | tf_op jit(solution)/shard_map/feed_2/pallas_call | solution.py:103
  41.4 7.7 %attend_1.1 = (bf16[6,256,768]{2,1,0:T(8,128)(2,1)S(1)}, f32[256,384]{1,0:T(8,128)S(1)}, bf16[256,384]{1,0:T(8,128)(2,1)S(1)}, bf16[6,256,768]{2,1,0:T(8,128)(2,...) custom-call(s32[1]{0:T(128)S(6)} %copy.70.refs_0_, bf16[256,384]{1,0:T(8,128)(2,1)S(1)} %get-tuple-element.278.refs_16_.refs_1_, ...), custom_call_target="tpu_custom_call" | custom-call | flops 1000000 | bytes 1000 | tf_op jit(solution)/shard_map/attend_1/pallas_call | solution.py:103
  49.4 15.6 %collective-permute-done.4.refs_2_ = f32[256,384]{1,0:T(8,128)S(1)} collective-permute-done((f32[256,384]{1,0:T(8,128)S(1)}, f32[256,384]{1,0:T(8,128)S(1)}, u32[]{:S(2)}, u32[]{:S(2)}) %collective-permute-start.4) | collective-permute-done | bytes 393248 | tf_op jit(solution)/shard_map/ppermute | solution.py:1131
  65.0 3.7 %feed_0.1 = (f32[256,768]{1,0:T(8,128)S(1)}, f32[256,128]{1,0:T(8,128)S(1)}, bf16[256,768]{1,0:T(8,128)(2,1)S(1)}, bf16[256,1536]{1,0:T(8,128)(2,1)S(1)}, f32[25...) custom-call(s32[5]{0:T(128)S(1)} %stack.23.refs_0_, ...), custom_call_target="tpu_custom_call" | custom-call | flops 1000000 | bytes 1000 | tf_op jit(solution)/shard_map/feed_0/pallas_call | solution.py:103
  69.1 4.4 %collective-permute-done.3.refs_2_ = f32[256,384]{1,0:T(8,128)S(1)} collective-permute-done((f32[256,384]{1,0:T(8,128)S(1)}, f32[256,384]{1,0:T(8,128)S(1)}, u32[]{:S(2)}, u32[]{:S(2)}) %collective-permute-start.3) | collective-permute-done | bytes 393248 | tf_op jit(solution)/shard_map/ppermute | solution.py:1131
  73.5 3.5 %feed_1.1 = (f32[256,768]{1,0:T(8,128)S(1)}, f32[256,128]{1,0:T(8,128)S(1)}, bf16[256,768]{1,0:T(8,128)(2,1)S(1)}, bf16[256,1536]{1,0:T(8,128)(2,1)S(1)}, f32[25...) custom-call(s32[5]{0:T(128)S(1)} %stack.23.refs_0_, f32[256,384]{1,0:T(8,128)S(1)} %get-tuple-element.305.refs_1_, ...), custom_call_target="tpu_custom_call" | custom-call | flops 1000000 | bytes 1000 | tf_op jit(solution)/shard_map/feed_1/pallas_call | solution.py:103
  86.5 3.9 %collective-permute-done.6.refs_2_ = f32[256,768]{1,0:T(8,128)S(1)} collective-permute-done((f32[256,768]{1,0:T(8,128)S(1)}, f32[256,768]{1,0:T(8,128)S(1)}, u32[]{:S(2)}, u32[]{:S(2)}) %collective-permute-start.6) | collective-permute-done | bytes 786464 | tf_op jit(solution)/shard_map/ppermute | solution.py:1131
  97.4 9.8 %collective-permute-done.5.refs_2_ = f32[256,768]{1,0:T(8,128)S(1)} collective-permute-done((f32[256,768]{1,0:T(8,128)S(1)}, f32[256,768]{1,0:T(8,128)S(1)}, u32[]{:S(2)}, u32[]{:S(2)}) %collective-permute-start.5) | collective-permute-done | bytes 786464 | tf_op jit(solution)/shard_map/ppermute | solution.py:1131
  117.3 3.6 %collective-permute-done.9.refs_2_ = f32[208,768]{1,0:T(8,128)S(1)} collective-permute-done((f32[208,768]{1,0:T(8,128)S(1)}, f32[208,768]{1,0:T(8,128)S(1)}, u32[]{:S(2)}, u32[]{:S(2)}) %collective-permute-start.9) | collective-permute-done | bytes 639008 | tf_op jit(solution)/shard_map/ppermute | solution.py:1131
  128.2 6.7 %attend_back_2.1 = (f32[208,384]{1,0:T(8,128)S(1)}, f32[768,384]{1,0:T(8,128)S(1)}, f32[768,384]{1,0:T(8,128)S(1)}, f32[128,3072]{1,0:T(8,128)S(1)}, f32[6,128,6...) custom-call(bf16[208,384]{1,0:T(8,128)(2,1)S(1)} %get-tuple-element.362.refs_0_, ...), custom_call_target="tpu_custom_call" | custom-call | flops 1000000 | bytes 1000 | tf_op jit(solution)/shard_map/attend_back_2/pallas_call | solution.py:103
  143.6 3.2 %collective-permute-start.15 = (f32[96,768]{1,0:T(8,128)S(1)}, f32[96,768]{1,0:T(8,128)S(1)}, u32[]{:S(2)}, u32[]{:S(2)}) collective-permute-start(f32[96,768]{1,0:T(8,128)S(1)} %get-tuple-element.410), channel_id=1, source_target_pairs={{0,16},{2,18},{4,20},{6,22},{8,24},{10,26},{12,28},{14,30},{16,0},... | collective-permute-start | bytes 884744 | tf_op jit(solution)/shard_map/ppermute | solution.py:1135
  146.8 8.0 %attend_back_0.1 = (f32[256,384]{1,0:T(8,128)S(1)}, f32[768,384]{1,0:T(8,128)S(1)}, f32[768,384]{1,0:T(8,128)S(1)}, f32[128,3072]{1,0:T(8,128)S(1)}, f32[6,128,6...) custom-call(bf16[256,384]{1,0:T(8,128)(2,1)S(1)} %get-tuple-element., ...), custom_call_target="tpu_custom_call", output_to_operand_aliasing={{1}: (8, {}), {2}: (9, {}), {3}: (10, {}), {4}: (11, {})} | custom-call | flops 1000000 | bytes 1000 | tf_op jit(solution)/shard_map/attend_back_0/pallas_call | solution.py:103
  162.5 7.7 %attend_back_1.1 = (f32[256,384]{1,0:T(8,128)S(1)}, f32[768,384]{1,0:T(8,128)S(1)}, f32[768,384]{1,0:T(8,128)S(1)}, f32[128,3072]{1,0:T(8,128)S(1)}, f32[6,128,640]{2,1,0:T(8,128)S(1)}, /*index=5*/f32[8,128]{1,0:T(8,128)S(1)}) custom-call(bf16[256,384]{1,0:T(8,128)(2,1)S(1)} %get-tuple-element., ...), custom_call_target="tpu_custom_call", output_to_operand_aliasing={{1}: (8, {}), {2}: (9, {}), {3}: (10, {}), {4}: (11, {})} | custom-call | flops 1000000 | bytes 1000 | tf_op jit(solution)/shard_map/attend_back_1/pallas_call | solution.py:103
  171.6 3.2 %attention_grads.1 = (f32[384,1024]{1,0:T(8,128)S(1)}, f32[384,1024]{1,0:T(8,128)S(1)}, f32[384,512]{1,0:T(8,128)S(1)}, f32[384,512]{1,0:T(8,128)S(1)}, f32[8,128]{1,0:T(8,128)S(1)}) custom-call(s32[5]{0:T(128)S(1)} %stack.23.refs_0_, bf16[256,768]{1,0:T(8,128)(2,1)S(1)} %get-tuple-element.423.refs_1_, bf16[256,768]{1,0:T(8,128)(2,1)S(1)} %get-tuple-element.424.refs_2_, ...), custom_call_target="tpu_custom_call" | custom-call | flops 1000000 | bytes 1000 | tf_op jit(solution)/shard_map/attention_grads/pallas_call | solution.py:103
  183.4 3.9 %table_sums.1 = (f32[8,256]{1,0:T(8,128)S(1)}, f32[8,128]{1,0:T(8,128)S(1)}) custom-call(f32[128,3072]{1,0:T(8,128)S(1)} %get-tuple-element.450.refs_0_, f32[6,128,640]{2,1,0:T(8,128)S(1)} %get-tuple-element.451.refs_1_, f32[8,128]{1,0:T(8,128)S(1)} %get-tuple-element.458.refs_2_), custom_call_target="tpu_custom_call" | custom-call | flops 1000000 | bytes 1000 | tf_op jit(solution)/shard_map/table_sums/pallas_call | solution.py:103
  187.3 3.4 %tap_sums.1 = (f32[16,768]{1,0:T(8,128)S(1)}, f32[8,128]{1,0:T(8,128)S(1)}) custom-call(s32[1]{0:T(128)S(6)} %copy.70.refs_0_, bf16[708,768]{1,0:T(8,128)(2,1)S(1)} %bitcast.23, f32[720,768]{1,0:T(8,128)S(1)} %get-tuple-element.446.refs_2_.refs_3_, f32[256,768]{1,0:T(8,128)S(1)} %get-tuple-element.447.refs_3_.refs_5_, ...), custom_call_target="tpu_custom_call" | custom-call | flops 1000000 | bytes 1000 | tf_op jit(solution)/shard_map/tap_sums/pallas_call | solution.py:103
  190.7 11.6 %collective-permute-done.29.refs_2_ = f32[104,768]{1,0:T(8,128)S(1)} collective-permute-done((f32[104,768]{1,0:T(8,128)S(1)}, f32[104,768]{1,0:T(8,128)S(1)}, u32[]{:S(2)}, u32[]{:S(2)}) %collective-permute-start.29) | collective-permute-done | bytes 319520 | tf_op jit(solution)/shard_map/ppermute | solution.py:1135
  207.2 3.4 %collective-permute-done.25.refs_1_ = f32[24,768]{1,0:T(8,128)S(1)} collective-permute-done((f32[24,768]{1,0:T(8,128)S(1)}, f32[24,768]{1,0:T(8,128)S(1)}, u32[]{:S(2)}, u32[]{:S(2)}) %collective-permute-start.25) | collective-permute-done | bytes 73760 | tf_op jit(solution)/shard_map/ppermute | solution.py:1135
  210.7 8.4 %collective-permute-done.32.refs_2_ = f32[96,1024]{1,0:T(8,128)S(1)} collective-permute-done((f32[96,1024]{1,0:T(8,128)S(1)}, f32[96,1024]{1,0:T(8,128)S(1)}, u32[]{:S(2)}, u32[]{:S(2)}) %collective-permute-start.32) | collective-permute-done | bytes 393248 | tf_op jit(solution)/shard_map/ppermute | solution.py:1135
  224.3 4.5 %collective-permute-done.30.refs_1_ = f32[24,768]{1,0:T(8,128)S(1)} collective-permute-done((f32[24,768]{1,0:T(8,128)S(1)}, f32[24,768]{1,0:T(8,128)S(1)}, u32[]{:S(2)}, u32[]{:S(2)}) %collective-permute-start.30) | collective-permute-done | bytes 73760 | tf_op jit(solution)/shard_map/ppermute | solution.py:1135
  231.5 5.4 %decode.1 = (bf16[708,768]{1,0:T(8,128)(2,1)}, f32[8,128]{1,0:T(8,128)S(1)}) custom-call(s32[1]{0:T(128)S(6)} %copy.70.refs_0_, bf16[3,3,768]{2,1,0:T(4,128)(2,1)S(1)} %copy-done.7, bf16[9,768]{1,0:T(8,128)(2,1)S(1)} %copy-done.6, f32[720,768]{1,0:T(8,128)S(1)} %get-tuple-element.446.refs_2_.refs_3_, f32[720,768]{1,0:T(8,128)S(1)} %collective-permute-done.22.refs_4_, ...), custom_call_target="tpu_custom_call" | custom-call | flops 1000000 | bytes 1000 | tf_op jit(solution)/shard_map/decode/pallas_call | solution.py:103
  (175 shorter events, 96.9 us)
Async XLA Ops:
  6.5 19.1 %collective-permute-start = (f32[192,768]{1,0:T(8,128)S(1)}, f32[192,768]{1,0:T(8,128)S(1)}, u32[]{:S(2)}, u32[]{:S(2)}) collective-permute-start(f32[192,768]{1,0:T(8,128)S(1)} %get-tuple-element.295), channel_id=1, source_target_pairs={{0,1},{1,0},{2,3},{3,2},{4,5},{5,4},{6,7},{7,6},{8,9},{9,8},{10,11... | collective-permute-start | bytes 1769480 | tf_op jit(solution)/shard_map/ppermute | solution.py:1131
  39.3 38.0 %collective-permute-start.7 = (f32[208,768]{1,0:T(8,128)S(1)}, f32[208,768]{1,0:T(8,128)S(1)}, u32[]{:S(2)}, u32[]{:S(2)}) collective-permute-start(f32[208,768]{1,0:T(8,128)S(1)} %get-tuple-element.319.refs_1_), channel_id=1, source_target_pairs={{0,1},{1,0},{2,3},{3,2},{4,5},{5,4},{6,7},{7,6},{8,9},{9,8},{10,11... | collective-permute-start | bytes 1916936 | tf_op jit(solution)/shard_map/ppermute | solution.py:1131
  39.6 25.5 %collective-permute-start.4 = (f32[256,384]{1,0:T(8,128)S(1)}, f32[256,384]{1,0:T(8,128)S(1)}, u32[]{:S(2)}, u32[]{:S(2)}) collective-permute-start(f32[256,384]{1,0:T(8,128)S(1)} %get-tuple-element.307.refs_1_), channel_id=1, source_target_pairs={{0,1},{1,0},{2,3},{3,2},{4,5},{5,4},{6,7},{7,6},{8,9},{9,8},{10,11... | collective-permute-start | bytes 1179656 | tf_op jit(solution)/shard_map/ppermute | solution.py:1131
  49.1 24.4 %collective-permute-start.3 = (f32[256,384]{1,0:T(8,128)S(1)}, f32[256,384]{1,0:T(8,128)S(1)}, u32[]{:S(2)}, u32[]{:S(2)}) collective-permute-start(f32[256,384]{1,0:T(8,128)S(1)} %get-tuple-element.305.refs_1_), channel_id=1, source_target_pairs={{0,1},{1,0},{2,3},{3,2},{4,5},{5,4},{6,7},{7,6},{8,9},{9,8},{10,11... | collective-permute-start | bytes 1179656 | tf_op jit(solution)/shard_map/ppermute | solution.py:1131
  68.8 21.5 %collective-permute-start.6 = (f32[256,768]{1,0:T(8,128)S(1)}, f32[256,768]{1,0:T(8,128)S(1)}, u32[]{:S(2)}, u32[]{:S(2)}) collective-permute-start(f32[256,768]{1,0:T(8,128)S(1)} %get-tuple-element.316.refs_1_), channel_id=1, source_target_pairs={{0,1},{1,0},{2,3},{3,2},{4,5},{5,4},{6,7},{7,6},{8,9},{9,8},{10,11... | collective-permute-start | bytes 2359304 | tf_op jit(solution)/shard_map/ppermute | solution.py:1131
  77.0 30.2 %collective-permute-start.5 = (f32[256,768]{1,0:T(8,128)S(1)}, f32[256,768]{1,0:T(8,128)S(1)}, u32[]{:S(2)}, u32[]{:S(2)}) collective-permute-start(f32[256,768]{1,0:T(8,128)S(1)} %get-tuple-element.313.refs_1_), channel_id=1, source_target_pairs={{0,1},{1,0},{2,3},{3,2},{4,5},{5,4},{6,7},{7,6},{8,9},{9,8},{10,11... | collective-permute-start | bytes 2359304 | tf_op jit(solution)/shard_map/ppermute | solution.py:1131
  80.4 40.5 %collective-permute-start.9 = (f32[208,768]{1,0:T(8,128)S(1)}, f32[208,768]{1,0:T(8,128)S(1)}, u32[]{:S(2)}, u32[]{:S(2)}) collective-permute-start(f32[208,768]{1,0:T(8,128)S(1)} %get-tuple-element.346.refs_1_), channel_id=1, source_target_pairs={{0,1},{1,0},{2,3},{3,2},{4,5},{5,4},{6,7},{7,6},{8,9},{9,8},{10,11... | collective-permute-start | bytes 1916936 | tf_op jit(solution)/shard_map/ppermute | solution.py:1131
  115.0 22.8 %collective-permute-start.8 = (f32[256,768]{1,0:T(8,128)S(1)}, f32[256,768]{1,0:T(8,128)S(1)}, u32[]{:S(2)}, u32[]{:S(2)}) collective-permute-start(f32[256,768]{1,0:T(8,128)S(1)} %get-tuple-element.343.refs_1_), channel_id=1, source_target_pairs={{0,1},{1,0},{2,3},{3,2},{4,5},{5,4},{6,7},{7,6},{8,9},{9,8},{10,11... | collective-permute-start | bytes 2359304 | tf_op jit(solution)/shard_map/ppermute | solution.py:1131
  115.2 39.7 %collective-permute-start.14 = (f32[256,768]{1,0:T(8,128)S(1)}, f32[256,768]{1,0:T(8,128)S(1)}, u32[]{:S(2)}, u32[]{:S(2)}) collective-permute-start(f32[256,768]{1,0:T(8,128)S(1)} %get-tuple-element.399.refs_1_), channel_id=1, source_target_pairs={{0,1},{1,0},{2,3},{3,2},{4,5},{5,4},{6,7},{7,6},{8,9},{9,8},{10,11... | collective-permute-start | bytes 2359304 | tf_op jit(solution)/shard_map/ppermute | solution.py:1131
  123.3 17.7 %collective-permute-start.13 = (f32[192,768]{1,0:T(8,128)S(1)}, f32[192,768]{1,0:T(8,128)S(1)}, u32[]{:S(2)}, u32[]{:S(2)}) collective-permute-start(f32[192,768]{1,0:T(8,128)S(1)} %get-tuple-element.391), channel_id=1, source_target_pairs={{0,4},{2,6},{4,0},{6,2},{8,12},{10,14},{12,8},{14,10},{16,20},{18,... | collective-permute-start | bytes 1769480 | tf_op jit(solution)/shard_map/ppermute | solution.py:1135
  125.7 17.1 %collective-permute-start.12 = (f32[192,768]{1,0:T(8,128)S(1)}, f32[192,768]{1,0:T(8,128)S(1)}, u32[]{:S(2)}, u32[]{:S(2)}) collective-permute-start(f32[192,768]{1,0:T(8,128)S(1)} %get-tuple-element.389), channel_id=1, source_target_pairs={{0,8},{2,10},{4,12},{6,14},{8,0},{10,2},{12,4},{14,6},{16,24},{18,... | collective-permute-start | bytes 1769480 | tf_op jit(solution)/shard_map/ppermute | solution.py:1135
  127.7 28.2 %collective-permute-start.17 = (f32[192,768]{1,0:T(8,128)S(1)}, f32[192,768]{1,0:T(8,128)S(1)}, u32[]{:S(2)}, u32[]{:S(2)}) collective-permute-start(f32[192,768]{1,0:T(8,128)S(1)} %get-tuple-element.414), channel_id=1, source_target_pairs={{0,4},{2,6},{4,0},{6,2},{8,12},{10,14},{12,8},{14,10},{16,20},{18,... | collective-permute-start | bytes 1769480 | tf_op jit(solution)/shard_map/ppermute | solution.py:1135
  139.5 30.8 %collective-permute-start.19 = (f32[200,768]{1,0:T(8,128)S(1)}, f32[200,768]{1,0:T(8,128)S(1)}, u32[]{:S(2)}, u32[]{:S(2)}) collective-permute-start(f32[200,768]{1,0:T(8,128)S(1)} %get-tuple-element.435), channel_id=1, source_target_pairs={{0,4},{2,6},{4,0},{6,2},{8,12},{10,14},{12,8},{14,10},{16,20},{18,... | collective-permute-start | bytes 1843208 | tf_op jit(solution)/shard_map/ppermute | solution.py:1135
  141.8 15.1 %collective-permute-start.16 = (f32[96,768]{1,0:T(8,128)S(1)}, f32[96,768]{1,0:T(8,128)S(1)}, u32[]{:S(2)}, u32[]{:S(2)}) collective-permute-start(f32[96,768]{1,0:T(8,128)S(1)} %get-tuple-element.412), channel_id=1, source_target_pairs={{0,8},{2,10},{4,12},{6,14},{8,0},{10,2},{12,4},{14,6},{16,24},{18,... | collective-permute-start | bytes 884744 | tf_op jit(solution)/shard_map/ppermute | solution.py:1135
  177.4 54.1 %collective-permute-start.22 = (f32[720,768]{1,0:T(8,128)S(1)}, f32[720,768]{1,0:T(8,128)S(1)}, u32[]{:S(2)}, u32[]{:S(2)}) collective-permute-start(f32[720,768]{1,0:T(8,128)S(1)} %get-tuple-element.446.refs_2_.refs_3_), channel_id=1, source_target_pairs={{0,1},{1,0},{2,3},{3,2},{4,5},{5,4},{6,7},{7,6},{8,9},{9,8},{10,11... | collective-permute-start | bytes 6635528 | tf_op jit(solution)/shard_map/ppermute | solution.py:1131
  179.6 24.0 %collective-permute-start.26 = (f32[192,1024]{1,0:T(8,128)S(1)}, f32[192,1024]{1,0:T(8,128)S(1)}, u32[]{:S(2)}, u32[]{:S(2)}) collective-permute-start(f32[192,1024]{1,0:T(8,128)S(1)} %get-tuple-element.469), channel_id=1, source_target_pairs={{0,4},{2,6},{4,0},{6,2},{8,12},{10,14},{12,8},{14,10},{16,20},{18,... | collective-permute-start | bytes 2359304 | tf_op jit(solution)/shard_map/ppermute | solution.py:1135
  181.0 21.9 %collective-permute-start.27 = (f32[192,512]{1,0:T(8,128)S(1)}, f32[192,512]{1,0:T(8,128)S(1)}, u32[]{:S(2)}, u32[]{:S(2)}) collective-permute-start(f32[192,512]{1,0:T(8,128)S(1)} %get-tuple-element.471), channel_id=1, source_target_pairs={{0,8},{2,10},{4,12},{6,14},{8,0},{10,2},{12,4},{14,6},{16,24},{18,... | collective-permute-start | bytes 1179656 | tf_op jit(solution)/shard_map/ppermute | solution.py:1135
  181.2 21.1 %collective-permute-start.29 = (f32[104,768]{1,0:T(8,128)S(1)}, f32[104,768]{1,0:T(8,128)S(1)}, u32[]{:S(2)}, u32[]{:S(2)}) collective-permute-start(f32[104,768]{1,0:T(8,128)S(1)} %get-tuple-element.475), channel_id=1, source_target_pairs={{0,8},{2,10},{4,12},{6,14},{8,0},{10,2},{12,4},{14,6},{16,24},{18,... | collective-permute-start | bytes 958472 | tf_op jit(solution)/shard_map/ppermute | solution.py:1135
  183.1 19.8 %collective-permute-start.28 = (f32[48,768]{1,0:T(8,128)S(1)}, f32[48,768]{1,0:T(8,128)S(1)}, u32[]{:S(2)}, u32[]{:S(2)}) collective-permute-start(f32[48,768]{1,0:T(8,128)S(1)} %get-tuple-element.473), channel_id=1, source_target_pairs={{0,16},{2,18},{4,20},{6,22},{8,24},{10,26},{12,28},{14,30},{16,0},... | collective-permute-start | bytes 442376 | tf_op jit(solution)/shard_map/ppermute | solution.py:1135
  204.4 14.7 %collective-permute-start.32 = (f32[96,1024]{1,0:T(8,128)S(1)}, f32[96,1024]{1,0:T(8,128)S(1)}, u32[]{:S(2)}, u32[]{:S(2)}) collective-permute-start(f32[96,1024]{1,0:T(8,128)S(1)} %get-tuple-element.485), channel_id=1, source_target_pairs={{0,8},{2,10},{4,12},{6,14},{8,0},{10,2},{12,4},{14,6},{16,24},{18,... | collective-permute-start | bytes 1179656 | tf_op jit(solution)/shard_map/ppermute | solution.py:1135
  204.5 18.3 %collective-permute-start.31 = (f32[96,512]{1,0:T(8,128)S(1)}, f32[96,512]{1,0:T(8,128)S(1)}, u32[]{:S(2)}, u32[]{:S(2)}) collective-permute-start(f32[96,512]{1,0:T(8,128)S(1)} %get-tuple-element.483), channel_id=1, source_target_pairs={{0,16},{2,18},{4,20},{6,22},{8,24},{10,26},{12,28},{14,30},{16,0},... | collective-permute-start | bytes 589832 | tf_op jit(solution)/shard_map/ppermute | solution.py:1135
  219.8 20.5 %collective-permute-start.33 = (f32[48,1024]{1,0:T(8,128)S(1)}, f32[48,1024]{1,0:T(8,128)S(1)}, u32[]{:S(2)}, u32[]{:S(2)}) collective-permute-start(f32[48,1024]{1,0:T(8,128)S(1)} %get-tuple-element.492), channel_id=1, source_target_pairs={{0,16},{2,18},{4,20},{6,22},{8,24},{10,26},{12,28},{14,30},{16,0},... | collective-permute-start | bytes 589832 | tf_op jit(solution)/shard_map/ppermute | solution.py:1135
  219.9 18.9 %collective-permute-start.35 = (f32[56,768]{1,0:T(8,128)S(1)}, f32[56,768]{1,0:T(8,128)S(1)}, u32[]{:S(2)}, u32[]{:S(2)}) collective-permute-start(f32[56,768]{1,0:T(8,128)S(1)} %get-tuple-element.496), channel_id=1, source_target_pairs={{0,16},{2,18},{4,20},{6,22},{8,24},{10,26},{12,28},{14,30},{16,0},... | collective-permute-start | bytes 516104 | tf_op jit(solution)/shard_map/ppermute | solution.py:1135
  223.4 16.9 %collective-permute-start.34 = (f32[48,512]{1,0:T(8,128)S(1)}, f32[48,512]{1,0:T(8,128)S(1)}, u32[]{:S(2)}, u32[]{:S(2)}) collective-permute-start(f32[48,512]{1,0:T(8,128)S(1)} %get-tuple-element.494), channel_id=1, source_target_pairs={{0,4},{2,6},{4,0},{6,2},{8,12},{10,14},{12,8},{14,10},{16,20},{18,... | collective-permute-start | bytes 294920 | tf_op jit(solution)/shard_map/ppermute | solution.py:1135
  (39 other events, 303.0 us)

commit v3 on v2

--- a/solution.py
+++ b/solution.py
@@ -606,7 +606,6 @@
         [block] + [vmem()] * 5,
         grid=(1,),
         input_output_aliases=aliases,
-        us=15000 if c == ORDER[0] else 1,
         name=f"feed_back_{c}",
     )
 
@@ -667,7 +666,7 @@
     )
 
 
-SPLIT = 1024
+SPLIT = 768
 
 
 def attention_grads_kernel(slab, where_ref, *refs):
@@ -953,20 +952,11 @@
 
 
 def project_back_kernel(
-    q0, q1, q2, dk_ref, dv_ref, wq_hbm, wk_hbm, wv_hbm, part_ref, bias_ref,
-    wq_ref, wk_ref, wv_ref, sems,
+    q0, q1, q2, dk_ref, dv_ref, wq_ref, wk_ref, wv_ref, part_ref, bias_ref,
 ):
-    copies = [
-        pltpu.make_async_copy(src, dst, sems.at[i])
-        for i, (src, dst) in enumerate(
-            zip((wq_hbm, wk_hbm, wv_hbm), (wq_ref, wk_ref, wv_ref))
-        )
-    ]
-    for copy in copies:
-        copy.start()
     sum_q = None
     sum_v = None
-    for i, ((start, rows), dq) in enumerate(zip(CHUNKS, (q0, q1, q2))):
+    for (start, rows), dq in zip(CHUNKS, (q0, q1, q2)):
         query = dq[...]
         value = dv_ref[start : start + rows, :]
         sum_q = col_sum(query) if sum_q is None else sum_q + col_sum(query)
@@ -974,9 +964,6 @@
         query = query.astype(BF16)
         key = dk_ref[start : start + rows, :].astype(BF16)
         value = value.astype(BF16)
-        if i == 0:
-            for copy in copies:
-                copy.wait()
         part_ref[start : start + rows, :] = (
             dot_nt(query, wq_ref[...]) + dot_nt(key, wk_ref[...]) + dot_nt(value, wv_ref[...])
         )
@@ -989,10 +976,9 @@
     return order(
         project_back_kernel,
         (*dq, dk, dv, wq, wk, wv),
-        [vmem()] * 5 + [hbm()] * 3,
+        [vmem()] * 8,
         (sds((ROWS, D), F32), sds((8, D), F32)),
         [vmem()] * 2,
-        scratch_shapes=[pltpu.VMEM((D, DL), BF16)] * 3 + [pltpu.SemaphoreType.DMA((3,))],
         us=15000,
         name="project_back",
     )
@@ -1178,7 +1164,11 @@
 
 
 def total_of(order, part, name):
-    pair = part.pair
+    return add_blocks(order, *part.pair, name)
+
+
+def add_blocks(order, *pair_name):
+    *pair, name = pair_name
     shapes = (sds(pair[0].shape, F32),)
     return order(
         add_kernel, pair, whole_blocks(pair), shapes, whole_blocks(shapes), grid=(1,), name=name
@@ -1195,29 +1185,50 @@
     )[0]
 
 
+def joint_kernel(where_ref, sum_ref, a_ref, b_ref, own_ref, out_ref):
+    mine = where_ref[4]
+    slab = a_ref.shape[0] // 2
+    width = a_ref.shape[1]
+    for ref, which in ((own_ref, mine), (out_ref, 1 - mine)):
+        rows = pl.ds(pl.multiple_of(which * slab, 8), slab)
+        ref[0:slab, 0:D] = sum_ref[rows, :]
+        ref[0:slab, D : D + width] = a_ref[rows, :] + b_ref[rows, :]
+        ref[slab:, 0:D] = sum_ref[2 * slab :, :]
+        ref[slab:, D : D + width] = jnp.zeros((EARLY, width), F32)
+
+
+def joint_step(order, dp, where, summed, part):
+    rows, width = part.pair[0].shape
+    shapes = (sds((rows // 2 + EARLY, D + width), F32),) * 2
+    operands = (summed, *part.pair)
+    own, out = order(
+        joint_kernel, (where, *operands), [smem()] + whole_blocks(operands), shapes,
+        whole_blocks(shapes), grid=(1,), name="joint_3",
+    )
+    return own, swap_dp(out, 8, dp)
+
+
 def last_totals_kernel(
-    a0, a1, b0, b1, oa, ob, ia, ib, late, late_other,
-    q_ref, k_ref, v_ref, o_ref, outer_ref, inner_ref, small_ref,
+    both, b0, b1, joint, ob, ia, q_ref, k_ref, v_ref, o_ref, outer_ref, inner_ref, small_ref,
 ):
     slab = q_ref.shape[0]
-    both = a0[...] + a1[...]
     q_ref[...] = both[0:slab, 0:DL]
     k_ref[...] = both[0:slab, DL:D]
-    v_ref[:, 0 : SPLIT - D] = both[0:slab, D:SPLIT]
-    small_ref[0:LATE, :] = late[...] + late_other[...]
     both = b0[...] + b1[...]
-    v_ref[:, SPLIT - D : DL] = both[:, 0 : D + DL - SPLIT]
-    o_ref[...] = both[:, D + DL - SPLIT :]
-    outer_ref[:, 0:D] = oa[0:slab, :]
-    outer_ref[:, D:FL] = ob[...]
+    v_ref[...] = both[0:slab, 0:DL]
+    o_ref[...] = both[0:slab, DL:D]
+    small_ref[0:LATE, :] = both[slab:, 0:D]
+    split = joint.shape[1] - D
+    outer_ref[:, 0:split] = joint[0:slab, D : D + split]
+    outer_ref[:, split:FL] = ob[...]
     inner_ref[:, 0:D] = ia[...]
-    inner_ref[:, D:FL] = ib[...]
-    small_ref[LATE : LATE + EARLY, :] = oa[slab:, :]
-
-
-def last_totals(order, part_a, part_b, *rest):
+    inner_ref[:, D:FL] = joint[0:slab, 0:D]
+    small_ref[LATE : LATE + EARLY, :] = joint[slab:, 0:D]
+
+
+def last_totals(order, total_a, part_b, *rest):
     *rest, slab = rest
-    operands = [*part_a.pair, *part_b.pair, *rest]
+    operands = [total_a, *part_b.pair, *rest]
     plain = sds((slab, DL), F32)
     wide = sds((slab, FL), F32)
     shapes = (plain,) * 4 + (wide, wide, sds((LATE + EARLY, D), F32))
@@ -1384,14 +1395,15 @@
         outer_other[c] = swap_tensor(got[5])
         return far
 
-    near, far = attention_of(ORDER[0], (*enc, *enc_low, q0, q1, q2, k, v))
-    enc, enc_low, q_far, k_far, v_far = far[0:3], far[3:6], far[6:9], far[9], far[10]
+    near, enc = attention_of(ORDER[0], enc)
     wo_a = pass_on(order, wo_a)
     wo_b = swap_dp(wo_a, 1, dp)
-    near, (probs[ORDER[0]], mix_low[ORDER[0]]) = attention_of(ORDER[1], near)
-    feed_of(ORDER[0])
+    near, far = attention_of(ORDER[1], (*near, *enc_low, q0, q1, q2, k, v))
+    probs[ORDER[0]], mix_low[ORDER[0]], *far = far
+    enc_low, q_far, k_far, v_far = far[0:3], far[3:6], far[6], far[7]
     near, (probs[ORDER[1]], mix_low[ORDER[1]]) = attention_of(ORDER[2], near)
-    probs[ORDER[2]], mix_low[ORDER[2]] = feed_of(ORDER[1], near)
+    probs[ORDER[2]], mix_low[ORDER[2]] = feed_of(ORDER[0], near)
+    feed_of(ORDER[1])
     feed_of(ORDER[2])
     layer_out, inner_grad, outer_grad = None, None, None
     dres2, g2, g1, dhid, dhid_other, sums2 = ([None] * 3 for _ in range(6))
@@ -1431,9 +1443,9 @@
         if c == ORDER[0]:
             inner.step()
             outer_b.step()
-            inner_b.step()
+            inner_b.step(early)
         if c == ORDER[1]:
-            outer_a.step(early)
+            outer_a.step()
             inner.step()
             outer_b.step()
         if c == ORDER[2]:
@@ -1441,18 +1453,22 @@
             inner.step()
             outer_b.step()
         into = [probs[after] for after in ORDER[ORDER.index(c) + 1 :][:1]]
+        if not into:
+            into = [query_weight, key_weight, value_weight]
         got = attend_back(
             order, c, got[2], prob, q_far[c], k_far, v_far, ur_far, r_far, o_far, carry, into
         )
-        if into:
-            got, (prob,) = got
+        got, into = got
+        prob = into[0]
         dq[c], *carry = got
+    weights = into
     dk, dv, dm, dz = carry
     if dp == 16:
         total_outer_b = total_of(order, outer_b, "outer_b_total")
         total_inner = total_of(order, inner, "inner_total")
     outer_a.step()
-    inner_b.step()
+    if dp == 16:
+        inner_b = total_of(order, inner_b, "inner_b_sum")
     operands = (enc_low, dq, dk, dv, g0, mix_low)
     if dp == 16:
         got = attention_grads(order, slab, where, *operands)
@@ -1461,34 +1477,28 @@
         first_pair = second_pair = plain_grads(order, *operands)
     rest = 0 if dp == 16 else SPLIT
     part_a = scatter(first_pair, x_first, "part_a", 0, SPLIT)
-    part_b = scatter(second_pair, z_first, "part_b", rest, 4 * DL - SPLIT)
-    part, bias_sums = project_back(order, dq, dk, dv, query_weight, key_weight, value_weight)
+    part_b = scatter(second_pair, x_first, "part_b", rest, 4 * DL - SPLIT)
+    part, bias_sums = project_back(order, dq, dk, dv, *weights)
     part_other = swap_tensor(part)
     part_a.step()
-    part_b.step()
     tables = table_sums(order, dm, dz)
     taps = tap_sums(order, patch_counts, x, part, dres1)
     late = gather_late(order, taps, *sums1, bias_sums, tables)
-    late_other = swap_dp(late, 2, dp)
-    outer_a.step()
     if dp == 16:
-        total_inner_b = total_of(order, inner_b, "inner_b_total")
-    part_b.step()
+        joint = joint_step(order, dp, where, inner_b, outer_a)
+    part_b.step(late)
     part_a.step()
     if dp == 16:
-        late = add_here(order, late, late_other, "late_2")
-        late_other = swap_dp(late, 4, dp)
+        joint = add_blocks(order, *joint, "joint_total")
     part_a.step()
     part_b.step()
     if dp == 16:
-        late = add_here(order, late, late_other, "late_4")
-        late_other = swap_dp(late, 8, dp)
+        total_a = total_of(order, part_a, "part_a_total")
+    part_b.step()
     input_grad = decode(order, patch_counts, text_weight, patch_weight, part, part_other, dres1)
     if dp == 16:
-        total_outer_a = total_of(order, outer_a, "outer_a_total")
         grad_q, grad_k, grad_v, grad_o, sum_outer, inner_total, small = last_totals(
-            order, part_a, part_b, total_outer_a, total_outer_b, total_inner, total_inner_b,
-            late, late_other, slab,
+            order, total_a, part_b, joint, total_outer_b, total_inner, slab
         )
     else:
         inner_total = jnp.concatenate([inner.total(), inner_b.total()], axis=1)
@@ -1500,9 +1510,11 @@
         while bit < dp:
             small = small + swap_dp(small, bit, dp)
             bit *= 2
+    small_others = (
+        swap_dp(small, 1, dp), swap_tensor(small[0:16]), swap_both(small[0:16], dp)
+    )
     small = finish(
-        order, jnp.reshape(place, (1,)).astype(jnp.int32), small, swap_dp(small, 1, dp),
-        swap_tensor(small[0:16]), swap_both(small[0:16], dp), D // dp,
+        order, jnp.reshape(place, (1,)).astype(jnp.int32), small, *small_others, D // dp
     )
     text, patch, out_b, gain1, shift1, outer_b, gain2, shift2 = small[:8]
     query_b, value_b, inner_b, line, width, height = small[8:]

time: 252 us -> 241 us (0.956)
  waiting for transfers between devices: 77.2 us -> 64.6 us
    ppermute x27 -> x23, waiting for transfers between devices: 32 us -> 25.3 us  [swap_dp(): return lax.ppermute(x, 'dp', [(i, i ^ bit) for i in range(dp)])]
    ppermute x12, waiting for transfers between devices: 44.2 us -> 38.7 us  [swap_tensor(): return lax.ppermute(x, 'tensor', [(0, 1), (1, 0)])]
    ppermute x27 -> x23, starting transfers between devices: 26 us -> 24.2 us  [swap_dp(): return lax.ppermute(x, 'dp', [(i, i ^ bit) for i in range(dp)])]
    pallas_call x57 -> x55, Pallas kernels: 126 us -> 128 us  [__call__(): pl.pallas_call(body, out_shape=tuple(out_shape) + tuple(shapes) + (TOKEN,...]
  transfers between devices with their start and end apart: 40 -> 36, of which waited for: 16 -> 16; matrix products, arithmetic and copies ran while one was open for 0% -> 0% of each run, Pallas kernels for 46% -> 51%
where the time goes in v3:
time: 241 us; the launch traced here: 237 us
  Pallas kernels  128 us (53%)
  waiting for transfers between devices  64.6 us (27%)
  starting transfers between devices  38.6 us (16%)
  between operations  2.44 us (1%)
    pallas_call x55, Pallas kernels, __call__(): pl.pallas_call(body, out_shape=tuple(out_shape) + tuple(shapes) + (TOKEN,...  128 us
    ppermute x12, waiting for transfers between devices, swap_tensor(): return lax.ppermute(x, 'tensor', [(0, 1), (1, 0)])  38.7 us
    ppermute x23, waiting for transfers between devices, swap_dp(): return lax.ppermute(x, 'dp', [(i, i ^ bit) for i in range(dp)])  25.3 us
    ppermute x23, starting transfers between devices, swap_dp(): return lax.ppermute(x, 'dp', [(i, i ^ bit) for i in range(dp)])  24.2 us
    ppermute x12, starting transfers between devices, swap_tensor(): return lax.ppermute(x, 'tensor', [(0, 1), (1, 0)])  13.7 us
  transfers between devices with their start and end apart: 36, of which 16 were waited for; matrix products, arithmetic and copies ran while one was open for 0% of the time, Pallas kernels for 51%

profile of v3, /device:TPU:0, one launch (start us, length us, event | category | flops | bytes accessed | tf_op | source)
XLA Modules:
  0.0 236.5 jit_solution(11226390906036277230)
XLA Ops:
  3.4 3.1 %bias_tables.1 = (f32[6,128,640]{2,1,0:T(8,128)S(1)}, bf16[128,3072]{1,0:T(8,128)(2,1)S(1)}, bf16[1024,768]{1,0:T(8,128)(2,1)S(1)}, bf16[720,128]{1,0:T(8,128)(2...) custom-call(s32[5]{0:T(128)S(1)} %stack.23.refs_0_, ...), custom_call_target="tpu_custom_call" | custom-call | flops 20000000000 | bytes 20000000 | tf_op jit(solution)/shard_map/bias_tables/pallas_call | solution.py:103
  6.5 3.0 %collective-permute-start = (f32[192,768]{1,0:T(8,128)S(1)}, f32[192,768]{1,0:T(8,128)S(1)}, u32[]{:S(2)}, u32[]{:S(2)}) collective-permute-start(f32[192,768]{1,0:T(8,128)S(1)} %get-tuple-element.293), channel_id=1, source_target_pairs={{0,1},{1,0},{2,3},{3,2},{4,5},{5,4},{6,7},{7,6},{8,9},{9,8},{10,11... | collective-permute-start | bytes 1769480 | tf_op jit(solution)/shard_map/ppermute | solution.py:1117
  10.3 6.4 %encode_project.1 = (bf16[256,384]{1,0:T(8,128)(2,1)S(1)}, bf16[256,384]{1,0:T(8,128)(2,1)S(1)}, bf16[208,384]{1,0:T(8,128)(2,1)S(1)}, bf16[768,384]{1,0:T(8,128...) custom-call(s32[1]{0:T(128)S(6)} %copy.70.refs_0_, ...), custom_call_target="tpu_custom_call" | custom-call | flops 8000000000 | bytes 8000000 | tf_op jit(solution)/shard_map/encode_project/pallas_call | solution.py:103
  16.7 7.1 %attend_2.1 = (bf16[6,208,768]{2,1,0:T(8,128)(2,1)S(1)}, f32[208,384]{1,0:T(8,128)S(1)}, bf16[208,384]{1,0:T(8,128)(2,1)S(1)}, f32[256,768]{1,0:T(8,128)S(1)}, f...) custom-call(s32[1]{0:T(128)S(6)} %copy.70.refs_0_, ...), custom_call_target="tpu_custom_call" | custom-call | flops 1000000 | bytes 1000 | tf_op jit(solution)/shard_map/attend_2/pallas_call | solution.py:103
  25.0 9.3 %attend_0.1 = (bf16[6,256,768]{2,1,0:T(8,128)(2,1)S(1)}, f32[256,384]{1,0:T(8,128)S(1)}, bf16[256,384]{1,0:T(8,128)(2,1)S(1)}, bf16[6,208,768]{2,1,0:T(8,128)(2,...) custom-call(s32[1]{0:T(128)S(6)} %copy.70.refs_0_, ...), custom_call_target="tpu_custom_call" | custom-call | flops 1000000 | bytes 1000 | tf_op jit(solution)/shard_map/attend_0/pallas_call | solution.py:103
  35.8 7.9 %attend_1.1 = (bf16[6,256,768]{2,1,0:T(8,128)(2,1)S(1)}, f32[256,384]{1,0:T(8,128)S(1)}, bf16[256,384]{1,0:T(8,128)(2,1)S(1)}, bf16[6,256,768]{2,1,0:T(8,128)(2,...) custom-call(s32[1]{0:T(128)S(6)} %copy.70.refs_0_, bf16[256,384]{1,0:T(8,128)(2,1)S(1)} %get-tuple-element.276.refs_15_.refs_1_, ...), custom_call_target="tpu_custom_call" | custom-call | flops 1000000 | bytes 1000 | tf_op jit(solution)/shard_map/attend_1/pallas_call | solution.py:103
  44.8 3.6 %feed_2.1 = (f32[208,768]{1,0:T(8,128)S(1)}, f32[208,128]{1,0:T(8,128)S(1)}, bf16[208,768]{1,0:T(8,128)(2,1)S(1)}, bf16[208,1536]{1,0:T(8,128)(2,1)S(1)}, f32[20...) custom-call(s32[5]{0:T(128)S(1)} %stack.23.refs_0_, ...), custom_call_target="tpu_custom_call" | custom-call | flops 1000000 | bytes 1000 | tf_op jit(solution)/shard_map/feed_2/pallas_call | solution.py:103
  49.7 3.3 %feed_0.1 = (f32[256,768]{1,0:T(8,128)S(1)}, f32[256,128]{1,0:T(8,128)S(1)}, bf16[256,768]{1,0:T(8,128)(2,1)S(1)}, bf16[256,1536]{1,0:T(8,128)(2,1)S(1)}, f32[25...) custom-call(s32[5]{0:T(128)S(1)} %stack.23.refs_0_, f32[256,384]{1,0:T(8,128)S(1)} %get-tuple-element.302.refs_1_, ...), custom_call_target="tpu_custom_call" | custom-call | flops 1000000 | bytes 1000 | tf_op jit(solution)/shard_map/feed_0/pallas_call | solution.py:103
  55.8 3.5 %feed_1.1 = (f32[256,768]{1,0:T(8,128)S(1)}, f32[256,128]{1,0:T(8,128)S(1)}, bf16[256,768]{1,0:T(8,128)(2,1)S(1)}, bf16[256,1536]{1,0:T(8,128)(2,1)S(1)}, f32[25...) custom-call(s32[5]{0:T(128)S(1)} %stack.23.refs_0_, f32[256,384]{1,0:T(8,128)S(1)} %get-tuple-element.299.refs_1_, ...), custom_call_target="tpu_custom_call" | custom-call | flops 1000000 | bytes 1000 | tf_op jit(solution)/shard_map/feed_1/pallas_call | solution.py:103
  60.1 9.3 %collective-permute-done.7.refs_2_ = f32[208,768]{1,0:T(8,128)S(1)} collective-permute-done((f32[208,768]{1,0:T(8,128)S(1)}, f32[208,768]{1,0:T(8,128)S(1)}, u32[]{:S(2)}, u32[]{:S(2)}) %collective-permute-start.7) | collective-permute-done | bytes 639008 | tf_op jit(solution)/shard_map/ppermute | solution.py:1117
  69.4 3.3 %feed_back_2.1 = (bf16[708,768]{1,0:T(8,128)(2,1)}, f32[208,768]{1,0:T(8,128)S(1)}, bf16[208,768]{1,0:T(8,128)(2,1)S(1)}, bf16[208,1536]{1,0:T(8,128)(2,1)S(1)},...) custom-call(s32[1]{0:T(128)S(6)} %copy.70.refs_0_, f32[208,768]{1,0:T(8,128)S(1)} %get-tuple-element.317.refs_1_, ...), custom_call_target="tpu_custom_call" | custom-call | flops 1000000 | bytes 1000 | tf_op jit(solution)/shard_map/feed_back_2/pallas_call | solution.py:103
  77.8 8.5 %collective-permute-done.6.refs_2_ = f32[256,768]{1,0:T(8,128)S(1)} collective-permute-done((f32[256,768]{1,0:T(8,128)S(1)}, f32[256,768]{1,0:T(8,128)S(1)}, u32[]{:S(2)}, u32[]{:S(2)}) %collective-permute-start.6) | collective-permute-done | bytes 786464 | tf_op jit(solution)/shard_map/ppermute | solution.py:1117
  93.4 9.8 %collective-permute-done.5.refs_2_ = f32[256,768]{1,0:T(8,128)S(1)} collective-permute-done((f32[256,768]{1,0:T(8,128)S(1)}, f32[256,768]{1,0:T(8,128)S(1)}, u32[]{:S(2)}, u32[]{:S(2)}) %collective-permute-start.5) | collective-permute-done | bytes 786464 | tf_op jit(solution)/shard_map/ppermute | solution.py:1117
  105.6 3.4 %inner_grads_1.1 = (f32[384,1536]{1,0:T(8,128)S(1)}, f32[384,1536]{1,0:T(8,128)}, f32[8,128]{1,0:T(8,128)S(1)}) custom-call(s32[5]{0:T(128)S(1)} %stack.23.refs_0_, bf16[256,768]{1,0:T(8,128)(2,1)S(1)} %get-tuple-element.353.refs_1_, bf16[256,1536]{1,0:T(8,128)(2,1)S(1)} %get-tuple-element.354.refs_2_, f32[768,1536]{1,0:T(8,128)S(1)} %get-tuple-element.355.refs_3_, ...), custom_call_target="tpu_custom_call" | custom-call | flops 1000000 | bytes 1000 | tf_op jit(solution)/shard_map/inner_grads_1/pallas_call | solution.py:103
  125.5 6.7 %attend_back_2.1 = (f32[208,384]{1,0:T(8,128)S(1)}, f32[768,384]{1,0:T(8,128)S(1)}, f32[768,384]{1,0:T(8,128)S(1)}, f32[128,3072]{1,0:T(8,128)S(1)}, f32[6,128,6...) custom-call(bf16[208,384]{1,0:T(8,128)(2,1)S(1)} %get-tuple-element.360.refs_0_, ...), custom_call_target="tpu_custom_call" | custom-call | flops 1000000 | bytes 1000 | tf_op jit(solution)/shard_map/attend_back_2/pallas_call | solution.py:103
  143.0 8.0 %attend_back_0.1 = (f32[256,384]{1,0:T(8,128)S(1)}, f32[768,384]{1,0:T(8,128)S(1)}, f32[768,384]{1,0:T(8,128)S(1)}, f32[128,3072]{1,0:T(8,128)S(1)}, f32[6,128,6...) custom-call(bf16[256,384]{1,0:T(8,128)(2,1)S(1)} %get-tuple-element., ...), custom_call_target="tpu_custom_call", output_to_operand_aliasing={{1}: (8, {}), {2}: (9, {}), {3}: (10, {}), {4}: (11, {})} | custom-call | flops 1000000 | bytes 1000 | tf_op jit(solution)/shard_map/attend_back_0/pallas_call | solution.py:103
  158.4 8.3 %attend_back_1.1 = (f32[256,384]{1,0:T(8,128)S(1)}, f32[768,384]{1,0:T(8,128)S(1)}, f32[768,384]{1,0:T(8,128)S(1)}, f32[128,3072]{1,0:T(8,128)S(1)}, f32[6,128,6...) custom-call(bf16[256,384]{1,0:T(8,128)(2,1)S(1)} %get-tuple-element., ...), custom_call_target="tpu_custom_call", output_to_operand_aliasing={{1}: (8, {}), {2}: (9, {}), {3}: (10, {}), {4}: (11, {})} | custom-call | flops 1000000 | bytes 1000 | tf_op jit(solution)/shard_map/attend_back_1/pallas_call | solution.py:103
  167.6 3.2 %attention_grads.1 = (f32[384,768]{1,0:T(8,128)S(1)}, f32[384,768]{1,0:T(8,128)S(1)}, f32[384,768]{1,0:T(8,128)S(1)}, f32[384,768]{1,0:T(8,128)S(1)}, f32[8,128]{1,0:T(8,128)S(1)}) custom-call(s32[5]{0:T(128)S(1)} %stack.23.refs_0_, bf16[256,768]{1,0:T(8,128)(2,1)S(1)} %get-tuple-element.424.refs_1_, bf16[256,768]{1,0:T(8,128)(2,1)S(1)} %get-tuple-element.425.refs_2_, ...), custom_call_target="tpu_custom_call" | custom-call | flops 1000000 | bytes 1000 | tf_op jit(solution)/shard_map/attention_grads/pallas_call | solution.py:103
  176.9 3.9 %table_sums.1 = (f32[8,256]{1,0:T(8,128)S(1)}, f32[8,128]{1,0:T(8,128)S(1)}) custom-call(f32[128,3072]{1,0:T(8,128)S(1)} %get-tuple-element.451.refs_0_, f32[6,128,640]{2,1,0:T(8,128)S(1)} %get-tuple-element.452.refs_1_, f32[8,128]{1,0:T(8,128)S(1)} %get-tuple-element.456.refs_2_), custom_call_target="tpu_custom_call" | custom-call | flops 1000000 | bytes 1000 | tf_op jit(solution)/shard_map/table_sums/pallas_call | solution.py:103
  180.8 3.4 %tap_sums.1 = (f32[16,768]{1,0:T(8,128)S(1)}, f32[8,128]{1,0:T(8,128)S(1)}) custom-call(s32[1]{0:T(128)S(6)} %copy.70.refs_0_, bf16[708,768]{1,0:T(8,128)(2,1)S(1)} %bitcast.23, f32[720,768]{1,0:T(8,128)S(1)} %get-tuple-element.447.refs_2_.refs_3_, f32[256,768]{1,0:T(8,128)S(1)} %get-tuple-element.448.refs_3_.refs_5_, ...), custom_call_target="tpu_custom_call" | custom-call | flops 1000000 | bytes 1000 | tf_op jit(solution)/shard_map/tap_sums/pallas_call | solution.py:103
  188.1 4.0 %collective-permute-done.27.refs_2_ = f32[192,768]{1,0:T(8,128)S(1)} collective-permute-done((f32[192,768]{1,0:T(8,128)S(1)}, f32[192,768]{1,0:T(8,128)S(1)}, u32[]{:S(2)}, u32[]{:S(2)}) %collective-permute-start.27) | collective-permute-done | bytes 589856 | tf_op jit(solution)/shard_map/ppermute | solution.py:1121
  194.6 9.4 %collective-permute-done.29.refs_1_ = f32[56,1536]{1,0:T(8,128)S(1)} collective-permute-done((f32[56,1536]{1,0:T(8,128)S(1)}, f32[56,1536]{1,0:T(8,128)S(1)}, u32[]{:S(2)}, u32[]{:S(2)}) %collective-permute-start.29) | collective-permute-done | bytes 344096 | tf_op jit(solution)/shard_map/ppermute | solution.py:1121
  208.9 8.0 %collective-permute-done.31.refs_1_ = f32[48,768]{1,0:T(8,128)S(1)} collective-permute-done((f32[48,768]{1,0:T(8,128)S(1)}, f32[48,768]{1,0:T(8,128)S(1)}, u32[]{:S(2)}, u32[]{:S(2)}) %collective-permute-start.31) | collective-permute-done | bytes 147488 | tf_op jit(solution)/shard_map/ppermute | solution.py:1121
  223.6 5.4 %decode.1 = (bf16[708,768]{1,0:T(8,128)(2,1)}, f32[8,128]{1,0:T(8,128)S(1)}) custom-call(s32[1]{0:T(128)S(6)} %copy.70.refs_0_, bf16[3,3,768]{2,1,0:T(4,128)(2,1)S(1)} %copy-done.10, bf16[9,768]{1,0:T(8,128)(2,1)S(1)} %copy-done.9, f32[720,768]{1,0:T(8,128)S(1)} %get-tuple-element.447.refs_2_.refs_3_, f32[720,768]{1,0:T(8,128)S(1)} %collective-permute-done.22.refs_4_, ...), custom_call_target="tpu_custom_call" | custom-call | flops 1000000 | bytes 1000 | tf_op jit(solution)/shard_map/decode/pallas_call | solution.py:103
  (161 shorter events, 92.0 us)
Async XLA Ops:
  6.5 17.3 %collective-permute-start = (f32[192,768]{1,0:T(8,128)S(1)}, f32[192,768]{1,0:T(8,128)S(1)}, u32[]{:S(2)}, u32[]{:S(2)}) collective-permute-start(f32[192,768]{1,0:T(8,128)S(1)} %get-tuple-element.293), channel_id=1, source_target_pairs={{0,1},{1,0},{2,3},{3,2},{4,5},{5,4},{6,7},{7,6},{8,9},{9,8},{10,11... | collective-permute-start | bytes 1769480 | tf_op jit(solution)/shard_map/ppermute | solution.py:1117
  24.1 20.6 %collective-permute-start.2 = (f32[192,768]{1,0:T(8,128)S(1)}, f32[192,768]{1,0:T(8,128)S(1)}, u32[]{:S(2)}, u32[]{:S(2)}) collective-permute-start(f32[192,768]{1,0:T(8,128)S(1)} %get-tuple-element.301.refs_6_), channel_id=1, source_target_pairs={{0,2},{2,0},{4,6},{6,4},{8,10},{10,8},{12,14},{14,12},{16,18},{18,... | collective-permute-start | bytes 1769480 | tf_op jit(solution)/shard_map/ppermute | solution.py:1121
  24.2 20.5 %collective-permute-start.4 = (f32[208,384]{1,0:T(8,128)S(1)}, f32[208,384]{1,0:T(8,128)S(1)}, u32[]{:S(2)}, u32[]{:S(2)}) collective-permute-start(f32[208,384]{1,0:T(8,128)S(1)} %get-tuple-element.304.refs_1_), channel_id=1, source_target_pairs={{0,1},{1,0},{2,3},{3,2},{4,5},{5,4},{6,7},{7,6},{8,9},{9,8},{10,11... | collective-permute-start | bytes 958472 | tf_op jit(solution)/shard_map/ppermute | solution.py:1117
  34.4 15.4 %collective-permute-start.3 = (f32[256,384]{1,0:T(8,128)S(1)}, f32[256,384]{1,0:T(8,128)S(1)}, u32[]{:S(2)}, u32[]{:S(2)}) collective-permute-start(f32[256,384]{1,0:T(8,128)S(1)} %get-tuple-element.302.refs_1_), channel_id=1, source_target_pairs={{0,1},{1,0},{2,3},{3,2},{4,5},{5,4},{6,7},{7,6},{8,9},{9,8},{10,11... | collective-permute-start | bytes 1179656 | tf_op jit(solution)/shard_map/ppermute | solution.py:1117
  43.7 12.1 %collective-permute-start.1 = (f32[256,384]{1,0:T(8,128)S(1)}, f32[256,384]{1,0:T(8,128)S(1)}, u32[]{:S(2)}, u32[]{:S(2)}) collective-permute-start(f32[256,384]{1,0:T(8,128)S(1)} %get-tuple-element.299.refs_1_), channel_id=1, source_target_pairs={{0,1},{1,0},{2,3},{3,2},{4,5},{5,4},{6,7},{7,6},{8,9},{9,8},{10,11... | collective-permute-start | bytes 1179656 | tf_op jit(solution)/shard_map/ppermute | solution.py:1117
  48.4 21.1 %collective-permute-start.7 = (f32[208,768]{1,0:T(8,128)S(1)}, f32[208,768]{1,0:T(8,128)S(1)}, u32[]{:S(2)}, u32[]{:S(2)}) collective-permute-start(f32[208,768]{1,0:T(8,128)S(1)} %get-tuple-element.317.refs_1_), channel_id=1, source_target_pairs={{0,1},{1,0},{2,3},{3,2},{4,5},{5,4},{6,7},{7,6},{8,9},{9,8},{10,11... | collective-permute-start | bytes 1916936 | tf_op jit(solution)/shard_map/ppermute | solution.py:1117
  53.0 33.3 %collective-permute-start.6 = (f32[256,768]{1,0:T(8,128)S(1)}, f32[256,768]{1,0:T(8,128)S(1)}, u32[]{:S(2)}, u32[]{:S(2)}) collective-permute-start(f32[256,768]{1,0:T(8,128)S(1)} %get-tuple-element.314.refs_1_), channel_id=1, source_target_pairs={{0,1},{1,0},{2,3},{3,2},{4,5},{5,4},{6,7},{7,6},{8,9},{9,8},{10,11... | collective-permute-start | bytes 2359304 | tf_op jit(solution)/shard_map/ppermute | solution.py:1117
  59.3 43.9 %collective-permute-start.5 = (f32[256,768]{1,0:T(8,128)S(1)}, f32[256,768]{1,0:T(8,128)S(1)}, u32[]{:S(2)}, u32[]{:S(2)}) collective-permute-start(f32[256,768]{1,0:T(8,128)S(1)} %get-tuple-element.311.refs_1_), channel_id=1, source_target_pairs={{0,1},{1,0},{2,3},{3,2},{4,5},{5,4},{6,7},{7,6},{8,9},{9,8},{10,11... | collective-permute-start | bytes 2359304 | tf_op jit(solution)/shard_map/ppermute | solution.py:1117
  72.7 44.2 %collective-permute-start.9 = (f32[208,768]{1,0:T(8,128)}, f32[208,768]{1,0:T(8,128)}, u32[]{:S(2)}, u32[]{:S(2)}) collective-permute-start(f32[208,768]{1,0:T(8,128)} %get-tuple-element.344.refs_1_), channel_id=1, source_target_pairs={{0,1},{1,0},{2,3},{3,2},{4,5},{5,4},{6,7},{7,6},{8,9},{9,8},{10,11... | collective-permute-start | bytes 1916936 | tf_op jit(solution)/shard_map/ppermute | solution.py:1117
  111.9 21.8 %collective-permute-start.8 = (f32[256,768]{1,0:T(8,128)S(1)}, f32[256,768]{1,0:T(8,128)S(1)}, u32[]{:S(2)}, u32[]{:S(2)}) collective-permute-start(f32[256,768]{1,0:T(8,128)S(1)} %get-tuple-element.341.refs_1_), channel_id=1, source_target_pairs={{0,1},{1,0},{2,3},{3,2},{4,5},{5,4},{6,7},{7,6},{8,9},{9,8},{10,11... | collective-permute-start | bytes 2359304 | tf_op jit(solution)/shard_map/ppermute | solution.py:1117
  112.7 38.3 %collective-permute-start.14 = (f32[256,768]{1,0:T(8,128)S(1)}, f32[256,768]{1,0:T(8,128)S(1)}, u32[]{:S(2)}, u32[]{:S(2)}) collective-permute-start(f32[256,768]{1,0:T(8,128)S(1)} %get-tuple-element.397.refs_1_), channel_id=1, source_target_pairs={{0,1},{1,0},{2,3},{3,2},{4,5},{5,4},{6,7},{7,6},{8,9},{9,8},{10,11... | collective-permute-start | bytes 2359304 | tf_op jit(solution)/shard_map/ppermute | solution.py:1117
  120.6 16.6 %collective-permute-start.13 = (f32[192,768]{1,0:T(8,128)S(1)}, f32[192,768]{1,0:T(8,128)S(1)}, u32[]{:S(2)}, u32[]{:S(2)}) collective-permute-start(f32[192,768]{1,0:T(8,128)S(1)} %get-tuple-element.390), channel_id=1, source_target_pairs={{0,4},{2,6},{4,0},{6,2},{8,12},{10,14},{12,8},{14,10},{16,20},{18,... | collective-permute-start | bytes 1769480 | tf_op jit(solution)/shard_map/ppermute | solution.py:1121
  123.1 16.5 %collective-permute-start.12 = (f32[192,768]{1,0:T(8,128)S(1)}, f32[192,768]{1,0:T(8,128)S(1)}, u32[]{:S(2)}, u32[]{:S(2)}) collective-permute-start(f32[192,768]{1,0:T(8,128)S(1)} %get-tuple-element.388), channel_id=1, source_target_pairs={{0,8},{2,10},{4,12},{6,14},{8,0},{10,2},{12,4},{14,6},{16,24},{18,... | collective-permute-start | bytes 1769480 | tf_op jit(solution)/shard_map/ppermute | solution.py:1121
  125.4 26.7 %collective-permute-start.17 = (f32[200,768]{1,0:T(8,128)S(1)}, f32[200,768]{1,0:T(8,128)S(1)}, u32[]{:S(2)}, u32[]{:S(2)}) collective-permute-start(f32[200,768]{1,0:T(8,128)S(1)} %get-tuple-element.412), channel_id=1, source_target_pairs={{0,4},{2,6},{4,0},{6,2},{8,12},{10,14},{12,8},{14,10},{16,20},{18,... | collective-permute-start | bytes 1843208 | tf_op jit(solution)/shard_map/ppermute | solution.py:1121
  135.6 31.2 %collective-permute-start.19 = (f32[192,768]{1,0:T(8,128)S(1)}, f32[192,768]{1,0:T(8,128)S(1)}, u32[]{:S(2)}, u32[]{:S(2)}) collective-permute-start(f32[192,768]{1,0:T(8,128)S(1)} %get-tuple-element.436), channel_id=1, source_target_pairs={{0,4},{2,6},{4,0},{6,2},{8,12},{10,14},{12,8},{14,10},{16,20},{18,... | collective-permute-start | bytes 1769480 | tf_op jit(solution)/shard_map/ppermute | solution.py:1121
  137.9 14.9 %collective-permute-start.16 = (f32[96,768]{1,0:T(8,128)S(1)}, f32[96,768]{1,0:T(8,128)S(1)}, u32[]{:S(2)}, u32[]{:S(2)}) collective-permute-start(f32[96,768]{1,0:T(8,128)S(1)} %get-tuple-element.410), channel_id=1, source_target_pairs={{0,8},{2,10},{4,12},{6,14},{8,0},{10,2},{12,4},{14,6},{16,24},{18,... | collective-permute-start | bytes 884744 | tf_op jit(solution)/shard_map/ppermute | solution.py:1121
  140.3 13.7 %collective-permute-start.15 = (f32[96,768]{1,0:T(8,128)S(1)}, f32[96,768]{1,0:T(8,128)S(1)}, u32[]{:S(2)}, u32[]{:S(2)}) collective-permute-start(f32[96,768]{1,0:T(8,128)S(1)} %get-tuple-element.408), channel_id=1, source_target_pairs={{0,16},{2,18},{4,20},{6,22},{8,24},{10,26},{12,28},{14,30},{16,0},... | collective-permute-start | bytes 884744 | tf_op jit(solution)/shard_map/ppermute | solution.py:1121
  152.7 14.9 %collective-permute-start.18 = (f32[104,768]{1,0:T(8,128)S(1)}, f32[104,768]{1,0:T(8,128)S(1)}, u32[]{:S(2)}, u32[]{:S(2)}) collective-permute-start(f32[104,768]{1,0:T(8,128)S(1)} %get-tuple-element.434), channel_id=1, source_target_pairs={{0,8},{2,10},{4,12},{6,14},{8,0},{10,2},{12,4},{14,6},{16,24},{18,... | collective-permute-start | bytes 958472 | tf_op jit(solution)/shard_map/ppermute | solution.py:1121
  170.9 13.9 %collective-permute-start.24 = (f32[384,768]{1,0:T(8,128)S(1)}, f32[384,768]{1,0:T(8,128)S(1)}, u32[]{:S(2)}, u32[]{:S(2)}) collective-permute-start(f32[384,768]{1,0:T(8,128)S(1)} %get-tuple-element.467), channel_id=1, source_target_pairs={{0,2},{2,0},{4,6},{6,4},{8,10},{10,8},{12,14},{14,12},{16,18},{18,... | collective-permute-start | bytes 3538952 | tf_op jit(solution)/shard_map/ppermute | solution.py:1121
  173.4 50.1 %collective-permute-start.22 = (f32[720,768]{1,0:T(8,128)S(1)}, f32[720,768]{1,0:T(8,128)S(1)}, u32[]{:S(2)}, u32[]{:S(2)}) collective-permute-start(f32[720,768]{1,0:T(8,128)S(1)} %get-tuple-element.447.refs_2_.refs_3_), channel_id=1, source_target_pairs={{0,1},{1,0},{2,3},{3,2},{4,5},{5,4},{6,7},{7,6},{8,9},{9,8},{10,11... | collective-permute-start | bytes 6635528 | tf_op jit(solution)/shard_map/ppermute | solution.py:1117
  175.8 16.3 %collective-permute-start.27 = (f32[192,768]{1,0:T(8,128)S(1)}, f32[192,768]{1,0:T(8,128)S(1)}, u32[]{:S(2)}, u32[]{:S(2)}) collective-permute-start(f32[192,768]{1,0:T(8,128)S(1)} %get-tuple-element.476), channel_id=1, source_target_pairs={{0,4},{2,6},{4,0},{6,2},{8,12},{10,14},{12,8},{14,10},{16,20},{18,... | collective-permute-start | bytes 1769480 | tf_op jit(solution)/shard_map/ppermute | solution.py:1121
  185.6 20.7 %collective-permute-start.26 = (f32[216,768]{1,0:T(8,128)S(1)}, f32[216,768]{1,0:T(8,128)S(1)}, u32[]{:S(2)}, u32[]{:S(2)}) collective-permute-start(f32[216,768]{1,0:T(8,128)S(1)} %get-tuple-element.474), channel_id=1, source_target_pairs={{0,4},{2,6},{4,0},{6,2},{8,12},{10,14},{12,8},{14,10},{16,20},{18,... | collective-permute-start | bytes 1990664 | tf_op jit(solution)/shard_map/ppermute | solution.py:1121
  186.7 17.3 %collective-permute-start.29 = (f32[56,1536]{1,0:T(8,128)S(1)}, f32[56,1536]{1,0:T(8,128)S(1)}, u32[]{:S(2)}, u32[]{:S(2)}) collective-permute-start(f32[56,1536]{1,0:T(8,128)S(1)} %get-tuple-element.481), channel_id=1, source_target_pairs={{0,16},{2,18},{4,20},{6,22},{8,24},{10,26},{12,28},{14,30},{16,0},... | collective-permute-start | bytes 1032200 | tf_op jit(solution)/shard_map/ppermute | solution.py:1121
  192.9 12.6 %collective-permute-start.28 = (f32[96,768]{1,0:T(8,128)S(1)}, f32[96,768]{1,0:T(8,128)S(1)}, u32[]{:S(2)}, u32[]{:S(2)}) collective-permute-start(f32[96,768]{1,0:T(8,128)S(1)} %get-tuple-element.479), channel_id=1, source_target_pairs={{0,8},{2,10},{4,12},{6,14},{8,0},{10,2},{12,4},{14,6},{16,24},{18,... | collective-permute-start | bytes 884744 | tf_op jit(solution)/shard_map/ppermute | solution.py:1121
  (33 other events, 262.0 us)
